TPU v7x, 32 devices: a whole 2x2x4 slice. The times are simulated.
32 devices in a mesh: grp: 2 (over y), bead: 4 (over z), space: 4 (over x, core).
Axes of the slice: x: 2, y: 2, z: 4, core: 2. Of those that a mesh axis runs over, the one named last changes fastest.
Arguments:
- positions: float32 [16, 3, 2048], P(('grp', 'bead'), None, 'space'), parts along dimension 0, may hold values from -6 to 6
- momenta: float32 [16, 3, 2048], P(('grp', 'bead'), None, 'space'), parts along dimension 0, may hold values from -6 to 6
- species: int32 [4096], P(('grp', 'space')), parts along dimension 0, may hold values from 0 to 3
- neighbour_index: int32 [32, 4096], P(None, ('grp', 'space')), parts along dimension 1, may hold values from 0 to 767, as said below
- neighbour_count: int32 [4096], P(('grp', 'space')), parts along dimension 0, may hold values from 1 to 32
- radial_rates: float32 [32], replicated, may hold values from 0.1 to 1
- weight_input: float32 [256, 128], replicated, may hold values from -0.5 to 0.5
- embedding: float32 [256, 4], replicated, may hold values from -6 to 6
- weight_middle: float32 [256, 256], replicated, may hold values from -0.375 to 0.375
- weight_deeper: float32 [256, 256], replicated, may hold values from -0.375 to 0.375
- weight_output: float32 [256], replicated, may hold values from -0.375 to 0.375
Outputs:
- momenta_next: float32 [16, 3, 2048], P(('grp', 'bead'), None, 'space'), parts along dimension 0
- displacement: float32 [16, 3, 2048], P(('grp', 'bead'), None, 'space'), parts along dimension 0
There are 2 independent parts, one for each index of `grp`. A program takes and returns all parts, laid end to end along the dimension named above; an argument that names none is the same for every part. Nothing has to cross between parts.
Inputs may be any that keep to these rules, and one draw needn't show every extreme that they name: `neighbour_index`: each atom's slots name atoms within 128 places of itself in the extended slab, never itself.
All inputs are finite; a program needn't handle non-finite values.
Results may differ from a plain program's by a relative error of at most 0.00005.
Values sent between devices are 32-bit elements; how exact they have to be, the bound alone decides.
No kernel may reach another device: no remote copies, remote signals or barrier semaphores. Data moves between devices by JAX's collectives and lax.ppermute only.
A program may use at most 64 MiB of HBM per device.

v0:
```python
import jax
import jax.numpy as jnp
import numpy as np
from jax import lax
from jax.experimental import pallas as pl
from jax.experimental.pallas import tpu as pltpu
from jax.sharding import PartitionSpec as P

HALO = 128
NC = 4
SPECIES = 4
LANES = 128
DEAD = 4096
LOG2E = 1.4426950408889634

MASS_TABLE = (1.0, 0.25, 1.5, 2.0)
SPRING_RATE = 0.2
TIME_STEP = 0.5


def contraction_table(bead_count, kept_modes):
    rows = np.arange(kept_modes)[:, None] / kept_modes
    cols = np.arange(bead_count)[None, :] / bead_count
    angles = 2.0 * np.pi * (rows - cols)
    summed = np.ones_like(angles)
    for order in range(1, kept_modes // 2):
        summed = summed + 2.0 * np.cos(order * angles)
    summed = summed + np.cos(kept_modes // 2 * angles)
    return (summed / bead_count).astype(np.float32)


def per_species(species, values):
    picked = jnp.full(species.shape, values[0], jnp.float32)
    for kind in range(1, SPECIES):
        picked = jnp.where(species == kind, values[kind], picked)
    return picked


def split2(value):
    high = value.astype(jnp.bfloat16)
    low = (value - high.astype(jnp.float32)).astype(jnp.bfloat16)
    return high, low


def dot(lhs, rhs):
    return lax.dot_general(
        lhs, rhs, (((1,), (0,)), ((), ())), preferred_element_type=jnp.float32
    )


def dot_nt(lhs, rhs):
    return lax.dot_general(
        lhs, rhs, (((1,), (1,)), ((), ())), preferred_element_type=jnp.float32
    )


def weights_kernel(w1, emb, w2, w3, l1, l2, l3, t1, t2, t3):
    hid, chan = w1.shape
    high, low = split2(w1[...])
    l1[:, 0:chan] = high
    l1[:, 2 * chan : 3 * chan] = low
    l1[:, 3 * chan : 4 * chan] = high
    e = emb[...]
    eh, el = split2(e)
    ell = (e - eh.astype(jnp.float32) - el.astype(jnp.float32)).astype(jnp.bfloat16)
    l1[:, chan : 2 * chan] = jnp.concatenate(
        [eh, el, ell, jnp.zeros((hid, chan - 3 * SPECIES), jnp.bfloat16)], axis=1
    )
    t1[0:chan, :], t1[chan : 2 * chan, :] = split2(w1[...].T)
    for src, fwd, bwd in ((w2, l2, t2), (w3, l3, t3)):
        fwd[0:hid, :], fwd[hid : 2 * hid, :] = split2(src[...])
        bwd[0:hid, :], bwd[hid : 2 * hid, :] = split2(src[...].T)


def split_weights(w1, emb, w2, w3):
    hid, chan = w1.shape
    vmem = pl.BlockSpec(memory_space=pltpu.VMEM)
    shapes = [
        (hid, 4 * chan),
        (2 * hid, hid),
        (2 * hid, hid),
        (2 * chan, hid),
        (2 * hid, hid),
        (2 * hid, hid),
    ]
    return pl.pallas_call(
        weights_kernel,
        out_shape=[jax.ShapeDtypeStruct(s, jnp.bfloat16) for s in shapes],
        in_specs=[vmem] * 4,
        out_specs=[vmem] * len(shapes),
        name="split_weights",
    )(w1, emb, w2, w3)


def force_kernel(
    ext,
    code,
    rates,
    wout,
    l1,
    l2,
    l3,
    t1,
    t2,
    t3,
    out,
    off_s,
    kind_s,
    dist_s,
    rad_s,
    desc_s,
    grad_s,
    pair_s,
    rel_s,
):
    slots, block = code.shape
    groups = block // LANES
    rate_count = rates.shape[0]
    octets = rate_count // 8
    chan = SPECIES * rate_count
    hid = wout.shape[0]
    band = LANES + 2 * HALO
    rates2 = rates[...] * (-LOG2E)
    rate8 = [
        jnp.broadcast_to(rates2[8 * o : 8 * o + 8, :], (8, LANES))
        for o in range(octets)
    ]

    for g in range(groups):
        lane0 = g * LANES
        src = [
            [
                jnp.broadcast_to(
                    ext[c : c + 1, lane0 + LANES * q : lane0 + LANES * (q + 1)],
                    (8, LANES),
                )
                for q in range(band // LANES)
            ]
            for c in range(4)
        ]
        for o in range(slots // 8):
            rows = slice(8 * o, 8 * o + 8)
            cols = slice(lane0, lane0 + LANES)
            word = code[rows, cols]
            lane = jnp.bitwise_and(word, LANES - 1)
            part = jnp.bitwise_and(word, DEAD - 1)
            is0 = part < LANES
            is1 = part < 2 * LANES
            got = []
            for c in range(4):
                a, b, d = (
                    jnp.take_along_axis(src[c][q], lane, axis=1) for q in range(3)
                )
                got.append(jnp.where(is0, a, jnp.where(is1, b, d)))
            total = None
            for c in range(3):
                diff = got[c] - src[c][1]
                off_s[c, rows, cols] = diff
                total = diff * diff if total is None else total + diff * diff
            dist_s[rows, cols] = total
            kind_s[rows, cols] = jnp.where(word >= DEAD, -1.0, got[3])

    for g in range(groups):
        cols = slice(g * LANES, (g + 1) * LANES)
        acc = [[jnp.zeros((8, LANES), jnp.float32)] * octets for _ in range(SPECIES)]
        for n in range(slots):
            kind = jnp.broadcast_to(kind_s[n : n + 1, cols], (8, LANES))
            dist = jnp.broadcast_to(dist_s[n : n + 1, cols], (8, LANES))
            masks = [kind == float(s) for s in range(SPECIES)]
            for o in range(octets):
                radial = jnp.exp2(rate8[o] * dist)
                first = (n * octets + o) * 8
                rad_s[first : first + 8, cols] = radial
                for s in range(SPECIES):
                    acc[s][o] = acc[s][o] + jnp.where(masks[s], radial, 0.0)
        for s in range(SPECIES):
            for o in range(octets):
                first = s * rate_count + 8 * o
                desc_s[first : first + 8, cols] = acc[s][o]

    kinds = lax.broadcasted_iota(jnp.int32, (16, block), 0)
    kinds = jnp.where(kinds < 3 * SPECIES, kinds % SPECIES, -1).astype(jnp.float32)
    centre = ext[3:4, HALO : HALO + block]
    onehot = jnp.where(kinds == centre, 1.0, 0.0).astype(jnp.bfloat16)
    dh, dl = split2(desc_s[...])
    pad = jnp.zeros((chan - 16, block), jnp.bfloat16)
    first = dot(l1[:, 0 : 2 * chan], jnp.concatenate([dh, onehot, pad], axis=0))
    first = first + dot(l1[:, 2 * chan : 4 * chan], jnp.concatenate([dh, dl], axis=0))

    def act(x):
        sig = 1.0 / (1.0 + jnp.exp2(x * (-LOG2E)))
        value = x * sig
        return value, sig + value * (1.0 - sig)

    def layer(pair, x):
        high, low = split2(x)
        both = dot(pair[...], high)
        rows = pair.shape[0] // 2
        return both[0:rows] + (both[rows:] + dot(pair[0:rows, :], low))

    h1, s1 = act(first)
    h2, s2 = act(layer(l2, h1))
    _, s3 = act(layer(l3, h2))
    g3 = wout[...] * s3
    g2 = layer(t3, g3) * s2
    g1 = layer(t2, g2) * s1
    grad_s[...] = layer(t1, g1)

    rate_true = [
        jnp.broadcast_to(rates[8 * o : 8 * o + 8, :], (8, LANES)) for o in range(octets)
    ]
    for g in range(groups):
        cols = slice(g * LANES, (g + 1) * LANES)
        grads = [
            [
                grad_s[s * rate_count + 8 * o : s * rate_count + 8 * o + 8, cols]
                * rate_true[o]
                for o in range(octets)
            ]
            for s in range(SPECIES)
        ]
        for n in range(slots):
            kind = jnp.broadcast_to(kind_s[n : n + 1, cols], (8, LANES))
            masks = [kind == float(s) for s in range(SPECIES - 1)]
            total = None
            for o in range(octets):
                picked = grads[SPECIES - 1][o]
                for s in range(SPECIES - 1):
                    picked = jnp.where(masks[s], grads[s][o], picked)
                first = (n * octets + o) * 8
                term = picked * rad_s[first : first + 8, cols]
                total = term if total is None else total + term
            dist_s[n : n + 1, cols] = jnp.sum(total, axis=0, keepdims=True)

    for g in range(groups):
        cols = slice(g * LANES, (g + 1) * LANES)
        centre_force = [jnp.zeros((8, LANES), jnp.float32)] * 3
        for o in range(slots // 8):
            rows = slice(8 * o, 8 * o + 8)
            word = code[rows, cols]
            part = jnp.bitwise_and(word, DEAD - 1)
            rel_s[0, rows, cols] = jnp.bitwise_and(part, 63)
            rel_s[1, rows, cols] = jnp.right_shift(part, 6)
            slope = jnp.where(word >= DEAD, 0.0, 2.0 * dist_s[rows, cols])
            for c in range(3):
                force = slope * off_s[c, rows, cols]
                centre_force[c] = centre_force[c] + force
                high = force.astype(jnp.bfloat16).astype(jnp.float32)
                pair_s[2 * c, rows, cols] = high
                pair_s[2 * c + 1, rows, cols] = force - high
        for c in range(3):
            rad_s[c : c + 1, cols] = jnp.sum(centre_force[c], axis=0, keepdims=True)

    low_ids = lax.broadcasted_iota(jnp.int32, (64, LANES), 0)
    high_ids = lax.broadcasted_iota(jnp.int32, (8, LANES), 0)
    out[...] = jnp.zeros_like(out)
    for g in range(groups):
        cols = slice(g * LANES, (g + 1) * LANES)
        total = jnp.zeros((48, 64), jnp.float32)
        for n in range(0, slots, 2):
            lefts, rights = [], []
            for k in (n, n + 1):
                low = rel_s[0, k : k + 1, cols]
                high = jnp.broadcast_to(rel_s[1, k : k + 1, cols], (8, LANES))
                rights.append(jnp.where(low_ids == low, 1.0, 0.0).astype(jnp.bfloat16))
                hit = high_ids == high
                lefts.append(
                    jnp.concatenate(
                        [
                            jnp.where(
                                hit,
                                jnp.broadcast_to(
                                    pair_s[c, k : k + 1, cols], (8, LANES)
                                ),
                                0.0,
                            )
                            for c in range(6)
                        ],
                        axis=0,
                    ).astype(jnp.bfloat16)
                )
            total = total + dot_nt(
                jnp.concatenate(lefts, axis=1), jnp.concatenate(rights, axis=1)
            )
        for c in range(3):
            merged = total[16 * c : 16 * c + 8, :] + total[16 * c + 8 : 16 * c + 16, :]
            for q in range(band // 64):
                first = g * LANES + 64 * q
                out[c : c + 1, first : first + 64] = (
                    out[c : c + 1, first : first + 64] + merged[q : q + 1, :]
                )
    for c in range(3):
        out[c : c + 1, HALO : HALO + block] = (
            out[c : c + 1, HALO : HALO + block] - rad_s[c : c + 1, :]
        )


def window_forces(ext, code, rates, wout, pairs):
    slots, block = code.shape
    rate_count = rates.shape[0]
    vmem = pl.BlockSpec(memory_space=pltpu.VMEM)
    f32 = jnp.float32
    return pl.pallas_call(
        force_kernel,
        out_shape=jax.ShapeDtypeStruct((8, block + 2 * HALO), f32),
        in_specs=[vmem] * 10,
        out_specs=vmem,
        scratch_shapes=[
            pltpu.VMEM((3, slots, block), f32),
            pltpu.VMEM((slots, block), f32),
            pltpu.VMEM((slots, block), f32),
            pltpu.VMEM((slots * rate_count, block), f32),
            pltpu.VMEM((SPECIES * rate_count, block), f32),
            pltpu.VMEM((SPECIES * rate_count, block), f32),
            pltpu.VMEM((6, slots, block), f32),
            pltpu.VMEM((2, slots, block), jnp.int32),
        ],
        compiler_params=pltpu.CompilerParams(vmem_limit_bytes=32 * 1024 * 1024),
        name="window_forces",
    )(ext, code, rates[:, None], wout[:, None], *pairs)


def swap_with_adjacent(send_inner, send_outer):
    count = lax.axis_size("space")
    inner = [(i, i ^ 1) for i in range(count)]
    outer = [(i, (i + 1) % count if i % 2 else (i - 1) % count) for i in range(count)]
    return (
        lax.ppermute(send_inner, "space", inner),
        lax.ppermute(send_outer, "space", outer),
    )


def on_device(
    positions,
    momenta,
    species,
    neighbour_index,
    neighbour_count,
    radial_rates,
    weight_input,
    embedding,
    weight_middle,
    weight_deeper,
    weight_output,
):
    bead_dev = positions.shape[0]
    atom_dev = positions.shape[2]
    bead_groups = lax.axis_size("bead")
    slab_count = lax.axis_size("space")
    bead_count = bead_dev * bead_groups
    table = jnp.asarray(contraction_table(bead_count, NC))
    place = lax.axis_index("bead")
    slab = lax.axis_index("space")
    even = slab % 2 == 0
    replica = place % NC
    block_size = atom_dev * NC // bead_groups
    block_start = (place // NC) * block_size
    direct = bead_groups == NC

    pairs = split_weights(weight_input, embedding, weight_middle, weight_deeper)

    slots = lax.dynamic_slice_in_dim(neighbour_index, block_start, block_size, 1)
    counts = lax.dynamic_slice_in_dim(neighbour_count, block_start, block_size, 0)
    targets = slab * atom_dev + slots - HALO
    slot_ids = lax.broadcasted_iota(jnp.int32, slots.shape, 0)
    live = (slot_ids < counts[None, :]) & (targets >= 0) & (targets < atom_dev * slab_count)
    group_first = lax.broadcasted_iota(jnp.int32, slots.shape, 1) // LANES * LANES
    code = slots - block_start - group_first + jnp.where(live, 0, DEAD)

    if direct:
        others = [
            lax.ppermute(positions, "bead", [(i, i ^ k) for i in range(bead_groups)])
            for k in range(1, bead_groups)
        ]
        contracted = jnp.zeros(positions.shape[1:], jnp.float32)
        for k, block in enumerate([positions] + others):
            owner = jnp.bitwise_xor(place, k)
            for j in range(bead_dev):
                contracted = contracted + table[replica, owner * bead_dev + j] * block[j]
        odd_place = place % 2 == 1
        near, far = others[0], others[bead_groups - 2]
        below = jnp.where(odd_place, near[-1], far[-1])
        above = jnp.where(odd_place, far[0], near[0])
    else:
        everything = lax.all_gather(positions, "bead", axis=0, tiled=True)
        weights = lax.dynamic_index_in_dim(table, replica, 0, keepdims=False)
        contracted = jnp.sum(weights[:, None, None] * everything, axis=0)
        first = place * bead_dev
        below = lax.dynamic_index_in_dim(
            everything, (first - 1) % bead_count, 0, keepdims=False
        )
        above = lax.dynamic_index_in_dim(
            everything, (first + bead_dev) % bead_count, 0, keepdims=False
        )

    stacked = jnp.concatenate(
        [
            contracted,
            species.astype(jnp.float32)[None, :],
            jnp.zeros((4, atom_dev), jnp.float32),
        ],
        axis=0,
    )
    bottom, top = stacked[:, :HALO], stacked[:, atom_dev - HALO :]
    got_inner, got_outer = swap_with_adjacent(
        jnp.where(even, top, bottom), jnp.where(even, bottom, top)
    )
    extended = jnp.concatenate(
        [
            jnp.where(even, got_outer, got_inner),
            stacked,
            jnp.where(even, got_inner, got_outer),
        ],
        axis=1,
    )
    window = lax.dynamic_slice_in_dim(extended, block_start, block_size + 2 * HALO, 1)
    force = window_forces(window, code, radial_rates, weight_output, pairs)[:3]

    if not direct:
        partial = jnp.zeros((3, atom_dev + 2 * HALO), jnp.float32)
        partial = lax.dynamic_update_slice_in_dim(partial, force, block_start, 1)
        chosen = (jnp.arange(NC, dtype=jnp.int32) == replica).astype(jnp.float32)
        force = lax.psum(chosen[:, None, None] * partial[None], "bead")

    lower, own, upper = (
        force[..., :HALO],
        force[..., HALO : HALO + atom_dev],
        force[..., HALO + atom_dev :],
    )
    got_inner, got_outer = swap_with_adjacent(
        jnp.where(even, upper, lower), jnp.where(even, lower, upper)
    )
    own = jnp.concatenate(
        [
            own[..., :HALO] + jnp.where(even, got_outer, got_inner),
            own[..., HALO : atom_dev - HALO],
            own[..., atom_dev - HALO :] + jnp.where(even, got_inner, got_outer),
        ],
        axis=-1,
    )

    if direct:
        expanded = [jnp.zeros((3, atom_dev), jnp.float32)] * bead_dev
        for k in range(bead_groups):
            if k == 0:
                block = own
            else:
                block = lax.ppermute(own, "bead", [(i, i ^ k) for i in range(bead_groups)])
            owner = jnp.bitwise_xor(place, k)
            for j in range(bead_dev):
                expanded[j] = expanded[j] + table[owner, place * bead_dev + j] * block
        expanded = jnp.stack(expanded)
    else:
        columns = lax.dynamic_slice_in_dim(table, place * bead_dev, bead_dev, 1)
        expanded = jnp.sum(columns[:, :, None, None] * own[:, None], axis=0)
    expanded = bead_count / NC * expanded

    masses = per_species(species, MASS_TABLE)
    cycle = jnp.concatenate([below[None], positions, above[None]], axis=0)
    laplace = 2.0 * positions - cycle[:-2] - cycle[2:]
    spring = -SPRING_RATE * masses[None, None, :] * laplace
    momenta_next = momenta + TIME_STEP * (spring + expanded)
    displacement = TIME_STEP * momenta_next / masses[None, None, :]
    return (momenta_next, displacement)


def solution(mesh):
    return jax.shard_map(
        on_device,
        mesh=mesh,
        in_specs=(
            P(("grp", "bead"), None, "space"),
            P(("grp", "bead"), None, "space"),
            P(("grp", "space")),
            P(None, ("grp", "space")),
            P(("grp", "space")),
            P(),
            P(),
            P(),
            P(),
            P(),
            P(),
        ),
        out_specs=(P(("grp", "bead"), None, "space"), P(("grp", "bead"), None, "space")),
        check_vma=False,
    )
```

profile of v0, /device:TPU:0, one launch (start us, length us, event | category | flops | bytes accessed | tf_op | source)
XLA Modules:
  0.0 50.8 jit_solution(5774585573218131276)
XLA Ops:
  0.6 0.7 %copy.27 = f32[2,3,512]{2,1,0:T(4,128)S(1)} copy(f32[2,3,512]{2,0,1:T(2,128)} %param.12) | data formatting | bytes 24576 | tf_op args[0]
  1.3 3.0 %collective-permute-start = (f32[2,3,512]{2,1,0:T(4,128)S(1)}, f32[2,3,512]{2,1,0:T(4,128)S(1)}, u32[]{:S(2)}, u32[]{:S(2)}) collective-permute-start(f32[2,3,512]{2,1,0:T(4,128)S(1)} %copy.27), channel_id=1, source_target_pairs={{0,4},{4,0},{8,12},{12,8},{1,5},{5,1},{9,13},{13,9},{2,6},{6,2},{1... | collective-permute-start | bytes 36872 | tf_op jit(solution)/shard_map/ppermute | solution.py:372
  4.4 2.5 %collective-permute-start.1 = (f32[2,3,512]{2,1,0:T(4,128)S(1)}, f32[2,3,512]{2,1,0:T(4,128)S(1)}, u32[]{:S(2)}, u32[]{:S(2)}) collective-permute-start(f32[2,3,512]{2,1,0:T(4,128)S(1)} %copy.27), channel_id=1, source_target_pairs={{0,12},{4,8},{8,4},{12,0},{1,13},{5,9},{9,5},{13,1},{2,14},{6,10},... | collective-permute-start | bytes 36872 | tf_op jit(solution)/shard_map/ppermute | solution.py:372
  7.1 0.7 %copy-done.9 = s32[512]{0:T(512)S(1)} copy-done((s32[512]{0:T(512)S(1)}, s32[512]{0:T(512)}, u32[]{:S(2)}) %copy-start.9) | copy-done | bytes 2072
  7.7 0.7 %copy-done.7 = f32[4,8]{1,0:T(4,128)S(1)} copy-done((f32[4,8]{1,0:T(4,128)S(1)}, f32[4,8]{1,0:T(4,128)}, u32[]{:S(2)}) %copy-start.7) | copy-done | bytes 152
  8.4 0.7 %fusion.20 = (f32[1,1]{1,0:T(1,128)}, f32[1,1]{1,0:T(1,128)}, f32[1,1]{1,0:T(1,128)}, f32[1,1]{1,0:T(1,128)}, f32[1,1]{1,0:T(1,128)}, /*index=5*/f32[1,1]{1,0:T(...) fusion(f32[4,8]{1,0:T(4,128)S(1)} %copy-done.7, ...), kind=kLoop, calls=%fused_computation.53 | loop fusion | bytes 180 | tf_op jit(solution)/shard_map/dynamic_slice | solution.py:451
  9.1 1.0 %collective-permute-done.1 = f32[2,3,512]{2,1,0:T(4,128)S(1)} collective-permute-done((f32[2,3,512]{2,1,0:T(4,128)S(1)}, f32[2,3,512]{2,1,0:T(4,128)S(1)}, u32[]{:S(2)}, u32[]{:S(2)}) %collective-permute-start.1) | collective-permute-done | bytes 12320 | tf_op jit(solution)/shard_map/ppermute | solution.py:372
  10.1 1.4 %collective-permute-done.2 = f32[2,3,512]{2,1,0:T(4,128)S(1)} collective-permute-done((f32[2,3,512]{2,1,0:T(4,128)S(1)}, f32[2,3,512]{2,1,0:T(4,128)S(1)}, u32[]{:S(2)}, u32[]{:S(2)}) %collective-permute-start.2) | collective-permute-done | bytes 12320 | tf_op jit(solution)/shard_map/ppermute | solution.py:372
  11.5 5.0 %slice_select_fusion.1 = (f32[1,3,512]{2,1,0:T(4,128)S(1)}, f32[3,512]{1,0:T(4,128)S(1)}) fusion(f32[2,3,512]{2,1,0:T(4,128)S(1)} %collective-permute-done.1, f32[2,3,512]{2,1,0:T(4,128)S(1)} %collective-permute-done, pred[]{:T(512)S(6)} %eq.34, f32[]{:T(128)} %bitcast.8, f32[]{:T(128)} %bitcast.7, f32[2,3,512]{2,1,0:T(4,128)S(1)} %collective-permute-done.2, ...), kind=kLoop, calls=%fused_computation.32 | loop fusion | flops 24576 | bytes 61473 | tf_op jit(solution)/shard_map/jit(_where)/select_n | solution.py:382
  16.6 1.6 %collective-permute-start.4 = (f32[8,128]{1,0:T(8,128)S(1)}, f32[8,128]{1,0:T(8,128)S(1)}, u32[]{:S(2)}, u32[]{:S(2)}) collective-permute-start(f32[8,128]{1,0:T(8,128)S(1)} %get-tuple-element.29), channel_id=1, source_target_pairs={{0,1},{1,0},{2,3},{3,2},{4,5},{5,4},{6,7},{7,6},{8,9},{9,8},{10,11... | collective-permute-start | bytes 12296 | tf_op jit(solution)/shard_map/ppermute | solution.py:328
  18.2 0.7 %copy-done.10 = f32[256,4]{0,1:T(4,128)S(1)} copy-done((f32[256,4]{0,1:T(4,128)S(1)}, f32[256,4]{0,1:T(4,128)}, u32[]{:S(2)}) %copy-start.10) | copy-done | bytes 4120
  18.9 0.8 %copy.35.emb = f32[256,4]{1,0:T(8,128)} copy(f32[256,4]{0,1:T(4,128)S(1)} %copy-done.10) | data formatting | bytes 8192 | tf_op args[7]
  19.7 0.7 %copy-done.12 = f32[256]{0:T(256)S(1)} copy-done((f32[256]{0:T(256)S(1)}, f32[256]{0:T(256)}, u32[]{:S(2)}) %copy-start.12) | copy-done | bytes 1048
  20.5 0.7 %copy-done.13 = f32[32]{0:T(128)S(1)} copy-done((f32[32]{0:T(128)S(1)}, f32[32]{0:T(128)}, u32[]{:S(2)}) %copy-start.13) | copy-done | bytes 152
  21.3 2.5 %split_weights.1 = (bf16[256,512]{1,0:T(8,128)(2,1)}, bf16[512,256]{1,0:T(8,128)(2,1)}, bf16[512,256]{1,0:T(8,128)(2,1)}, bf16[256,256]{1,0:T(8,128)(2,1)}, bf16...) custom-call(f32[256,128]{1,0:T(8,128)} %w1.1, f32[256,4]{1,0:T(8,128)} %copy.35.emb, f32[256,256]{1,0:T(8,128)} %w2.1, ...), custom_call_target="tpu_custom_call" | custom-call | tf_op jit(solution)/shard_map/split_weights/pallas_call | solution.py:86
  23.8 0.9 %copy-done = bf16[256,512]{1,0:T(8,128)(2,1)S(1)} copy-done((bf16[256,512]{1,0:T(8,128)(2,1)S(1)}, bf16[256,512]{1,0:T(8,128)(2,1)}, u32[]{:S(2)}) %copy-start) | copy-done | bytes 262168
  24.7 0.9 %copy-done.1 = bf16[512,256]{1,0:T(8,128)(2,1)S(1)} copy-done((bf16[512,256]{1,0:T(8,128)(2,1)S(1)}, bf16[512,256]{1,0:T(8,128)(2,1)}, u32[]{:S(2)}) %copy-start.1) | copy-done | bytes 262168
  25.7 0.9 %copy-done.2 = bf16[512,256]{1,0:T(8,128)(2,1)S(1)} copy-done((bf16[512,256]{1,0:T(8,128)(2,1)S(1)}, bf16[512,256]{1,0:T(8,128)(2,1)}, u32[]{:S(2)}) %copy-start.2) | copy-done | bytes 262168
  26.6 0.9 %copy-done.3 = bf16[512,256]{1,0:T(8,128)(2,1)S(1)} copy-done((bf16[512,256]{1,0:T(8,128)(2,1)S(1)}, bf16[512,256]{1,0:T(8,128)(2,1)}, u32[]{:S(2)}) %copy-start.3) | copy-done | bytes 262168
  27.6 0.9 %copy-done.4 = bf16[512,256]{1,0:T(8,128)(2,1)S(1)} copy-done((bf16[512,256]{1,0:T(8,128)(2,1)S(1)}, bf16[512,256]{1,0:T(8,128)(2,1)}, u32[]{:S(2)}) %copy-start.4) | copy-done | bytes 262168
  28.5 0.9 %copy-done.5 = bf16[256,256]{1,0:T(8,128)(2,1)S(1)} copy-done((bf16[256,256]{1,0:T(8,128)(2,1)S(1)}, bf16[256,256]{1,0:T(8,128)(2,1)}, u32[]{:S(2)}) %copy-start.5) | copy-done | bytes 131096
  29.4 4.5 %window_forces.1 = f32[8,768]{1,0:T(8,128)S(1)} custom-call(f32[8,768]{1,0:T(8,128)S(1)} %pad_maximum_fusion.ext, s32[32,512]{1,0:T(8,128)S(1)} %select_add_fusion.code, f32[32,1]{1,0:T(8,128)S(1)} %copy.36.rates, f32[256,1]{1,0:T(8,128)S(1)} %copy.37.wout, bf16[256,512]{1,0:T(8,128)(2,1)S(1)} %copy-done, bf16[512,256]{1,0:T(8,128)(2,1)S(1)} %copy-done.1, ...), custom_call_target="tpu_custom_call" | custom-call | tf_op jit(solution)/shard_map/window_forces/pallas_call | solution.py:303
  34.0 0.9 %collective-permute-start.5 = (f32[3,128]{1,0:T(4,128)S(1)}, f32[3,128]{1,0:T(4,128)S(1)}, u32[]{:S(2)}, u32[]{:S(2)}) collective-permute-start(f32[3,128]{1,0:T(4,128)S(1)} %get-tuple-element.26), channel_id=1, source_target_pairs={{0,3},{1,2},{2,1},{3,0},{4,7},{5,6},{6,5},{7,4},{8,11},{9,10},{10,... | collective-permute-start | bytes 4616 | tf_op jit(solution)/shard_map/ppermute | solution.py:329
  34.9 2.2 %collective-permute-done.5 = f32[3,128]{1,0:T(4,128)S(1)} collective-permute-done((f32[3,128]{1,0:T(4,128)S(1)}, f32[3,128]{1,0:T(4,128)S(1)}, u32[]{:S(2)}, u32[]{:S(2)}) %collective-permute-start.5) | collective-permute-done | bytes 1568 | tf_op jit(solution)/shard_map/ppermute | solution.py:329
  37.1 0.8 %collective-permute-start.7 = (f32[3,512]{1,0:T(4,128)S(1)}, f32[3,512]{1,0:T(4,128)S(1)}, u32[]{:S(2)}, u32[]{:S(2)}) collective-permute-start(f32[3,512]{1,0:T(4,128)S(1)} %pad_maximum_fusion.3), channel_id=1, source_target_pairs={{0,4},{4,0},{8,12},{12,8},{1,5},{5,1},{9,13},{13,9},{2,6},{6,2},{1... | collective-permute-start | bytes 18440 | tf_op jit(solution)/shard_map/ppermute | solution.py:448
  37.9 1.2 %collective-permute-start.8 = (f32[3,512]{1,0:T(4,128)S(1)}, f32[3,512]{1,0:T(4,128)S(1)}, u32[]{:S(2)}, u32[]{:S(2)}) collective-permute-start(f32[3,512]{1,0:T(4,128)S(1)} %pad_maximum_fusion.3), channel_id=1, source_target_pairs={{0,8},{4,12},{8,0},{12,4},{1,9},{5,13},{9,1},{13,5},{2,10},{6,14},... | collective-permute-start | bytes 18440 | tf_op jit(solution)/shard_map/ppermute | solution.py:448
  39.1 2.5 %collective-permute-start.9 = (f32[3,512]{1,0:T(4,128)S(1)}, f32[3,512]{1,0:T(4,128)S(1)}, u32[]{:S(2)}, u32[]{:S(2)}) collective-permute-start(f32[3,512]{1,0:T(4,128)S(1)} %pad_maximum_fusion.3), channel_id=1, source_target_pairs={{0,12},{4,8},{8,4},{12,0},{1,13},{5,9},{9,5},{13,1},{2,14},{6,10},... | collective-permute-start | bytes 18440 | tf_op jit(solution)/shard_map/ppermute | solution.py:448
  41.6 0.8 %collective-permute-done.8 = f32[3,512]{1,0:T(4,128)S(1)} collective-permute-done((f32[3,512]{1,0:T(4,128)S(1)}, f32[3,512]{1,0:T(4,128)S(1)}, u32[]{:S(2)}, u32[]{:S(2)}) %collective-permute-start.8) | collective-permute-done | bytes 6176 | tf_op jit(solution)/shard_map/ppermute | solution.py:448
  42.4 2.1 %collective-permute-done.9 = f32[3,512]{1,0:T(4,128)S(1)} collective-permute-done((f32[3,512]{1,0:T(4,128)S(1)}, f32[3,512]{1,0:T(4,128)S(1)}, u32[]{:S(2)}, u32[]{:S(2)}) %collective-permute-start.9) | collective-permute-done | bytes 6176 | tf_op jit(solution)/shard_map/ppermute | solution.py:448
  44.5 5.0 %add_bitcast_fusion.1 = (f32[1,3,512]{2,1,0:T(4,128)S(1)}, f32[1,3,512]{2,1,0:T(4,128)S(1)}) fusion(f32[3,512]{1,0:T(4,128)S(1)} %collective-permute-done.9, f32[3,512]{1,0:T(4,128)S(1)} %collective-permute-done.8, f32[3,512]{1,0:T(4,128)S(1)} %collective-permute-done.7, f32[]{:T(128)} %bitcast.15, f32[]{:T(128)} %bitcast.14, f32[]{:T(128)} %bitcast.13, ...), kind=kLoop, calls=%fused_computation.30 | loop fusion | flops 24576 | bytes 36896 | tf_op jit(solution)/shard_map/stack | solution.py:452
  49.6 0.6 %copy.39 = f32[2,3,512]{2,0,1:T(2,128)} copy(f32[2,3,512]{2,1,0:T(4,128)S(1)} %get-tuple-element.19) | data formatting | bytes 24576
  50.2 0.6 %copy.40 = f32[2,3,512]{2,0,1:T(2,128)} copy(f32[2,3,512]{2,1,0:T(4,128)S(1)} %get-tuple-element.18) | data formatting | bytes 24576
  (42 shorter events, 0.6 us)
Async XLA Ops:
  1.3 7.8 %collective-permute-start = (f32[2,3,512]{2,1,0:T(4,128)S(1)}, f32[2,3,512]{2,1,0:T(4,128)S(1)}, u32[]{:S(2)}, u32[]{:S(2)}) collective-permute-start(f32[2,3,512]{2,1,0:T(4,128)S(1)} %copy.27), channel_id=1, source_target_pairs={{0,4},{4,0},{8,12},{12,8},{1,5},{5,1},{9,13},{13,9},{2,6},{6,2},{1... | collective-permute-start | bytes 36872 | tf_op jit(solution)/shard_map/ppermute | solution.py:372
  4.4 5.8 %collective-permute-start.1 = (f32[2,3,512]{2,1,0:T(4,128)S(1)}, f32[2,3,512]{2,1,0:T(4,128)S(1)}, u32[]{:S(2)}, u32[]{:S(2)}) collective-permute-start(f32[2,3,512]{2,1,0:T(4,128)S(1)} %copy.27), channel_id=1, source_target_pairs={{0,12},{4,8},{8,4},{12,0},{1,13},{5,9},{9,5},{13,1},{2,14},{6,10},... | collective-permute-start | bytes 36872 | tf_op jit(solution)/shard_map/ppermute | solution.py:372
  6.8 4.6 %collective-permute-start.2 = (f32[2,3,512]{2,1,0:T(4,128)S(1)}, f32[2,3,512]{2,1,0:T(4,128)S(1)}, u32[]{:S(2)}, u32[]{:S(2)}) collective-permute-start(f32[2,3,512]{2,1,0:T(4,128)S(1)} %copy.27), channel_id=1, source_target_pairs={{0,8},{4,12},{8,0},{12,4},{1,9},{5,13},{9,1},{13,5},{2,10},{6,14},... | collective-permute-start | bytes 36872 | tf_op jit(solution)/shard_map/ppermute | solution.py:372
  7.0 0.7 %copy-start.9 = (s32[512]{0:T(512)S(1)}, s32[512]{0:T(512)}, u32[]{:S(2)}) copy-start(s32[512]{0:T(512)} %param.14) | copy-start | bytes 6148
  7.7 0.7 %copy-start.7 = (f32[4,8]{1,0:T(4,128)S(1)}, f32[4,8]{1,0:T(4,128)}, u32[]{:S(2)}) copy-start(f32[4,8]{1,0:T(4,128)} %constant.104.clone) | copy-start | bytes 388
  11.5 6.7 %copy-start.6 = (s32[32,512]{1,0:T(8,128)S(1)}, s32[32,512]{1,0:T(8,128)}, u32[]{:S(2)}) copy-start(s32[32,512]{1,0:T(8,128)} %param.15) | copy-start | bytes 196612
  16.5 7.2 %collective-permute-start.3 = (f32[8,128]{1,0:T(8,128)S(1)}, f32[8,128]{1,0:T(8,128)S(1)}, u32[]{:S(2)}, u32[]{:S(2)}) collective-permute-start(f32[8,128]{1,0:T(8,128)S(1)} %get-tuple-element.28), channel_id=1, source_target_pairs={{0,3},{1,2},{2,1},{3,0},{4,7},{5,6},{6,5},{7,4},{8,11},{9,10},{10,... | collective-permute-start | bytes 12296 | tf_op jit(solution)/shard_map/ppermute | solution.py:329
  16.6 1.6 %copy-start.11 = (s32[512]{0:T(512)S(1)}, s32[512]{0:T(512)}, u32[]{:S(2)}) copy-start(s32[512]{0:T(512)} %param.16) | copy-start | bytes 6148
  16.6 7.1 %collective-permute-start.4 = (f32[8,128]{1,0:T(8,128)S(1)}, f32[8,128]{1,0:T(8,128)S(1)}, u32[]{:S(2)}, u32[]{:S(2)}) collective-permute-start(f32[8,128]{1,0:T(8,128)S(1)} %get-tuple-element.29), channel_id=1, source_target_pairs={{0,1},{1,0},{2,3},{3,2},{4,5},{5,4},{6,7},{7,6},{8,9},{9,8},{10,11... | collective-permute-start | bytes 12296 | tf_op jit(solution)/shard_map/ppermute | solution.py:328
  18.2 0.7 %copy-start.10 = (f32[256,4]{0,1:T(4,128)S(1)}, f32[256,4]{0,1:T(4,128)}, u32[]{:S(2)}) copy-start(f32[256,4]{0,1:T(4,128)} %param.19) | copy-start | bytes 12292
  19.7 0.7 %copy-start.12 = (f32[256]{0:T(256)S(1)}, f32[256]{0:T(256)}, u32[]{:S(2)}) copy-start(f32[256]{0:T(256)} %param.22) | copy-start | bytes 3076
  20.5 0.7 %copy-start.13 = (f32[32]{0:T(128)S(1)}, f32[32]{0:T(128)}, u32[]{:S(2)}) copy-start(f32[32]{0:T(128)} %param.17) | copy-start | bytes 388
  23.8 1.0 %copy-start = (bf16[256,512]{1,0:T(8,128)(2,1)S(1)}, bf16[256,512]{1,0:T(8,128)(2,1)}, u32[]{:S(2)}) copy-start(bf16[256,512]{1,0:T(8,128)(2,1)} %get-tuple-element.8.l1) | copy-start | bytes 786436
  24.7 0.9 %copy-start.1 = (bf16[512,256]{1,0:T(8,128)(2,1)S(1)}, bf16[512,256]{1,0:T(8,128)(2,1)}, u32[]{:S(2)}) copy-start(bf16[512,256]{1,0:T(8,128)(2,1)} %get-tuple-element.9.l2) | copy-start | bytes 786436
  25.7 0.9 %copy-start.2 = (bf16[512,256]{1,0:T(8,128)(2,1)S(1)}, bf16[512,256]{1,0:T(8,128)(2,1)}, u32[]{:S(2)}) copy-start(bf16[512,256]{1,0:T(8,128)(2,1)} %get-tuple-element.10.l3) | copy-start | bytes 786436
  26.6 0.9 %copy-start.3 = (bf16[512,256]{1,0:T(8,128)(2,1)S(1)}, bf16[512,256]{1,0:T(8,128)(2,1)}, u32[]{:S(2)}) copy-start(bf16[512,256]{1,0:T(8,128)(2,1)} %get-tuple-element.12.t2) | copy-start | bytes 786436
  27.6 0.9 %copy-start.4 = (bf16[512,256]{1,0:T(8,128)(2,1)S(1)}, bf16[512,256]{1,0:T(8,128)(2,1)}, u32[]{:S(2)}) copy-start(bf16[512,256]{1,0:T(8,128)(2,1)} %get-tuple-element.13.t3) | copy-start | bytes 786436
  28.5 0.9 %copy-start.5 = (bf16[256,256]{1,0:T(8,128)(2,1)S(1)}, bf16[256,256]{1,0:T(8,128)(2,1)}, u32[]{:S(2)}) copy-start(bf16[256,256]{1,0:T(8,128)(2,1)} %get-tuple-element.11.t1) | copy-start | bytes 393220
  34.0 3.1 %collective-permute-start.5 = (f32[3,128]{1,0:T(4,128)S(1)}, f32[3,128]{1,0:T(4,128)S(1)}, u32[]{:S(2)}, u32[]{:S(2)}) collective-permute-start(f32[3,128]{1,0:T(4,128)S(1)} %get-tuple-element.26), channel_id=1, source_target_pairs={{0,3},{1,2},{2,1},{3,0},{4,7},{5,6},{6,5},{7,4},{8,11},{9,10},{10,... | collective-permute-start | bytes 4616 | tf_op jit(solution)/shard_map/ppermute | solution.py:329
  34.9 2.2 %collective-permute-start.6 = (f32[3,128]{1,0:T(4,128)S(1)}, f32[3,128]{1,0:T(4,128)S(1)}, u32[]{:S(2)}, u32[]{:S(2)}) collective-permute-start(f32[3,128]{1,0:T(4,128)S(1)} %get-tuple-element.27), channel_id=1, source_target_pairs={{0,1},{1,0},{2,3},{3,2},{4,5},{5,4},{6,7},{7,6},{8,9},{9,8},{10,11... | collective-permute-start | bytes 4616 | tf_op jit(solution)/shard_map/ppermute | solution.py:328
  37.1 4.5 %collective-permute-start.7 = (f32[3,512]{1,0:T(4,128)S(1)}, f32[3,512]{1,0:T(4,128)S(1)}, u32[]{:S(2)}, u32[]{:S(2)}) collective-permute-start(f32[3,512]{1,0:T(4,128)S(1)} %pad_maximum_fusion.3), channel_id=1, source_target_pairs={{0,4},{4,0},{8,12},{12,8},{1,5},{5,1},{9,13},{13,9},{2,6},{6,2},{1... | collective-permute-start | bytes 18440 | tf_op jit(solution)/shard_map/ppermute | solution.py:448
  37.9 4.5 %collective-permute-start.8 = (f32[3,512]{1,0:T(4,128)S(1)}, f32[3,512]{1,0:T(4,128)S(1)}, u32[]{:S(2)}, u32[]{:S(2)}) collective-permute-start(f32[3,512]{1,0:T(4,128)S(1)} %pad_maximum_fusion.3), channel_id=1, source_target_pairs={{0,8},{4,12},{8,0},{12,4},{1,9},{5,13},{9,1},{13,5},{2,10},{6,14},... | collective-permute-start | bytes 18440 | tf_op jit(solution)/shard_map/ppermute | solution.py:448
  39.1 5.4 %collective-permute-start.9 = (f32[3,512]{1,0:T(4,128)S(1)}, f32[3,512]{1,0:T(4,128)S(1)}, u32[]{:S(2)}, u32[]{:S(2)}) collective-permute-start(f32[3,512]{1,0:T(4,128)S(1)} %pad_maximum_fusion.3), channel_id=1, source_target_pairs={{0,12},{4,8},{8,4},{12,0},{1,13},{5,9},{9,5},{13,1},{2,14},{6,10},... | collective-permute-start | bytes 18440 | tf_op jit(solution)/shard_map/ppermute | solution.py:448
  44.5 5.0 %copy-start.8 = (f32[2,3,512]{2,0,1:T(2,128)S(1)}, f32[2,3,512]{2,0,1:T(2,128)}, u32[]{:S(2)}) copy-start(f32[2,3,512]{2,0,1:T(2,128)} %param.13) | copy-start | bytes 36868
where the time goes:
time: 51.5 us; the launch traced here: 50.8 us
  local copies, waits for them, and re-layouts  12.7 us (25%)
  starting transfers between devices  12.6 us (24%)
  other arithmetic  10.1 us (20%)
  waiting for transfers between devices  7.49 us (15%)
  Pallas kernels  7 us (14%)
  between operations  0.89 us (2%)
    unnamed x32, local copies, waits for them, and re-layouts  11.7 us
    ppermute x3, starting transfers between devices, on_device(): lax.ppermute(positions, 'bead', [(i, i ^ k) for i in range(bead_groups)])  5.62 us
    another operation x1, other arithmetic, on_device(): expanded = jnp.stack(expanded)  5.02 us
    select_n x1, other arithmetic, on_device(): below = jnp.where(odd_place, near[-1], far[-1])  5 us
    pallas_call x1, Pallas kernels, window_forces(): pl.pallas_call(force_kernel, out_shape=jax.ShapeDtypeStruct((8, block + 2...  4.54 us
    ppermute x3, starting transfers between devices, on_device(): block = lax.ppermute(own, 'bead', [(i, i ^ k) for i in range(bead_groups)])  4.48 us
    ppermute x3, waiting for transfers between devices, on_device(): block = lax.ppermute(own, 'bead', [(i, i ^ k) for i in range(bead_groups)])  2.96 us
    pallas_call x1, Pallas kernels, split_weights(): pl.pallas_call(weights_kernel, out_shape=[jax.ShapeDtypeStruct(s, jnp.bfl...  2.46 us
  transfers between devices with their start and end apart: 10, of which 5 were waited for; matrix products, arithmetic and copies ran while one was open for 4% of the time, Pallas kernels for 5%

commit v1 on v0

--- a/solution.py
+++ b/solution.py
@@ -54,25 +54,33 @@
     )
 
 
-def weights_kernel(w1, emb, w2, w3, l1, l2, l3, t1, t2, t3):
+def weights_kernel(w1, emb, w2, w3, rates, wout, l1, l2, l3, t1, t2, t3, rates_b, wout_b):
     hid, chan = w1.shape
     high, low = split2(w1[...])
     l1[:, 0:chan] = high
     l1[:, 2 * chan : 3 * chan] = low
     l1[:, 3 * chan : 4 * chan] = high
     e = emb[...]
-    eh, el = split2(e)
-    ell = (e - eh.astype(jnp.float32) - el.astype(jnp.float32)).astype(jnp.bfloat16)
-    l1[:, chan : 2 * chan] = jnp.concatenate(
-        [eh, el, ell, jnp.zeros((hid, chan - 3 * SPECIES), jnp.bfloat16)], axis=1
-    )
+    eh = e.astype(jnp.bfloat16).astype(jnp.float32)
+    el = (e - eh).astype(jnp.bfloat16).astype(jnp.float32)
+    terms = jnp.concatenate([eh, el, e - eh - el, jnp.zeros_like(e)], axis=0)
+    terms = jnp.concatenate(
+        [terms, jnp.zeros((chan - 4 * SPECIES, hid), jnp.float32)], axis=0
+    )
+    l1[:, chan : 2 * chan] = terms.T.astype(jnp.bfloat16)
     t1[0:chan, :], t1[chan : 2 * chan, :] = split2(w1[...].T)
     for src, fwd, bwd in ((w2, l2, t2), (w3, l3, t3)):
         fwd[0:hid, :], fwd[hid : 2 * hid, :] = split2(src[...])
         bwd[0:hid, :], bwd[hid : 2 * hid, :] = split2(src[...].T)
-
-
-def split_weights(w1, emb, w2, w3):
+    count = rates.shape[1]
+    tall = jnp.concatenate(
+        [rates[...], jnp.zeros((1, LANES - count), jnp.float32)], axis=1
+    )
+    rates_b[...] = jnp.broadcast_to(tall, (LANES, LANES)).T[0:count, :]
+    wout_b[...] = jnp.broadcast_to(wout[...], (LANES, hid)).T
+
+
+def split_weights(w1, emb, w2, w3, rates, wout):
     hid, chan = w1.shape
     vmem = pl.BlockSpec(memory_space=pltpu.VMEM)
     shapes = [
@@ -83,26 +91,31 @@
         (2 * hid, hid),
         (2 * hid, hid),
     ]
+    out_shape = [pltpu.VMEM(s, jnp.bfloat16) for s in shapes]
+    out_shape += [
+        pltpu.VMEM((rates.shape[0], LANES), jnp.float32),
+        pltpu.VMEM((hid, LANES), jnp.float32),
+    ]
     return pl.pallas_call(
         weights_kernel,
-        out_shape=[jax.ShapeDtypeStruct(s, jnp.bfloat16) for s in shapes],
-        in_specs=[vmem] * 4,
-        out_specs=[vmem] * len(shapes),
+        out_shape=out_shape,
+        in_specs=[vmem] * 6,
+        out_specs=[vmem] * len(out_shape),
         name="split_weights",
-    )(w1, emb, w2, w3)
+    )(w1, emb.T, w2, w3, rates[None, :], wout[None, :])
 
 
 def force_kernel(
     ext,
     code,
-    rates,
-    wout,
     l1,
     l2,
     l3,
     t1,
     t2,
     t3,
+    rates,
+    wout,
     out,
     off_s,
     kind_s,
@@ -120,11 +133,7 @@
     chan = SPECIES * rate_count
     hid = wout.shape[0]
     band = LANES + 2 * HALO
-    rates2 = rates[...] * (-LOG2E)
-    rate8 = [
-        jnp.broadcast_to(rates2[8 * o : 8 * o + 8, :], (8, LANES))
-        for o in range(octets)
-    ]
+    rate8 = [rates[8 * o : 8 * o + 8, :] * (-LOG2E) for o in range(octets)]
 
     for g in range(groups):
         lane0 = g * LANES
@@ -201,14 +210,12 @@
     h1, s1 = act(first)
     h2, s2 = act(layer(l2, h1))
     _, s3 = act(layer(l3, h2))
-    g3 = wout[...] * s3
+    g3 = jnp.concatenate([wout[...]] * groups, axis=1) * s3
     g2 = layer(t3, g3) * s2
     g1 = layer(t2, g2) * s1
     grad_s[...] = layer(t1, g1)
 
-    rate_true = [
-        jnp.broadcast_to(rates[8 * o : 8 * o + 8, :], (8, LANES)) for o in range(octets)
-    ]
+    rate_true = [rates[8 * o : 8 * o + 8, :] for o in range(octets)]
     for g in range(groups):
         cols = slice(g * LANES, (g + 1) * LANES)
         grads = [
@@ -295,9 +302,9 @@
         )
 
 
-def window_forces(ext, code, rates, wout, pairs):
+def window_forces(ext, code, prepared):
     slots, block = code.shape
-    rate_count = rates.shape[0]
+    rate_count = prepared[6].shape[0]
     vmem = pl.BlockSpec(memory_space=pltpu.VMEM)
     f32 = jnp.float32
     return pl.pallas_call(
@@ -317,7 +324,7 @@
         ],
         compiler_params=pltpu.CompilerParams(vmem_limit_bytes=32 * 1024 * 1024),
         name="window_forces",
-    )(ext, code, rates[:, None], wout[:, None], *pairs)
+    )(ext, code, *prepared)
 
 
 def swap_with_adjacent(send_inner, send_outer):
@@ -348,7 +355,7 @@
     bead_groups = lax.axis_size("bead")
     slab_count = lax.axis_size("space")
     bead_count = bead_dev * bead_groups
-    table = jnp.asarray(contraction_table(bead_count, NC))
+    table = contraction_table(bead_count, NC)
     place = lax.axis_index("bead")
     slab = lax.axis_index("space")
     even = slab % 2 == 0
@@ -357,7 +364,9 @@
     block_start = (place // NC) * block_size
     direct = bead_groups == NC
 
-    pairs = split_weights(weight_input, embedding, weight_middle, weight_deeper)
+    prepared = split_weights(
+        weight_input, embedding, weight_middle, weight_deeper, radial_rates, weight_output
+    )
 
     slots = lax.dynamic_slice_in_dim(neighbour_index, block_start, block_size, 1)
     counts = lax.dynamic_slice_in_dim(neighbour_count, block_start, block_size, 0)
@@ -367,30 +376,40 @@
     group_first = lax.broadcasted_iota(jnp.int32, slots.shape, 1) // LANES * LANES
     code = slots - block_start - group_first + jnp.where(live, 0, DEAD)
 
+    own_beads = positions.transpose(1, 0, 2)
     if direct:
-        others = [
-            lax.ppermute(positions, "bead", [(i, i ^ k) for i in range(bead_groups)])
-            for k in range(1, bead_groups)
+        pairs = [[(i, i ^ k) for i in range(NC)] for k in range(NC)]
+        blocks = [own_beads] + [
+            lax.ppermute(own_beads, "bead", pairs[k]) for k in range(1, NC)
         ]
-        contracted = jnp.zeros(positions.shape[1:], jnp.float32)
-        for k, block in enumerate([positions] + others):
-            owner = jnp.bitwise_xor(place, k)
+        odd_place = place % 2 == 1
+
+        def share(k, j, expand):
+            ahead, behind = k % NC, -k % NC
+            if expand:
+                values = table[ahead, j], table[behind, j]
+            else:
+                values = table[0, ahead * bead_dev + j], table[0, behind * bead_dev + j]
+            if values[0] == values[1]:
+                return values[0]
+            return jnp.where(odd_place, values[1], values[0])
+
+        contracted = jnp.zeros((3, atom_dev), jnp.float32)
+        for k in range(NC):
             for j in range(bead_dev):
-                contracted = contracted + table[replica, owner * bead_dev + j] * block[j]
-        odd_place = place % 2 == 1
-        near, far = others[0], others[bead_groups - 2]
-        below = jnp.where(odd_place, near[-1], far[-1])
-        above = jnp.where(odd_place, far[0], near[0])
+                contracted = contracted + share(k, j, False) * blocks[k][:, j]
+        below = jnp.where(odd_place, blocks[1][:, -1], blocks[NC - 1][:, -1])
+        above = jnp.where(odd_place, blocks[NC - 1][:, 0], blocks[1][:, 0])
     else:
-        everything = lax.all_gather(positions, "bead", axis=0, tiled=True)
-        weights = lax.dynamic_index_in_dim(table, replica, 0, keepdims=False)
-        contracted = jnp.sum(weights[:, None, None] * everything, axis=0)
+        everything = lax.all_gather(own_beads, "bead", axis=1, tiled=True)
+        weights = lax.dynamic_index_in_dim(jnp.asarray(table), replica, 0, keepdims=False)
+        contracted = jnp.sum(weights[None, :, None] * everything, axis=1)
         first = place * bead_dev
         below = lax.dynamic_index_in_dim(
-            everything, (first - 1) % bead_count, 0, keepdims=False
+            everything, (first - 1) % bead_count, 1, keepdims=False
         )
         above = lax.dynamic_index_in_dim(
-            everything, (first + bead_dev) % bead_count, 0, keepdims=False
+            everything, (first + bead_dev) % bead_count, 1, keepdims=False
         )
 
     stacked = jnp.concatenate(
@@ -414,7 +433,7 @@
         axis=1,
     )
     window = lax.dynamic_slice_in_dim(extended, block_start, block_size + 2 * HALO, 1)
-    force = window_forces(window, code, radial_rates, weight_output, pairs)[:3]
+    force = window_forces(window, code, prepared)[:3]
 
     if not direct:
         partial = jnp.zeros((3, atom_dev + 2 * HALO), jnp.float32)
@@ -441,27 +460,25 @@
 
     if direct:
         expanded = [jnp.zeros((3, atom_dev), jnp.float32)] * bead_dev
-        for k in range(bead_groups):
-            if k == 0:
-                block = own
-            else:
-                block = lax.ppermute(own, "bead", [(i, i ^ k) for i in range(bead_groups)])
-            owner = jnp.bitwise_xor(place, k)
+        for k in range(NC):
+            block = lax.ppermute(own, "bead", pairs[k]) if k else own
             for j in range(bead_dev):
-                expanded[j] = expanded[j] + table[owner, place * bead_dev + j] * block
-        expanded = jnp.stack(expanded)
+                expanded[j] = expanded[j] + share(k, j, True) * block
+        expanded = jnp.stack(expanded, axis=1)
     else:
-        columns = lax.dynamic_slice_in_dim(table, place * bead_dev, bead_dev, 1)
-        expanded = jnp.sum(columns[:, :, None, None] * own[:, None], axis=0)
+        columns = lax.dynamic_slice_in_dim(
+            jnp.asarray(table), place * bead_dev, bead_dev, 1
+        )
+        expanded = jnp.sum(columns[:, None, :, None] * own[:, :, None, :], axis=0)
     expanded = bead_count / NC * expanded
 
     masses = per_species(species, MASS_TABLE)
-    cycle = jnp.concatenate([below[None], positions, above[None]], axis=0)
-    laplace = 2.0 * positions - cycle[:-2] - cycle[2:]
-    spring = -SPRING_RATE * masses[None, None, :] * laplace
-    momenta_next = momenta + TIME_STEP * (spring + expanded)
-    displacement = TIME_STEP * momenta_next / masses[None, None, :]
-    return (momenta_next, displacement)
+    cycle = jnp.concatenate([below[:, None], own_beads, above[:, None]], axis=1)
+    laplace = 2.0 * own_beads - cycle[:, :-2] - cycle[:, 2:]
+    spring = -SPRING_RATE * masses * laplace
+    momenta_next = momenta.transpose(1, 0, 2) + TIME_STEP * (spring + expanded)
+    displacement = TIME_STEP * momenta_next / masses
+    return (momenta_next.transpose(1, 0, 2), displacement.transpose(1, 0, 2))
 
 
 def solution(mesh):

time: 51.5 us -> 32.2 us (0.63)
  other arithmetic: 10.1 us -> 0.15 us
  local copies, waits for them, and re-layouts: 12.7 us -> 3.3 us
  waiting for transfers between devices: 7.49 us -> 8.37 us
  Pallas kernels: 7 us -> 6.13 us
  starting transfers between devices: 12.6 us -> 13.2 us
    unnamed x32 -> x11, local copies, waits for them, and re-layouts: 11.7 us -> 3.3 us
    another operation x1, other arithmetic: 5.02 us -> 0.01 us  [on_device(): expanded = jnp.stack(expanded, axis=1)]
    select_n x2 -> x1, other arithmetic: 5 us -> 0.02 us  [on_device(): below = jnp.where(odd_place, blocks[1][:, -1], blocks[NC - 1][:, -1])]
    ppermute x6, waiting for transfers between devices: 5.31 us -> 6.75 us  [the longest x3 3.79 us: on_device(): lax.ppermute(own_beads, 'bead', pairs[k])]
    pallas_call x1, Pallas kernels: 2.46 us -> 1.58 us  [split_weights(): pl.pallas_call(weights_kernel, out_shape=out_shape, in_specs=[vmem] * 6,...]
    dynamic_slice x1 -> x0, local copies, waits for them, and re-layouts: 0.71 us -> none  [on_device(): expanded[j] = expanded[j] + table[owner, place * bead_dev + j] * block]
    ppermute x2, starting transfers between devices: 1.59 us -> 2.16 us  [swap_with_adjacent(): lax.ppermute(send_inner, 'space', inner)]
    ppermute x2, waiting for transfers between devices: 2.18 us -> 1.62 us  [swap_with_adjacent(): lax.ppermute(send_outer, 'space', outer)]
  transfers between devices with their start and end apart: 10 -> 10, of which waited for: 5 -> 5; matrix products, arithmetic and copies ran while one was open for 4% -> 0% of each run, Pallas kernels for 5% -> 5%
where the time goes in v1:
time: 32.2 us; the launch traced here: 31.9 us
  starting transfers between devices  13.2 us (41%)
  waiting for transfers between devices  8.37 us (26%)
  Pallas kernels  6.13 us (19%)
  local copies, waits for them, and re-layouts  3.3 us (10%)
  between operations  0.79 us (2%)
    ppermute x3, starting transfers between devices, on_device(): lax.ppermute(own_beads, 'bead', pairs[k])  5.62 us
    pallas_call x1, Pallas kernels, window_forces(): pl.pallas_call(force_kernel, out_shape=jax.ShapeDtypeStruct((8, block + 2...  4.56 us
    ppermute x3, starting transfers between devices, on_device(): block = lax.ppermute(own, 'bead', pairs[k]) if k else own  4.45 us
    ppermute x3, waiting for transfers between devices, on_device(): lax.ppermute(own_beads, 'bead', pairs[k])  3.79 us
    unnamed x11, local copies, waits for them, and re-layouts  3.3 us
    ppermute x3, waiting for transfers between devices, on_device(): block = lax.ppermute(own, 'bead', pairs[k]) if k else own  2.96 us
    ppermute x2, starting transfers between devices, swap_with_adjacent(): lax.ppermute(send_inner, 'space', inner)  2.16 us
    ppermute x2, waiting for transfers between devices, swap_with_adjacent(): lax.ppermute(send_outer, 'space', outer)  1.62 us
  transfers between devices with their start and end apart: 10, of which 5 were waited for; matrix products, arithmetic and copies ran while one was open for 0% of the time, Pallas kernels for 5%

profile of v1, /device:TPU:0, one launch (start us, length us, event | category | flops | bytes accessed | tf_op | source)
XLA Modules:
  0.0 31.9 jit_solution(5369863734626053434)
XLA Ops:
  0.6 0.7 %copy.20 = f32[2,3,512]{2,1,0:T(4,128)S(1)} copy(f32[2,3,512]{2,0,1:T(2,128)} %param.11) | data formatting | bytes 24576 | tf_op args[0]
  1.3 3.0 %collective-permute-start = (f32[3,2,512]{2,0,1:T(4,128)S(1)}, f32[3,2,512]{2,0,1:T(4,128)S(1)}, u32[]{:S(2)}, u32[]{:S(2)}) collective-permute-start(f32[3,2,512]{2,0,1:T(4,128)S(1)} %bitcast.19), channel_id=1, source_target_pairs={{0,4},{4,0},{8,12},{12,8},{1,5},{5,1},{9,13},{13,9},{2,6},{6,2},{1... | collective-permute-start | bytes 36872 | tf_op jit(solution)/shard_map/ppermute | solution.py:383
  4.4 2.5 %collective-permute-start.1 = (f32[3,2,512]{2,0,1:T(4,128)S(1)}, f32[3,2,512]{2,0,1:T(4,128)S(1)}, u32[]{:S(2)}, u32[]{:S(2)}) collective-permute-start(f32[3,2,512]{2,0,1:T(4,128)S(1)} %bitcast.20), channel_id=1, source_target_pairs={{0,12},{4,8},{8,4},{12,0},{1,13},{5,9},{9,5},{13,1},{2,14},{6,10},... | collective-permute-start | bytes 36872 | tf_op jit(solution)/shard_map/ppermute | solution.py:383
  6.8 0.1 collective-permute-start.2
  7.0 0.0 copy-start.2
  7.0 0.7 %copy-done.2 = s32[512]{0:T(512)S(1)} copy-done((s32[512]{0:T(512)S(1)}, s32[512]{0:T(512)}, u32[]{:S(2)}) %copy-start.2) | copy-done | bytes 2072
  7.7 0.0 copy-start
  7.7 0.0 collective-permute-done
  7.7 2.4 %collective-permute-done.1 = f32[3,2,512]{2,0,1:T(4,128)S(1)} collective-permute-done((f32[3,2,512]{2,0,1:T(4,128)S(1)}, f32[3,2,512]{2,0,1:T(4,128)S(1)}, u32[]{:S(2)}, u32[]{:S(2)}) %collective-permute-start.1) | collective-permute-done | bytes 12320 | tf_op jit(solution)/shard_map/ppermute | solution.py:383
  10.1 1.4 %collective-permute-done.2 = f32[3,2,512]{2,0,1:T(4,128)S(1)} collective-permute-done((f32[3,2,512]{2,0,1:T(4,128)S(1)}, f32[3,2,512]{2,0,1:T(4,128)S(1)}, u32[]{:S(2)}, u32[]{:S(2)}) %collective-permute-start.2) | collective-permute-done | bytes 12320 | tf_op jit(solution)/shard_map/ppermute | solution.py:383
  11.5 0.1 collective-permute-start.3
  11.6 0.0 copy-start.3
  11.6 1.6 %collective-permute-start.4 = (f32[8,128]{1,0:T(8,128)S(1)}, f32[8,128]{1,0:T(8,128)S(1)}, u32[]{:S(2)}, u32[]{:S(2)}) collective-permute-start(f32[8,128]{1,0:T(8,128)S(1)} %get-tuple-element.32), channel_id=1, source_target_pairs={{0,1},{1,0},{2,3},{3,2},{4,5},{5,4},{6,7},{7,6},{8,9},{9,8},{10,11... | collective-permute-start | bytes 12296 | tf_op jit(solution)/shard_map/ppermute | solution.py:335
  13.2 0.0 copy-done
  13.2 0.0 copy-done.3
  13.3 1.6 %split_weights.1 = (bf16[256,512]{1,0:T(8,128)(2,1)S(1)}, bf16[512,256]{1,0:T(8,128)(2,1)S(1)}, bf16[512,256]{1,0:T(8,128)(2,1)S(1)}, bf16[256,256]{1,0:T(8,128)...) custom-call(f32[256,128]{1,0:T(8,128)} %w1.1, ...), custom_call_target="tpu_custom_call" | custom-call | tf_op jit(solution)/shard_map/split_weights/pallas_call | solution.py:99
  14.8 0.0 collective-permute-done.3
  14.8 0.0 collective-permute-done.4
  14.9 4.6 %window_forces.1 = f32[8,768]{1,0:T(8,128)S(1)} custom-call(f32[8,768]{1,0:T(8,128)S(1)} %pad_maximum_fusion.ext, s32[32,512]{1,0:T(8,128)S(1)} %select_add_fusion.code, bf16[256,512]{1,0:T(8,128)(2,1)S(1)} %get-tuple-element.10.l1, bf16[512,256]{1,0:T(8,128)(2,1)S(1)} %get-tuple-element.11.l2, bf16[512,256]{1,0:T(8,128)(2,1)S(1)} %get-tuple-element.12.l3, ...), custom_call_target="tpu_custom_call" | custom-call | tf_op jit(solution)/shard_map/window_forces/pallas_call | solution.py:310
  19.5 0.9 %collective-permute-start.5 = (f32[3,128]{1,0:T(4,128)S(1)}, f32[3,128]{1,0:T(4,128)S(1)}, u32[]{:S(2)}, u32[]{:S(2)}) collective-permute-start(f32[3,128]{1,0:T(4,128)S(1)} %get-tuple-element.29), channel_id=1, source_target_pairs={{0,3},{1,2},{2,1},{3,0},{4,7},{5,6},{6,5},{7,4},{8,11},{9,10},{10,... | collective-permute-start | bytes 4616 | tf_op jit(solution)/shard_map/ppermute | solution.py:336
  20.3 0.6 %collective-permute-start.6 = (f32[3,128]{1,0:T(4,128)S(1)}, f32[3,128]{1,0:T(4,128)S(1)}, u32[]{:S(2)}, u32[]{:S(2)}) collective-permute-start(f32[3,128]{1,0:T(4,128)S(1)} %get-tuple-element.30), channel_id=1, source_target_pairs={{0,1},{1,0},{2,3},{3,2},{4,5},{5,4},{6,7},{7,6},{8,9},{9,8},{10,11... | collective-permute-start | bytes 4616 | tf_op jit(solution)/shard_map/ppermute | solution.py:335
  20.9 1.6 %collective-permute-done.5 = f32[3,128]{1,0:T(4,128)S(1)} collective-permute-done((f32[3,128]{1,0:T(4,128)S(1)}, f32[3,128]{1,0:T(4,128)S(1)}, u32[]{:S(2)}, u32[]{:S(2)}) %collective-permute-start.5) | collective-permute-done | bytes 1568 | tf_op jit(solution)/shard_map/ppermute | solution.py:336
  22.5 0.0 collective-permute-done.6
  22.6 0.8 %collective-permute-start.7 = (f32[3,512]{1,0:T(4,128)S(1)}, f32[3,512]{1,0:T(4,128)S(1)}, u32[]{:S(2)}, u32[]{:S(2)}) collective-permute-start(f32[3,512]{1,0:T(4,128)S(1)} %pad_maximum_fusion.3), channel_id=1, source_target_pairs={{0,4},{4,0},{8,12},{12,8},{1,5},{5,1},{9,13},{13,9},{2,6},{6,2},{1... | collective-permute-start | bytes 18440 | tf_op jit(solution)/shard_map/ppermute | solution.py:464
  23.4 1.2 %collective-permute-start.8 = (f32[3,512]{1,0:T(4,128)S(1)}, f32[3,512]{1,0:T(4,128)S(1)}, u32[]{:S(2)}, u32[]{:S(2)}) collective-permute-start(f32[3,512]{1,0:T(4,128)S(1)} %pad_maximum_fusion.3), channel_id=1, source_target_pairs={{0,8},{4,12},{8,0},{12,4},{1,9},{5,13},{9,1},{13,5},{2,10},{6,14},... | collective-permute-start | bytes 18440 | tf_op jit(solution)/shard_map/ppermute | solution.py:464
  24.5 2.5 %collective-permute-start.9 = (f32[3,512]{1,0:T(4,128)S(1)}, f32[3,512]{1,0:T(4,128)S(1)}, u32[]{:S(2)}, u32[]{:S(2)}) collective-permute-start(f32[3,512]{1,0:T(4,128)S(1)} %pad_maximum_fusion.3), channel_id=1, source_target_pairs={{0,12},{4,8},{8,4},{12,0},{1,13},{5,9},{9,5},{13,1},{2,14},{6,10},... | collective-permute-start | bytes 18440 | tf_op jit(solution)/shard_map/ppermute | solution.py:464
  27.0 0.0 collective-permute-done.7
  27.0 0.9 %collective-permute-done.8 = f32[3,512]{1,0:T(4,128)S(1)} collective-permute-done((f32[3,512]{1,0:T(4,128)S(1)}, f32[3,512]{1,0:T(4,128)S(1)}, u32[]{:S(2)}, u32[]{:S(2)}) %collective-permute-start.8) | collective-permute-done | bytes 6176 | tf_op jit(solution)/shard_map/ppermute | solution.py:464
  27.9 2.0 %collective-permute-done.9 = f32[3,512]{1,0:T(4,128)S(1)} collective-permute-done((f32[3,512]{1,0:T(4,128)S(1)}, f32[3,512]{1,0:T(4,128)S(1)}, u32[]{:S(2)}, u32[]{:S(2)}) %collective-permute-start.9) | collective-permute-done | bytes 6176 | tf_op jit(solution)/shard_map/ppermute | solution.py:464
  30.0 0.7 %copy-done.1 = f32[2,3,512]{2,0,1:T(2,128)S(1)} copy-done((f32[2,3,512]{2,0,1:T(2,128)S(1)}, f32[2,3,512]{2,0,1:T(2,128)}, u32[]{:S(2)}) %copy-start.1) | copy-done | bytes 12312
  30.7 0.6 %copy.15 = f32[2,3,512]{2,0,1:T(2,128)} copy(f32[2,3,512]{2,1,0:T(4,128)S(1)} %bitcast.24) | data formatting | bytes 24576
  31.3 0.6 %copy.16 = f32[2,3,512]{2,0,1:T(2,128)} copy(f32[2,3,512]{2,1,0:T(4,128)S(1)} %get-tuple-element.20) | data formatting | bytes 24576
  (17 shorter events, 0.2 us)
Async XLA Ops:
  1.3 6.4 %collective-permute-start = (f32[3,2,512]{2,0,1:T(4,128)S(1)}, f32[3,2,512]{2,0,1:T(4,128)S(1)}, u32[]{:S(2)}, u32[]{:S(2)}) collective-permute-start(f32[3,2,512]{2,0,1:T(4,128)S(1)} %bitcast.19), channel_id=1, source_target_pairs={{0,4},{4,0},{8,12},{12,8},{1,5},{5,1},{9,13},{13,9},{2,6},{6,2},{1... | collective-permute-start | bytes 36872 | tf_op jit(solution)/shard_map/ppermute | solution.py:383
  4.4 5.8 %collective-permute-start.1 = (f32[3,2,512]{2,0,1:T(4,128)S(1)}, f32[3,2,512]{2,0,1:T(4,128)S(1)}, u32[]{:S(2)}, u32[]{:S(2)}) collective-permute-start(f32[3,2,512]{2,0,1:T(4,128)S(1)} %bitcast.20), channel_id=1, source_target_pairs={{0,12},{4,8},{8,4},{12,0},{1,13},{5,9},{9,5},{13,1},{2,14},{6,10},... | collective-permute-start | bytes 36872 | tf_op jit(solution)/shard_map/ppermute | solution.py:383
  6.8 4.6 %collective-permute-start.2 = (f32[3,2,512]{2,0,1:T(4,128)S(1)}, f32[3,2,512]{2,0,1:T(4,128)S(1)}, u32[]{:S(2)}, u32[]{:S(2)}) collective-permute-start(f32[3,2,512]{2,0,1:T(4,128)S(1)} %bitcast.21), channel_id=1, source_target_pairs={{0,8},{4,12},{8,0},{12,4},{1,9},{5,13},{9,1},{13,5},{2,10},{6,14},... | collective-permute-start | bytes 36872 | tf_op jit(solution)/shard_map/ppermute | solution.py:383
  7.0 0.7 %copy-start.2 = (s32[512]{0:T(512)S(1)}, s32[512]{0:T(512)}, u32[]{:S(2)}) copy-start(s32[512]{0:T(512)} %param.13) | copy-start | bytes 6148
  7.7 5.5 %copy-start = (s32[32,512]{1,0:T(8,128)S(1)}, s32[32,512]{1,0:T(8,128)}, u32[]{:S(2)}) copy-start(s32[32,512]{1,0:T(8,128)} %param.14) | copy-start | bytes 196612
  11.5 3.3 %collective-permute-start.3 = (f32[8,128]{1,0:T(8,128)S(1)}, f32[8,128]{1,0:T(8,128)S(1)}, u32[]{:S(2)}, u32[]{:S(2)}) collective-permute-start(f32[8,128]{1,0:T(8,128)S(1)} %get-tuple-element.31), channel_id=1, source_target_pairs={{0,3},{1,2},{2,1},{3,0},{4,7},{5,6},{6,5},{7,4},{8,11},{9,10},{10,... | collective-permute-start | bytes 12296 | tf_op jit(solution)/shard_map/ppermute | solution.py:336
  11.6 1.6 %copy-start.3 = (s32[512]{0:T(512)S(1)}, s32[512]{0:T(512)}, u32[]{:S(2)}) copy-start(s32[512]{0:T(512)} %param.15) | copy-start | bytes 6148
  11.6 3.2 %collective-permute-start.4 = (f32[8,128]{1,0:T(8,128)S(1)}, f32[8,128]{1,0:T(8,128)S(1)}, u32[]{:S(2)}, u32[]{:S(2)}) collective-permute-start(f32[8,128]{1,0:T(8,128)S(1)} %get-tuple-element.32), channel_id=1, source_target_pairs={{0,1},{1,0},{2,3},{3,2},{4,5},{5,4},{6,7},{7,6},{8,9},{9,8},{10,11... | collective-permute-start | bytes 12296 | tf_op jit(solution)/shard_map/ppermute | solution.py:335
  19.5 3.1 %collective-permute-start.5 = (f32[3,128]{1,0:T(4,128)S(1)}, f32[3,128]{1,0:T(4,128)S(1)}, u32[]{:S(2)}, u32[]{:S(2)}) collective-permute-start(f32[3,128]{1,0:T(4,128)S(1)} %get-tuple-element.29), channel_id=1, source_target_pairs={{0,3},{1,2},{2,1},{3,0},{4,7},{5,6},{6,5},{7,4},{8,11},{9,10},{10,... | collective-permute-start | bytes 4616 | tf_op jit(solution)/shard_map/ppermute | solution.py:336
  20.3 2.2 %collective-permute-start.6 = (f32[3,128]{1,0:T(4,128)S(1)}, f32[3,128]{1,0:T(4,128)S(1)}, u32[]{:S(2)}, u32[]{:S(2)}) collective-permute-start(f32[3,128]{1,0:T(4,128)S(1)} %get-tuple-element.30), channel_id=1, source_target_pairs={{0,1},{1,0},{2,3},{3,2},{4,5},{5,4},{6,7},{7,6},{8,9},{9,8},{10,11... | collective-permute-start | bytes 4616 | tf_op jit(solution)/shard_map/ppermute | solution.py:335
  22.6 4.5 %collective-permute-start.7 = (f32[3,512]{1,0:T(4,128)S(1)}, f32[3,512]{1,0:T(4,128)S(1)}, u32[]{:S(2)}, u32[]{:S(2)}) collective-permute-start(f32[3,512]{1,0:T(4,128)S(1)} %pad_maximum_fusion.3), channel_id=1, source_target_pairs={{0,4},{4,0},{8,12},{12,8},{1,5},{5,1},{9,13},{13,9},{2,6},{6,2},{1... | collective-permute-start | bytes 18440 | tf_op jit(solution)/shard_map/ppermute | solution.py:464
  23.4 4.6 %collective-permute-start.8 = (f32[3,512]{1,0:T(4,128)S(1)}, f32[3,512]{1,0:T(4,128)S(1)}, u32[]{:S(2)}, u32[]{:S(2)}) collective-permute-start(f32[3,512]{1,0:T(4,128)S(1)} %pad_maximum_fusion.3), channel_id=1, source_target_pairs={{0,8},{4,12},{8,0},{12,4},{1,9},{5,13},{9,1},{13,5},{2,10},{6,14},... | collective-permute-start | bytes 18440 | tf_op jit(solution)/shard_map/ppermute | solution.py:464
  24.5 5.4 %collective-permute-start.9 = (f32[3,512]{1,0:T(4,128)S(1)}, f32[3,512]{1,0:T(4,128)S(1)}, u32[]{:S(2)}, u32[]{:S(2)}) collective-permute-start(f32[3,512]{1,0:T(4,128)S(1)} %pad_maximum_fusion.3), channel_id=1, source_target_pairs={{0,12},{4,8},{8,4},{12,0},{1,13},{5,9},{9,5},{13,1},{2,14},{6,10},... | collective-permute-start | bytes 18440 | tf_op jit(solution)/shard_map/ppermute | solution.py:464
  30.0 0.7 %copy-start.1 = (f32[2,3,512]{2,0,1:T(2,128)S(1)}, f32[2,3,512]{2,0,1:T(2,128)}, u32[]{:S(2)}) copy-start(f32[2,3,512]{2,0,1:T(2,128)} %param.12) | copy-start | bytes 36868

commit v2 on v1

v2 whole, which is shorter than its diff:
```python
import functools

import jax
import jax.numpy as jnp
import numpy as np
from jax import lax
from jax.experimental import pallas as pl
from jax.experimental.pallas import tpu as pltpu
from jax.sharding import PartitionSpec as P

HALO = 128
NC = 4
SPECIES = 4
LANES = 128
DEAD = 4096
LOG2E = 1.4426950408889634

MASS_TABLE = (1.0, 0.25, 1.5, 2.0)
SPRING_RATE = 0.2
TIME_STEP = 0.5


def contraction_table(bead_count, kept_modes):
    rows = np.arange(kept_modes)[:, None] / kept_modes
    cols = np.arange(bead_count)[None, :] / bead_count
    angles = 2.0 * np.pi * (rows - cols)
    summed = np.ones_like(angles)
    for order in range(1, kept_modes // 2):
        summed = summed + 2.0 * np.cos(order * angles)
    summed = summed + np.cos(kept_modes // 2 * angles)
    return (summed / bead_count).astype(np.float32)


def per_species(species, values):
    picked = jnp.full(species.shape, values[0], jnp.float32)
    for kind in range(1, SPECIES):
        picked = jnp.where(species == kind, values[kind], picked)
    return picked


VMEM = pl.BlockSpec(memory_space=pltpu.VMEM)
SMEM = pl.BlockSpec(memory_space=pltpu.SMEM)


PARAMS = pltpu.CompilerParams(vmem_limit_bytes=16 * 1024 * 1024)


def cost(micros):
    return pl.CostEstimate(
        flops=0, transcendentals=0, bytes_accessed=int(micros * 3_000_000)
    )


def split2(value):
    high = value.astype(jnp.bfloat16)
    low = (value - high.astype(jnp.float32)).astype(jnp.bfloat16)
    return high, low


def dot(lhs, rhs):
    return lax.dot_general(
        lhs, rhs, (((1,), (0,)), ((), ())), preferred_element_type=jnp.float32
    )


def dot_nt(lhs, rhs):
    return lax.dot_general(
        lhs, rhs, (((1,), (1,)), ((), ())), preferred_element_type=jnp.float32
    )


def prepare_kernel(slab_atoms, block_start, *refs):
    held, outs = refs[:9], refs[9:19]
    copied, sems = refs[19:28], refs[28]
    copies = [
        pltpu.make_async_copy(src, dst, sems.at[i])
        for i, (src, dst) in enumerate(zip(held, copied, strict=True))
    ]
    for copy in copies:
        copy.start()
    slots, counts, species, w1, emb, w2, w3, rates, wout = copied
    code, kinds, l1, l2, l3, t1, t2, t3, rates_b, wout_b = outs
    for copy in copies[:3]:
        copy.wait()
    kinds[...] = species[...].astype(jnp.float32)

    slab = lax.axis_index("space")
    last = lax.axis_size("space") - 1
    lowest = jnp.where(slab == 0, HALO, 0)
    highest = jnp.where(slab == last, slab_atoms + HALO, slab_atoms + 2 * HALO)
    word = slots[...]
    slot_ids = lax.broadcasted_iota(jnp.int32, word.shape, 0)
    lane_ids = lax.broadcasted_iota(jnp.int32, word.shape, 1)
    live = (slot_ids < counts[...]) & (word >= lowest) & (word < highest)
    band = word - block_start() - jnp.bitwise_and(lane_ids, -LANES)
    code[...] = jnp.where(live, band, band + DEAD)

    for copy in copies[3:]:
        copy.wait()
    hid, chan = w1.shape
    high, low = split2(w1[...])
    l1[:, 0:chan] = high
    l1[:, 2 * chan : 3 * chan] = low
    l1[:, 3 * chan : 4 * chan] = high
    e = emb[...]
    eh = e.astype(jnp.bfloat16).astype(jnp.float32)
    el = (e - eh).astype(jnp.bfloat16).astype(jnp.float32)
    terms = jnp.concatenate([eh, el, e - eh - el, jnp.zeros_like(e)], axis=0)
    terms = jnp.concatenate(
        [terms, jnp.zeros((chan - 4 * SPECIES, hid), jnp.float32)], axis=0
    )
    l1[:, chan : 2 * chan] = terms.T.astype(jnp.bfloat16)
    t1[0:chan, :], t1[chan : 2 * chan, :] = split2(w1[...].T)
    for src, fwd, bwd in ((w2, l2, t2), (w3, l3, t3)):
        fwd[0:hid, :], fwd[hid : 2 * hid, :] = split2(src[...])
        bwd[0:hid, :], bwd[hid : 2 * hid, :] = split2(src[...].T)
    count = rates.shape[1]
    tall = jnp.concatenate(
        [rates[...], jnp.zeros((1, LANES - count), jnp.float32)], axis=1
    )
    rates_b[...] = jnp.broadcast_to(tall, (LANES, LANES)).T[0:count, :]
    wout_b[...] = jnp.broadcast_to(wout[...], (LANES, hid)).T


def prepare(slab_atoms, block_start, slots, counts, species, w1, emb, w2, w3, rates, wout):
    hid, chan = w1.shape
    shapes = [
        (hid, 4 * chan),
        (2 * hid, hid),
        (2 * hid, hid),
        (2 * chan, hid),
        (2 * hid, hid),
        (2 * hid, hid),
    ]
    out_shape = [
        pltpu.VMEM(slots.shape, jnp.int32),
        pltpu.VMEM(species.shape, jnp.float32),
    ]
    out_shape += [pltpu.VMEM(s, jnp.bfloat16) for s in shapes]
    out_shape += [
        pltpu.VMEM((rates.shape[0], LANES), jnp.float32),
        pltpu.VMEM((hid, LANES), jnp.float32),
    ]
    operands = (
        slots,
        counts[None, :],
        species,
        w1,
        emb.T,
        w2,
        w3,
        rates[None, :],
        wout[None, :],
    )
    code, kinds, *pairs, rates_b, wout_b = pl.pallas_call(
        functools.partial(prepare_kernel, slab_atoms, block_start),
        out_shape=out_shape,
        in_specs=[pl.BlockSpec(memory_space=pltpu.HBM)] * len(operands),
        out_specs=[VMEM] * len(out_shape),
        scratch_shapes=[pltpu.VMEM(x.shape, x.dtype) for x in operands]
        + [pltpu.SemaphoreType.DMA((len(operands),))],
        cost_estimate=cost(1.2),
        name="prepare",
    )(*operands)
    return code, kinds, pairs, rates_b, wout_b


def neighbours(places, word, g, off, kind, dist):
    src = [
        [
            jnp.broadcast_to(
                places[4 * (g + q) + c : 4 * (g + q) + c + 1, :], (8, LANES)
            )
            for q in range(3)
        ]
        for c in range(4)
    ]
    for o in range(word.shape[0] // 8):
        rows = slice(8 * o, 8 * o + 8)
        lane = jnp.bitwise_and(word[rows, :], LANES - 1)
        part = jnp.bitwise_and(word[rows, :], DEAD - 1)
        is0 = part < LANES
        is1 = part < 2 * LANES
        got = []
        for c in range(4):
            x0, x1, x2 = (
                jnp.take_along_axis(src[c][q], lane, axis=1) for q in range(3)
            )
            got.append(jnp.where(is0, x0, jnp.where(is1, x1, x2)))
        total = None
        for c in range(3):
            diff = got[c] - src[c][1]
            off[c, rows, :] = diff
            total = diff * diff if total is None else total + diff * diff
        dist[rows, :] = total
        kind[rows, :] = jnp.where(word[rows, :] >= DEAD, -1.0, got[3])


def describe(kind, dist, rates, rad, desc, cols):
    slots = kind.shape[0]
    rate_count = rates.shape[0]
    octets = rate_count // 8
    rate8 = [rates[8 * o : 8 * o + 8, :] * (-LOG2E) for o in range(octets)]
    acc = [[jnp.zeros((8, LANES), jnp.float32)] * octets for _ in range(SPECIES)]
    for n in range(slots):
        kind_n = jnp.broadcast_to(kind[n : n + 1, :], (8, LANES))
        dist_n = jnp.broadcast_to(dist[n : n + 1, :], (8, LANES))
        masks = [kind_n == float(s) for s in range(SPECIES)]
        for o in range(octets):
            radial = jnp.exp2(rate8[o] * dist_n)
            first = n * rate_count + 8 * o
            rad[first : first + 8, :] = radial
            for s in range(SPECIES):
                acc[s][o] = acc[s][o] + jnp.where(masks[s], radial, 0.0)
    for s in range(SPECIES):
        for o in range(octets):
            first = s * rate_count + 8 * o
            desc[first : first + 8, cols] = acc[s][o]


def network(desc, onehot, pairs, wout):
    l1, l2, l3, t1, t2, t3 = pairs
    chan, block = desc.shape
    dh, dl = split2(desc)
    pad = jnp.zeros((chan - onehot.shape[0], block), jnp.bfloat16)
    first = dot(l1[:, 0 : 2 * chan], jnp.concatenate([dh, onehot, pad], axis=0))
    first = first + dot(l1[:, 2 * chan : 4 * chan], jnp.concatenate([dh, dl], axis=0))

    def act(x):
        sig = 1.0 / (1.0 + jnp.exp2(x * (-LOG2E)))
        value = x * sig
        return value, sig + value * (1.0 - sig)

    def layer(pair, x):
        high, low = split2(x)
        both = dot(pair[...], high)
        rows = pair.shape[0] // 2
        return both[0:rows] + (both[rows:] + dot(pair[0:rows, :], low))

    h1, s1 = act(first)
    h2, s2 = act(layer(l2, h1))
    _, s3 = act(layer(l3, h2))
    g3 = jnp.concatenate([wout[...]] * (block // LANES), axis=1) * s3
    g2 = layer(t3, g3) * s2
    g1 = layer(t2, g2) * s1
    return layer(t1, g1)


def slot_slopes(grad, cols, kind, rates, rad, slope):
    slots = kind.shape[0]
    rate_count = rates.shape[0]
    octets = rate_count // 8
    grads = [
        [
            grad[s * rate_count + 8 * o : s * rate_count + 8 * o + 8, cols]
            * rates[8 * o : 8 * o + 8, :]
            for o in range(octets)
        ]
        for s in range(SPECIES)
    ]
    for n in range(slots):
        kind_n = jnp.broadcast_to(kind[n : n + 1, :], (8, LANES))
        masks = [kind_n == float(s) for s in range(SPECIES - 1)]
        total = None
        for o in range(octets):
            picked = grads[SPECIES - 1][o]
            for s in range(SPECIES - 1):
                picked = jnp.where(masks[s], grads[s][o], picked)
            first = n * rate_count + 8 * o
            term = picked * rad[first : first + 8, :]
            total = term if total is None else total + term
        slope[n : n + 1, :] = jnp.sum(total, axis=0, keepdims=True)


def pair_forces(word, slope, off, pair, rel):
    sums = [jnp.zeros((8, LANES), jnp.float32)] * 3
    for o in range(word.shape[0] // 8):
        rows = slice(8 * o, 8 * o + 8)
        part = jnp.bitwise_and(word[rows, :], DEAD - 1)
        rel[0, rows, :] = jnp.bitwise_and(part, 63)
        rel[1, rows, :] = jnp.right_shift(part, 6)
        twice = jnp.where(word[rows, :] >= DEAD, 0.0, 2.0 * slope[rows, :])
        for c in range(3):
            force = twice * off[c, rows, :]
            sums[c] = sums[c] + force
            high = force.astype(jnp.bfloat16).astype(jnp.float32)
            pair[2 * c, rows, :] = high
            pair[2 * c + 1, rows, :] = force - high
    return [jnp.sum(x, axis=0, keepdims=True) for x in sums]


def scatter(pair, rel, slots, out, block0, centre):
    low_ids = lax.broadcasted_iota(jnp.int32, (64, LANES), 0)
    high_ids = lax.broadcasted_iota(jnp.int32, (8, LANES), 0)
    total = jnp.zeros((48, 64), jnp.float32)
    for n in range(0, slots, 2):
        lefts, rights = [], []
        for k in (n, n + 1):
            low = rel[0, k : k + 1, :]
            high = jnp.broadcast_to(rel[1, k : k + 1, :], (8, LANES))
            rights.append(jnp.where(low_ids == low, 1.0, 0.0).astype(jnp.bfloat16))
            hit = high_ids == high
            picked = [
                jnp.where(hit, jnp.broadcast_to(pair[c, k : k + 1, :], (8, LANES)), 0.0)
                for c in range(6)
            ]
            lefts.append(jnp.concatenate(picked, axis=0).astype(jnp.bfloat16))
        total = total + dot_nt(
            jnp.concatenate(lefts, axis=1), jnp.concatenate(rights, axis=1)
        )
    for c in range(3):
        merged = total[16 * c : 16 * c + 8, :] + total[16 * c + 8 : 16 * c + 16, :]
        for q in range(3):
            row = 4 * (block0 + q) + c
            both = jnp.concatenate(
                [merged[2 * q : 2 * q + 1, :], merged[2 * q + 1 : 2 * q + 2, :]], axis=1
            )
            if q == 1:
                both = both - centre[c]
            out[row : row + 1, :] = out[row : row + 1, :] + both


def inner_kernel(own, code, rates, off, kind, rad, desc, dist):
    for i in range(kind.shape[0]):
        cols = slice(i * LANES, (i + 1) * LANES)
        word = code[:, (i + 1) * LANES : (i + 2) * LANES]
        neighbours(own, word, i, off.at[i], kind.at[i], dist)
        describe(kind.at[i], dist, rates, rad.at[i], desc, cols)


def inner_stage(own, code, rates, count):
    slots = code.shape[0]
    rate_count = rates.shape[0]
    out_shape = [
        pltpu.VMEM((count, 3, slots, LANES), jnp.float32),
        pltpu.VMEM((count, slots, LANES), jnp.float32),
        pltpu.VMEM((count, slots * rate_count, LANES), jnp.float32),
        pltpu.VMEM((SPECIES * rate_count, count * LANES), jnp.float32),
    ]
    return pl.pallas_call(
        inner_kernel,
        out_shape=out_shape,
        in_specs=[VMEM] * 3,
        out_specs=[VMEM] * 4,
        scratch_shapes=[pltpu.VMEM((slots, LANES), jnp.float32)],
        compiler_params=PARAMS,
        cost_estimate=cost(1.0),
        name="inner_descriptor",
    )(own, code, rates)


def outer_kernel(inner, *refs):
    ins = 10 + (1 if inner else 0)
    places, code, l1, l2, l3, t1, t2, t3, rates, wout = refs[:10]
    out = refs[ins]
    grad_inner = refs[ins + 1] if inner else None
    off, kind, dist, rad, desc, grad, pair, rel = refs[ins + (2 if inner else 1) :]
    slots, block = code.shape
    groups = block // LANES
    outer = sorted({0, groups - 1})
    order = outer + list(range(1, groups - 1))
    words = [code[:, g * LANES : (g + 1) * LANES] for g in outer]
    for i, g in enumerate(outer):
        cols = slice(i * LANES, (i + 1) * LANES)
        neighbours(places, words[i], g, off.at[i], kind.at[i], dist)
        describe(kind.at[i], dist, rates, rad.at[i], desc, cols)

    kinds = lax.broadcasted_iota(jnp.int32, (16, LANES), 0)
    kinds = jnp.where(
        kinds < 3 * SPECIES, jnp.bitwise_and(kinds, SPECIES - 1), -1
    ).astype(jnp.float32)
    onehot = jnp.concatenate(
        [
            jnp.where(kinds == places[4 * (g + 1) + 3 : 4 * (g + 1) + 4, :], 1.0, 0.0)
            for g in order
        ],
        axis=1,
    ).astype(jnp.bfloat16)
    whole = desc[...]
    if inner:
        whole = jnp.concatenate([whole, refs[10][...]], axis=1)
    slopes = network(whole, onehot, (l1, l2, l3, t1, t2, t3), wout)
    split = len(outer) * LANES
    grad[...] = slopes[:, :split]
    if inner:
        grad_inner[...] = slopes[:, split:]

    out[...] = jnp.zeros_like(out)
    for i, g in enumerate(outer):
        cols = slice(i * LANES, (i + 1) * LANES)
        slot_slopes(grad, cols, kind.at[i], rates, rad.at[i], dist)
        centre = pair_forces(words[i], dist, off.at[i], pair, rel)
        scatter(pair, rel, slots, out, g, centre)


def outer_stage(places, code, pairs, rates, wout, desc_inner):
    slots, block = code.shape
    rate_count = rates.shape[0]
    chan = SPECIES * rate_count
    groups = block // LANES
    count = len({0, groups - 1})
    inner = groups - count
    f32 = jnp.float32
    out_shape = [pltpu.VMEM((4 * (groups + 2), LANES), f32)]
    operands = [places, code, *pairs, rates, wout]
    if inner:
        out_shape.append(pltpu.VMEM((chan, inner * LANES), f32))
        operands.append(desc_inner)
    return pl.pallas_call(
        functools.partial(outer_kernel, inner),
        out_shape=out_shape,
        in_specs=[VMEM] * len(operands),
        out_specs=[VMEM] * len(out_shape),
        scratch_shapes=[
            pltpu.VMEM((count, 3, slots, LANES), f32),
            pltpu.VMEM((count, slots, LANES), f32),
            pltpu.VMEM((slots, LANES), f32),
            pltpu.VMEM((count, slots * rate_count, LANES), f32),
            pltpu.VMEM((chan, count * LANES), f32),
            pltpu.VMEM((chan, count * LANES), f32),
            pltpu.VMEM((6, slots, LANES), f32),
            pltpu.VMEM((2, slots, LANES), jnp.int32),
        ],
        compiler_params=PARAMS,
        cost_estimate=cost(3.0),
        name="outer_forces",
    )(*operands)


def inner_force_kernel(code, rates, off, kind, rad, grad, out, slope, pair, rel):
    slots = code.shape[0]
    out[...] = jnp.zeros_like(out)
    for i in range(kind.shape[0]):
        cols = slice(i * LANES, (i + 1) * LANES)
        word = code[:, (i + 1) * LANES : (i + 2) * LANES]
        slot_slopes(grad, cols, kind.at[i], rates, rad.at[i], slope)
        centre = pair_forces(word, slope, off.at[i], pair, rel)
        scatter(pair, rel, slots, out, i, centre)


def inner_forces(code, rates, off, kind, rad, grad):
    slots, block = code.shape
    return pl.pallas_call(
        inner_force_kernel,
        out_shape=pltpu.VMEM((block // LANES * 4, LANES), jnp.float32),
        in_specs=[VMEM] * 6,
        out_specs=VMEM,
        scratch_shapes=[
            pltpu.VMEM((slots, LANES), jnp.float32),
            pltpu.VMEM((6, slots, LANES), jnp.float32),
            pltpu.VMEM((2, slots, LANES), jnp.int32),
        ],
        compiler_params=PARAMS,
        cost_estimate=cost(1.2),
        name="inner_forces",
    )(code, rates, off, kind, rad, grad)


def bead_rows(array):
    beads, comps, atoms = array.shape
    split = array.reshape(beads, comps, atoms // LANES, LANES)
    return split.transpose(1, 2, 0, 3).reshape(-1, LANES)


def from_bead_rows(rows, shape):
    beads, comps, atoms = shape
    split = rows.reshape(comps, atoms // LANES, beads, LANES)
    return split.transpose(2, 0, 1, 3).reshape(shape)


def contract_kernel(table, beads, *refs):
    blocks, species, out = refs[:NC], refs[NC], refs[NC + 1]
    tiles = species.shape[0]
    for c in range(3):
        total = None
        for r in range(NC):
            for j in range(beads):
                rows = pl.ds(c * tiles * beads + j, tiles, stride=beads)
                term = float(table[r, j]) * blocks[r][rows, :]
                total = term if total is None else total + term
        out[pl.ds(c, tiles, stride=4), :] = total
    out[pl.ds(3, tiles, stride=4), :] = species[...]


def contract(table, beads, blocks, species):
    return pl.pallas_call(
        functools.partial(contract_kernel, table, beads),
        out_shape=pltpu.VMEM((4 * species.shape[0], LANES), jnp.float32),
        in_specs=[VMEM] * (NC + 1),
        out_specs=VMEM,
        compiler_params=PARAMS,
        cost_estimate=cost(0.2),
        name="contract",
    )(*blocks, species)


def masses_of(species):
    return per_species(species, MASS_TABLE)


def spring_kernel(beads, own, before, after, momenta, species, out):
    tiles = species.shape[0]
    pull = TIME_STEP * SPRING_RATE * masses_of(species[...])

    def row(ref, c, j):
        return ref[pl.ds(c * tiles * beads + j, tiles, stride=beads), :]

    for c in range(3):
        for j in range(beads):
            below = row(own, c, j - 1) if j else row(before, c, beads - 1)
            above = row(own, c, j + 1) if j + 1 < beads else row(after, c, 0)
            laplace = 2.0 * row(own, c, j) - below - above
            out[pl.ds(c * tiles * beads + j, tiles, stride=beads), :] = (
                row(momenta, c, j) - pull * laplace
            )


def spring_kick(beads, own, before, after, momenta, species):
    return pl.pallas_call(
        functools.partial(spring_kernel, beads),
        out_shape=pltpu.VMEM(own.shape, jnp.float32),
        in_specs=[VMEM] * 5,
        out_specs=VMEM,
        compiler_params=PARAMS,
        cost_estimate=cost(0.8),
        name="spring_kick",
    )(own, before, after, momenta, species)


def expand_kernel(table, beads, *refs):
    forces, kicked, species = refs[:NC], refs[NC], refs[NC + 1]
    momenta, displacement = refs[NC + 2 :]
    tiles = species.shape[0]
    scale = TIME_STEP * beads * NC / NC
    drift = per_species(species[...], [TIME_STEP / m for m in MASS_TABLE])
    for c in range(3):
        pulls = [force[pl.ds(c, tiles, stride=4), :] for force in forces]
        for j in range(beads):
            rows = pl.ds(c * tiles * beads + j, tiles, stride=beads)
            total = kicked[rows, :]
            for r in range(NC):
                total = total + (scale * float(table[-r % NC, j])) * pulls[r]
            momenta[rows, :] = total
            displacement[rows, :] = drift * total


def expand(table, beads, forces, kicked, species):
    shape = jax.ShapeDtypeStruct(kicked.shape, jnp.float32)
    return pl.pallas_call(
        functools.partial(expand_kernel, table, beads),
        out_shape=[shape, shape],
        in_specs=[VMEM] * (NC + 2),
        out_specs=[VMEM] * 2,
        compiler_params=PARAMS,
        cost_estimate=cost(0.8),
        name="expand",
    )(*forces, kicked, species)


def swap_with_adjacent(send_inner, send_outer):
    count = lax.axis_size("space")
    inner = [(i, i ^ 1) for i in range(count)]
    outer = [(i, (i + 1) % count if i % 2 else (i - 1) % count) for i in range(count)]
    return (
        lax.ppermute(send_inner, "space", inner),
        lax.ppermute(send_outer, "space", outer),
    )


def around(block):
    count = lax.axis_size("bead")
    blocks = [
        lax.ppermute(block, "bead", [(i, (i + r) % count) for i in range(count)])
        for r in range(count - 1, 0, -1)
    ]
    return [block] + blocks[::-1]


def on_device(
    positions,
    momenta,
    species,
    neighbour_index,
    neighbour_count,
    radial_rates,
    weight_input,
    embedding,
    weight_middle,
    weight_deeper,
    weight_output,
):
    bead_dev = positions.shape[0]
    atom_dev = positions.shape[2]
    bead_groups = lax.axis_size("bead")
    bead_count = bead_dev * bead_groups
    table = contraction_table(bead_count, NC)
    place = lax.axis_index("bead")
    slab = lax.axis_index("space")
    even = jnp.bitwise_and(slab, 1) == 0
    direct = bead_groups == NC
    block_size = atom_dev * NC // bead_groups
    tiles = atom_dev // LANES

    if direct:
        block_start = 0
        slots, counts = neighbour_index, neighbour_count
    else:
        block_start = (place // NC) * block_size
        slots = lax.dynamic_slice_in_dim(neighbour_index, block_start, block_size, 1)
        counts = lax.dynamic_slice_in_dim(neighbour_count, block_start, block_size, 0)
    code, kinds, pairs, rates, wout = prepare(
        atom_dev,
        lambda: 0 if direct else (lax.axis_index("bead") // NC) * block_size,
        slots,
        counts,
        species.reshape(tiles, LANES),
        weight_input,
        embedding,
        weight_middle,
        weight_deeper,
        radial_rates,
        weight_output,
    )

    if direct:
        blocks = around(bead_rows(positions))
        own = contract(table, bead_dev, blocks, kinds)
    else:
        replica = place % NC
        everything = lax.all_gather(positions, "bead", axis=0, tiled=True)
        weights = lax.dynamic_index_in_dim(jnp.asarray(table), replica, 0, keepdims=False)
        contracted = jnp.sum(weights[:, None, None] * everything, axis=0)
        stacked = contracted.reshape(3, tiles, LANES).transpose(1, 0, 2)
        own = jnp.concatenate([stacked, kinds[:, None]], axis=1).reshape(-1, LANES)

    bottom, top = own[:4], own[4 * tiles - 4 :]
    got_inner, got_outer = swap_with_adjacent(
        jnp.where(even, top, bottom), jnp.where(even, bottom, top)
    )
    inner_count = max(block_size // LANES - 2, 0)
    if inner_count:
        off, kind, rad, desc_inner = inner_stage(own, code, rates, inner_count)
    else:
        desc_inner = None
    window = jnp.concatenate(
        [
            jnp.where(even, got_outer, got_inner),
            own,
            jnp.where(even, got_inner, got_outer),
        ],
        axis=0,
    )
    if not direct:
        first = block_start // LANES * 4
        window = lax.dynamic_slice_in_dim(window, first, 4 * (block_size // LANES + 2), 0)
    force, *grad_inner = outer_stage(window, code, pairs, rates, wout, desc_inner)

    if not direct:
        partial = jnp.zeros((4 * (tiles + 2), LANES), jnp.float32)
        partial = lax.dynamic_update_slice_in_dim(partial, force, first, 0)
        chosen = (jnp.arange(NC, dtype=jnp.int32) == replica).astype(jnp.float32)
        force = lax.psum(chosen[:, None, None] * partial[None], "bead")

    lower, middle, upper = force[..., :4, :], force[..., 4:-4, :], force[..., -4:, :]
    got_inner, got_outer = swap_with_adjacent(
        jnp.where(even, upper, lower), jnp.where(even, lower, upper)
    )
    if inner_count:
        middle = middle + inner_forces(code, rates, off, kind, rad, *grad_inner)
    middle = jnp.concatenate(
        [
            middle[..., :4, :] + jnp.where(even, got_outer, got_inner),
            middle[..., 4:-4, :],
            middle[..., -4:, :] + jnp.where(even, got_inner, got_outer),
        ],
        axis=-2,
    )

    if direct:
        forces = around(middle)
        kicked = spring_kick(
            bead_dev, blocks[0], blocks[1], blocks[NC - 1], bead_rows(momenta), kinds
        )
        moved = expand(table, bead_dev, forces, kicked, kinds)
        return tuple(from_bead_rows(rows, positions.shape) for rows in moved)

    first = place * bead_dev
    below = lax.dynamic_index_in_dim(everything, (first - 1) % bead_count, 0)
    above = lax.dynamic_index_in_dim(everything, (first + bead_dev) % bead_count, 0)
    whole = middle.reshape(NC, tiles, 4, LANES).transpose(0, 2, 1, 3)[:, :3]
    whole = whole.reshape(NC, 3, atom_dev)
    columns = lax.dynamic_slice_in_dim(jnp.asarray(table), first, bead_dev, 1)
    expanded = jnp.sum(columns[:, :, None, None] * whole[:, None], axis=0)
    expanded = bead_count / NC * expanded
    masses = masses_of(species)
    cycle = jnp.concatenate([below, positions, above], axis=0)
    laplace = 2.0 * positions - cycle[:-2] - cycle[2:]
    spring = -SPRING_RATE * masses * laplace
    momenta_next = momenta + TIME_STEP * (spring + expanded)
    return (momenta_next, TIME_STEP * momenta_next / masses)


def solution(mesh):
    return jax.shard_map(
        on_device,
        mesh=mesh,
        in_specs=(
            P(("grp", "bead"), None, "space"),
            P(("grp", "bead"), None, "space"),
            P(("grp", "space")),
            P(None, ("grp", "space")),
            P(("grp", "space")),
            P(),
            P(),
            P(),
            P(),
            P(),
            P(),
        ),
        out_specs=(P(("grp", "bead"), None, "space"), P(("grp", "bead"), None, "space")),
        check_vma=False,
    )
```

time: 32.2 us -> 28.6 us (0.89)
  local copies, waits for them, and re-layouts: 3.3 us -> 0.01 us
  Pallas kernels: 6.13 us -> 7.21 us
  waiting for transfers between devices: 8.37 us -> 7.83 us
  starting transfers between devices: 13.2 us -> 12.7 us
    unnamed x11 -> x4, local copies, waits for them, and re-layouts: 3.3 us -> 0.01 us
    pallas_call x2 -> x7, Pallas kernels: 6.13 us -> 7.21 us  [the longest x1 3.45 us: outer_stage(): pl.pallas_call(functools.partial(outer_kernel, inner), out_shape=out_shap...]
    ppermute x2, starting transfers between devices: 2.16 us -> 3.18 us  [swap_with_adjacent(): lax.ppermute(send_inner, 'space', inner)]
    ppermute x2, starting transfers between devices: 0.95 us -> 0.14 us  [swap_with_adjacent(): lax.ppermute(send_outer, 'space', outer)]
    ppermute x6, starting transfers between devices: 10.1 us -> 9.33 us  [around(): lax.ppermute(block, 'bead', [(i, (i + r) % count) for i in range(count)])]
    ppermute x6, waiting for transfers between devices: 6.75 us -> 6.42 us  [around(): lax.ppermute(block, 'bead', [(i, (i + r) % count) for i in range(count)])]
  transfers between devices with their start and end apart: 10 -> 10, of which waited for: 5 -> 7; matrix products, arithmetic and copies ran while one was open for 0% -> 0% of each run, Pallas kernels for 5% -> 11%
where the time goes in v2:
time: 28.6 us; the launch traced here: 28.5 us
  starting transfers between devices  12.7 us (44%)
  waiting for transfers between devices  7.83 us (27%)
  Pallas kernels  7.21 us (25%)
  between operations  0.75 us (3%)
    ppermute x6, starting transfers between devices, around(): lax.ppermute(block, 'bead', [(i, (i + r) % count) for i in range(count)])  9.33 us
    ppermute x6, waiting for transfers between devices, around(): lax.ppermute(block, 'bead', [(i, (i + r) % count) for i in range(count)])  6.42 us
    pallas_call x1, Pallas kernels, outer_stage(): pl.pallas_call(functools.partial(outer_kernel, inner), out_shape=out_shap...  3.45 us
    ppermute x2, starting transfers between devices, swap_with_adjacent(): lax.ppermute(send_inner, 'space', inner)  3.18 us
    pallas_call x1, Pallas kernels, prepare(): pl.pallas_call(functools.partial(prepare_kernel, slab_atoms, block_start)...  1.73 us
    ppermute x2, waiting for transfers between devices, swap_with_adjacent(): lax.ppermute(send_outer, 'space', outer)  1.4 us
    pallas_call x1, Pallas kernels, inner_forces(): pl.pallas_call(inner_force_kernel, out_shape=pltpu.VMEM((block // LANES *...  0.84 us
    pallas_call x1, Pallas kernels, expand(): pl.pallas_call(functools.partial(expand_kernel, table, beads), out_shape=...  0.62 us
  transfers between devices with their start and end apart: 10, of which 7 were waited for; matrix products, arithmetic and copies ran while one was open for 0% of the time, Pallas kernels for 11%

profile of v2, /device:TPU:0, one launch (start us, length us, event | category | flops | bytes accessed | tf_op | source)
XLA Modules:
  0.0 28.5 jit_solution(837694359185514733)
XLA Ops:
  0.6 5.1 %collective-permute-start.2 = (f32[24,128]{1,0:T(8,128)}, f32[24,128]{1,0:T(8,128)S(1)}, u32[]{:S(2)}, u32[]{:S(2)}) collective-permute-start(f32[24,128]{1,0:T(8,128)} %bitcast.25), channel_id=1, source_target_pairs={{0,12},{4,0},{8,4},{12,8},{1,13},{5,1},{9,5},{13,9},{2,14},{6,2},{... | collective-permute-start | bytes 36872 | tf_op jit(solution)/shard_map/ppermute | solution.py:573
  5.7 0.0 collective-permute-start.1
  5.7 1.0 %collective-permute-start = (f32[24,128]{1,0:T(8,128)}, f32[24,128]{1,0:T(8,128)S(1)}, u32[]{:S(2)}, u32[]{:S(2)}) collective-permute-start(f32[24,128]{1,0:T(8,128)} %bitcast.27), channel_id=1, source_target_pairs={{0,4},{4,8},{8,12},{12,0},{1,5},{5,9},{9,13},{13,1},{2,6},{6,10},{... | collective-permute-start | bytes 36872 | tf_op jit(solution)/shard_map/ppermute | solution.py:573
  6.7 0.0 copy-start
  6.8 1.7 %prepare.1 = (s32[32,512]{1,0:T(8,128)S(1)}, f32[4,128]{1,0:T(4,128)S(1)}, bf16[256,512]{1,0:T(8,128)(2,1)S(1)}, bf16[512,256]{1,0:T(8,128)(2,1)S(1)}, bf16[512,...) custom-call(s32[32,512]{1,0:T(8,128)} %refs_0_.1, ...), custom_call_target="tpu_custom_call" | custom-call | bytes 3600000 | tf_op jit(solution)/shard_map/prepare/pallas_call | solution.py:155
  8.5 0.0 collective-permute-done.2.refs_3_.after
  8.5 2.0 %collective-permute-done.1.refs_2_ = f32[24,128]{1,0:T(8,128)S(1)} collective-permute-done((f32[24,128]{1,0:T(8,128)}, f32[24,128]{1,0:T(8,128)S(1)}, u32[]{:S(2)}, u32[]{:S(2)}) %collective-permute-start.1) | collective-permute-done | bytes 12320 | tf_op jit(solution)/shard_map/ppermute | solution.py:573
  10.5 0.9 %collective-permute-done.refs_1_.before = f32[24,128]{1,0:T(8,128)S(1)} collective-permute-done((f32[24,128]{1,0:T(8,128)}, f32[24,128]{1,0:T(8,128)S(1)}, u32[]{:S(2)}, u32[]{:S(2)}) %collective-permute-start) | collective-permute-done | bytes 12320 | tf_op jit(solution)/shard_map/ppermute | solution.py:573
  11.4 0.0 copy-done
  11.5 0.1 collective-permute-start.3
  11.6 1.6 %collective-permute-start.4 = (f32[4,128]{1,0:T(4,128)S(1)}, f32[4,128]{1,0:T(4,128)S(1)}, u32[]{:S(2)}, u32[]{:S(2)}) collective-permute-start(f32[4,128]{1,0:T(4,128)S(1)} %get-tuple-element.43), channel_id=1, source_target_pairs={{0,1},{1,0},{2,3},{3,2},{4,5},{5,4},{6,7},{7,6},{8,9},{9,8},{10,11... | collective-permute-start | bytes 6152 | tf_op jit(solution)/shard_map/ppermute | solution.py:565
  13.2 0.5 %inner_descriptor.1 = (f32[2,3,32,128]{3,2,1,0:T(8,128)S(1)}, f32[2,32,128]{2,1,0:T(8,128)S(1)}, f32[2,1024,128]{2,1,0:T(8,128)S(1)}, f32[128,256]{1,0:T(8,128)S(1)}) custom-call(f32[16,128]{1,0:T(8,128)S(1)} %contract.1.own, s32[32,512]{1,0:T(8,128)S(1)} %get-tuple-element.21.code.refs_1_, f32[32,128]{1,0:T(8,128)S(1)} %get-tuple-element.28.rates.refs_8_), custom_call_target="tpu_custom_call" | custom-call | bytes 3000000 | tf_op jit(solution)/shard_map/inner_descriptor/pallas_call | solution.py:340
  13.7 0.9 %collective-permute-done.3 = f32[4,128]{1,0:T(4,128)S(1)} collective-permute-done((f32[4,128]{1,0:T(4,128)S(1)}, f32[4,128]{1,0:T(4,128)S(1)}, u32[]{:S(2)}, u32[]{:S(2)}) %collective-permute-start.3) | collective-permute-done | bytes 2080 | tf_op jit(solution)/shard_map/ppermute | solution.py:566
  14.6 0.0 collective-permute-done.4
  14.6 3.5 %outer_forces.1 = (f32[24,128]{1,0:T(8,128)S(1)}, f32[128,256]{1,0:T(8,128)S(1)}) custom-call(f32[24,128]{1,0:T(8,128)S(1)} %pad_maximum_fusion.refs_0_, s32[32,512]{1,0:T(8,128)S(1)} %get-tuple-element.21.code.refs_1_, bf16[256,512]{1,0:T(8,128)(2,1)S(1)} %get-tuple-element.22.refs_2_, bf16[512,256]{1,0:T(8,128)(2,1)S(1)} %get-tuple-element.23.refs_3_, ...), custom_call_target="tpu_custom_call" | custom-call | bytes 9000000 | tf_op jit(solution)/shard_map/outer_forces/pallas_call | solution.py:409
  18.0 0.1 collective-permute-start.5
  18.1 1.6 %collective-permute-start.6 = (f32[4,128]{1,0:T(4,128)S(1)}, f32[4,128]{1,0:T(4,128)S(1)}, u32[]{:S(2)}, u32[]{:S(2)}) collective-permute-start(f32[4,128]{1,0:T(4,128)S(1)} %get-tuple-element.41), channel_id=1, source_target_pairs={{0,1},{1,0},{2,3},{3,2},{4,5},{5,4},{6,7},{7,6},{8,9},{9,8},{10,11... | collective-permute-start | bytes 6152 | tf_op jit(solution)/shard_map/ppermute | solution.py:565
  19.7 0.8 %inner_forces.1 = f32[16,128]{1,0:T(8,128)S(1)} custom-call(s32[32,512]{1,0:T(8,128)S(1)} %get-tuple-element.21.code.refs_1_, f32[32,128]{1,0:T(8,128)S(1)} %get-tuple-element.28.rates.refs_8_, f32[2,3,32,128]{3,2,1,0:T(8,128)S(1)} %get-tuple-element.32.off, f32[2,32,128]{2,1,0:T(8,128)S(1)} %get-tuple-element.33.kind, ...), custom_call_target="tpu_custom_call" | custom-call | bytes 3600000 | tf_op jit(solution)/shard_map/inner_forces/pallas_call | solution.py:443
  20.6 0.5 %collective-permute-done.5 = f32[4,128]{1,0:T(4,128)S(1)} collective-permute-done((f32[4,128]{1,0:T(4,128)S(1)}, f32[4,128]{1,0:T(4,128)S(1)}, u32[]{:S(2)}, u32[]{:S(2)}) %collective-permute-start.5) | collective-permute-done | bytes 2080 | tf_op jit(solution)/shard_map/ppermute | solution.py:566
  21.1 0.0 collective-permute-done.6
  21.1 0.0 copy-start.1
  21.2 0.7 %collective-permute-start.9 = (f32[16,128]{1,0:T(8,128)S(1)}, f32[16,128]{1,0:T(8,128)S(1)}, u32[]{:S(2)}, u32[]{:S(2)}) collective-permute-start(f32[16,128]{1,0:T(8,128)S(1)} %pad_maximum_fusion.1.refs_0_), channel_id=1, source_target_pairs={{0,12},{4,0},{8,4},{12,8},{1,13},{5,1},{9,5},{13,9},{2,14},{6,2},{... | collective-permute-start | bytes 24584 | tf_op jit(solution)/shard_map/ppermute | solution.py:573
  21.8 0.6 %collective-permute-start.8 = (f32[16,128]{1,0:T(8,128)S(1)}, f32[16,128]{1,0:T(8,128)S(1)}, u32[]{:S(2)}, u32[]{:S(2)}) collective-permute-start(f32[16,128]{1,0:T(8,128)S(1)} %pad_maximum_fusion.1.refs_0_), channel_id=1, source_target_pairs={{0,8},{4,12},{8,0},{12,4},{1,9},{5,13},{9,1},{13,5},{2,10},{6,14},... | collective-permute-start | bytes 24584 | tf_op jit(solution)/shard_map/ppermute | solution.py:573
  22.4 1.9 %collective-permute-start.7 = (f32[16,128]{1,0:T(8,128)S(1)}, f32[16,128]{1,0:T(8,128)S(1)}, u32[]{:S(2)}, u32[]{:S(2)}) collective-permute-start(f32[16,128]{1,0:T(8,128)S(1)} %pad_maximum_fusion.1.refs_0_), channel_id=1, source_target_pairs={{0,4},{4,8},{8,12},{12,0},{1,5},{5,9},{9,13},{13,1},{2,6},{6,10},{... | collective-permute-start | bytes 24584 | tf_op jit(solution)/shard_map/ppermute | solution.py:573
  24.4 0.0 copy-done.1
  24.4 0.5 %collective-permute-done.9.refs_3_ = f32[16,128]{1,0:T(8,128)S(1)} collective-permute-done((f32[16,128]{1,0:T(8,128)S(1)}, f32[16,128]{1,0:T(8,128)S(1)}, u32[]{:S(2)}, u32[]{:S(2)}) %collective-permute-start.9) | collective-permute-done | bytes 8224 | tf_op jit(solution)/shard_map/ppermute | solution.py:573
  24.9 1.5 %collective-permute-done.8.refs_2_ = f32[16,128]{1,0:T(8,128)S(1)} collective-permute-done((f32[16,128]{1,0:T(8,128)S(1)}, f32[16,128]{1,0:T(8,128)S(1)}, u32[]{:S(2)}, u32[]{:S(2)}) %collective-permute-start.8) | collective-permute-done | bytes 8224 | tf_op jit(solution)/shard_map/ppermute | solution.py:573
  26.4 1.5 %collective-permute-done.7.refs_1_ = f32[16,128]{1,0:T(8,128)S(1)} collective-permute-done((f32[16,128]{1,0:T(8,128)S(1)}, f32[16,128]{1,0:T(8,128)S(1)}, u32[]{:S(2)}, u32[]{:S(2)}) %collective-permute-start.7) | collective-permute-done | bytes 8224 | tf_op jit(solution)/shard_map/ppermute | solution.py:573
  27.9 0.6 %expand.1 = (f32[24,128]{1,0:T(8,128)}, f32[24,128]{1,0:T(8,128)}) custom-call(f32[16,128]{1,0:T(8,128)S(1)} %pad_maximum_fusion.1.refs_0_, f32[16,128]{1,0:T(8,128)S(1)} %collective-permute-done.7.refs_1_, f32[16,128]{1,0:T(8,128)S(1)} %collective-permute-done.8.refs_2_, f32[16,128]{1,0:T(8,128)S(1)} %collective-permute-done.9.refs_3_, ...), custom_call_target="tpu_custom_call" | custom-call | bytes 2400000 | tf_op jit(solution)/shard_map/expand/pallas_call | solution.py:549
  (10 shorter events, 0.1 us)
Async XLA Ops:
  0.6 7.9 %collective-permute-start.2 = (f32[24,128]{1,0:T(8,128)}, f32[24,128]{1,0:T(8,128)S(1)}, u32[]{:S(2)}, u32[]{:S(2)}) collective-permute-start(f32[24,128]{1,0:T(8,128)} %bitcast.25), channel_id=1, source_target_pairs={{0,12},{4,0},{8,4},{12,8},{1,13},{5,1},{9,5},{13,9},{2,14},{6,2},{... | collective-permute-start | bytes 36872 | tf_op jit(solution)/shard_map/ppermute | solution.py:573
  5.7 4.8 %collective-permute-start.1 = (f32[24,128]{1,0:T(8,128)}, f32[24,128]{1,0:T(8,128)S(1)}, u32[]{:S(2)}, u32[]{:S(2)}) collective-permute-start(f32[24,128]{1,0:T(8,128)} %bitcast.26), channel_id=1, source_target_pairs={{0,8},{4,12},{8,0},{12,4},{1,9},{5,13},{9,1},{13,5},{2,10},{6,14},... | collective-permute-start | bytes 36872 | tf_op jit(solution)/shard_map/ppermute | solution.py:573
  5.7 5.7 %collective-permute-start = (f32[24,128]{1,0:T(8,128)}, f32[24,128]{1,0:T(8,128)S(1)}, u32[]{:S(2)}, u32[]{:S(2)}) collective-permute-start(f32[24,128]{1,0:T(8,128)} %bitcast.27), channel_id=1, source_target_pairs={{0,4},{4,8},{8,12},{12,0},{1,5},{5,9},{9,13},{13,1},{2,6},{6,10},{... | collective-permute-start | bytes 36872 | tf_op jit(solution)/shard_map/ppermute | solution.py:573
  6.7 4.7 %copy-start = (f32[2,3,512]{2,0,1:T(2,128)S(1)}, f32[2,3,512]{2,0,1:T(2,128)}, u32[]{:S(2)}) copy-start(f32[2,3,512]{2,0,1:T(2,128)} %param.11) | copy-start | bytes 36868
  11.5 3.1 %collective-permute-start.3 = (f32[4,128]{1,0:T(4,128)S(1)}, f32[4,128]{1,0:T(4,128)S(1)}, u32[]{:S(2)}, u32[]{:S(2)}) collective-permute-start(f32[4,128]{1,0:T(4,128)S(1)} %get-tuple-element.42), channel_id=1, source_target_pairs={{0,3},{1,2},{2,1},{3,0},{4,7},{5,6},{6,5},{7,4},{8,11},{9,10},{10,... | collective-permute-start | bytes 6152 | tf_op jit(solution)/shard_map/ppermute | solution.py:566
  11.6 3.0 %collective-permute-start.4 = (f32[4,128]{1,0:T(4,128)S(1)}, f32[4,128]{1,0:T(4,128)S(1)}, u32[]{:S(2)}, u32[]{:S(2)}) collective-permute-start(f32[4,128]{1,0:T(4,128)S(1)} %get-tuple-element.43), channel_id=1, source_target_pairs={{0,1},{1,0},{2,3},{3,2},{4,5},{5,4},{6,7},{7,6},{8,9},{9,8},{10,11... | collective-permute-start | bytes 6152 | tf_op jit(solution)/shard_map/ppermute | solution.py:565
  18.0 3.1 %collective-permute-start.5 = (f32[4,128]{1,0:T(4,128)S(1)}, f32[4,128]{1,0:T(4,128)S(1)}, u32[]{:S(2)}, u32[]{:S(2)}) collective-permute-start(f32[4,128]{1,0:T(4,128)S(1)} %get-tuple-element.40), channel_id=1, source_target_pairs={{0,3},{1,2},{2,1},{3,0},{4,7},{5,6},{6,5},{7,4},{8,11},{9,10},{10,... | collective-permute-start | bytes 6152 | tf_op jit(solution)/shard_map/ppermute | solution.py:566
  18.1 3.0 %collective-permute-start.6 = (f32[4,128]{1,0:T(4,128)S(1)}, f32[4,128]{1,0:T(4,128)S(1)}, u32[]{:S(2)}, u32[]{:S(2)}) collective-permute-start(f32[4,128]{1,0:T(4,128)S(1)} %get-tuple-element.41), channel_id=1, source_target_pairs={{0,1},{1,0},{2,3},{3,2},{4,5},{5,4},{6,7},{7,6},{8,9},{9,8},{10,11... | collective-permute-start | bytes 6152 | tf_op jit(solution)/shard_map/ppermute | solution.py:565
  21.1 3.2 %copy-start.1 = (f32[2,3,512]{2,0,1:T(2,128)S(1)}, f32[2,3,512]{2,0,1:T(2,128)}, u32[]{:S(2)}) copy-start(f32[2,3,512]{2,0,1:T(2,128)} %param.12) | copy-start | bytes 36868
  21.2 3.7 %collective-permute-start.9 = (f32[16,128]{1,0:T(8,128)S(1)}, f32[16,128]{1,0:T(8,128)S(1)}, u32[]{:S(2)}, u32[]{:S(2)}) collective-permute-start(f32[16,128]{1,0:T(8,128)S(1)} %pad_maximum_fusion.1.refs_0_), channel_id=1, source_target_pairs={{0,12},{4,0},{8,4},{12,8},{1,13},{5,1},{9,5},{13,9},{2,14},{6,2},{... | collective-permute-start | bytes 24584 | tf_op jit(solution)/shard_map/ppermute | solution.py:573
  21.8 4.5 %collective-permute-start.8 = (f32[16,128]{1,0:T(8,128)S(1)}, f32[16,128]{1,0:T(8,128)S(1)}, u32[]{:S(2)}, u32[]{:S(2)}) collective-permute-start(f32[16,128]{1,0:T(8,128)S(1)} %pad_maximum_fusion.1.refs_0_), channel_id=1, source_target_pairs={{0,8},{4,12},{8,0},{12,4},{1,9},{5,13},{9,1},{13,5},{2,10},{6,14},... | collective-permute-start | bytes 24584 | tf_op jit(solution)/shard_map/ppermute | solution.py:573
  22.4 5.4 %collective-permute-start.7 = (f32[16,128]{1,0:T(8,128)S(1)}, f32[16,128]{1,0:T(8,128)S(1)}, u32[]{:S(2)}, u32[]{:S(2)}) collective-permute-start(f32[16,128]{1,0:T(8,128)S(1)} %pad_maximum_fusion.1.refs_0_), channel_id=1, source_target_pairs={{0,4},{4,8},{8,12},{12,0},{1,5},{5,9},{9,13},{13,1},{2,6},{6,10},{... | collective-permute-start | bytes 24584 | tf_op jit(solution)/shard_map/ppermute | solution.py:573

commit v3 on v2

--- a/solution.py
+++ b/solution.py
@@ -18,6 +18,9 @@
 MASS_TABLE = (1.0, 0.25, 1.5, 2.0)
 SPRING_RATE = 0.2
 TIME_STEP = 0.5
+
+GATHER = ("swap", (1, 3, 2))
+SPREAD = ("turn", (3, 2, 1))
 
 
 def contraction_table(bead_count, kept_modes):
@@ -51,6 +54,10 @@
     )
 
 
+def at_even(axis):
+    return jnp.bitwise_and(lax.axis_index(axis), 1) == 0
+
+
 def split2(value):
     high = value.astype(jnp.bfloat16)
     low = (value - high.astype(jnp.float32)).astype(jnp.bfloat16)
@@ -70,8 +77,8 @@
 
 
 def prepare_kernel(slab_atoms, block_start, *refs):
-    held, outs = refs[:9], refs[9:19]
-    copied, sems = refs[19:28], refs[28]
+    held, outs = refs[:9], refs[9:18]
+    copied, sems = refs[18:27], refs[27]
     copies = [
         pltpu.make_async_copy(src, dst, sems.at[i])
         for i, (src, dst) in enumerate(zip(held, copied, strict=True))
@@ -79,7 +86,7 @@
     for copy in copies:
         copy.start()
     slots, counts, species, w1, emb, w2, w3, rates, wout = copied
-    code, kinds, l1, l2, l3, t1, t2, t3, rates_b, wout_b = outs
+    code, kinds, t1, t2, t3, l2, l3, rates_b, wout_b = outs
     for copy in copies[:3]:
         copy.wait()
     kinds[...] = species[...].astype(jnp.float32)
@@ -97,38 +104,32 @@
 
     for copy in copies[3:]:
         copy.wait()
-    hid, chan = w1.shape
-    high, low = split2(w1[...])
-    l1[:, 0:chan] = high
-    l1[:, 2 * chan : 3 * chan] = low
-    l1[:, 3 * chan : 4 * chan] = high
+    chan = w1.shape[1]
+    t1[0:chan, :], t1[chan : 2 * chan, :] = split2(w1[...].T)
     e = emb[...]
     eh = e.astype(jnp.bfloat16).astype(jnp.float32)
     el = (e - eh).astype(jnp.bfloat16).astype(jnp.float32)
-    terms = jnp.concatenate([eh, el, e - eh - el, jnp.zeros_like(e)], axis=0)
-    terms = jnp.concatenate(
-        [terms, jnp.zeros((chan - 4 * SPECIES, hid), jnp.float32)], axis=0
-    )
-    l1[:, chan : 2 * chan] = terms.T.astype(jnp.bfloat16)
-    t1[0:chan, :], t1[chan : 2 * chan, :] = split2(w1[...].T)
-    for src, fwd, bwd in ((w2, l2, t2), (w3, l3, t3)):
-        fwd[0:hid, :], fwd[hid : 2 * hid, :] = split2(src[...])
-        bwd[0:hid, :], bwd[hid : 2 * hid, :] = split2(src[...].T)
+    rest = jnp.zeros((chan - 3 * SPECIES, e.shape[1]), jnp.float32)
+    terms = jnp.concatenate([eh, el, e - eh - el, rest], axis=0)
+    t1[2 * chan : 3 * chan, :] = terms.astype(jnp.bfloat16)
+    for src, fwd, bwd in ((w2, t2, l2), (w3, t3, l3)):
+        hid = src.shape[0]
+        fwd[0:hid, :], fwd[hid : 2 * hid, :] = split2(src[...].T)
+        bwd[0:hid, :], bwd[hid : 2 * hid, :] = split2(src[...])
     count = rates.shape[1]
     tall = jnp.concatenate(
         [rates[...], jnp.zeros((1, LANES - count), jnp.float32)], axis=1
     )
     rates_b[...] = jnp.broadcast_to(tall, (LANES, LANES)).T[0:count, :]
-    wout_b[...] = jnp.broadcast_to(wout[...], (LANES, hid)).T
+    wout_b[...] = jnp.broadcast_to(wout[...], wout_b.shape)
 
 
 def prepare(slab_atoms, block_start, slots, counts, species, w1, emb, w2, w3, rates, wout):
     hid, chan = w1.shape
     shapes = [
-        (hid, 4 * chan),
+        (3 * chan, hid),
         (2 * hid, hid),
         (2 * hid, hid),
-        (2 * chan, hid),
         (2 * hid, hid),
         (2 * hid, hid),
     ]
@@ -139,7 +140,7 @@
     out_shape += [pltpu.VMEM(s, jnp.bfloat16) for s in shapes]
     out_shape += [
         pltpu.VMEM((rates.shape[0], LANES), jnp.float32),
-        pltpu.VMEM((hid, LANES), jnp.float32),
+        pltpu.VMEM((8, hid), jnp.float32),
     ]
     operands = (
         slots,
@@ -196,7 +197,7 @@
         kind[rows, :] = jnp.where(word[rows, :] >= DEAD, -1.0, got[3])
 
 
-def describe(kind, dist, rates, rad, desc, cols):
+def describe(kind, dist, rates, rad, desc):
     slots = kind.shape[0]
     rate_count = rates.shape[0]
     octets = rate_count // 8
@@ -215,44 +216,58 @@
     for s in range(SPECIES):
         for o in range(octets):
             first = s * rate_count + 8 * o
-            desc[first : first + 8, cols] = acc[s][o]
-
-
-def network(desc, onehot, pairs, wout):
-    l1, l2, l3, t1, t2, t3 = pairs
-    chan, block = desc.shape
-    dh, dl = split2(desc)
-    pad = jnp.zeros((chan - onehot.shape[0], block), jnp.bfloat16)
-    first = dot(l1[:, 0 : 2 * chan], jnp.concatenate([dh, onehot, pad], axis=0))
-    first = first + dot(l1[:, 2 * chan : 4 * chan], jnp.concatenate([dh, dl], axis=0))
+            desc[first : first + 8, :] = acc[s][o]
+
+
+def left_factor(desc, centre):
+    chan = desc.shape[0]
+    high, low = split2(desc[...].T)
+    ids = lax.broadcasted_iota(jnp.int32, (chan, LANES), 0)
+    ids = jnp.where(ids < 3 * SPECIES, jnp.bitwise_and(ids, SPECIES - 1), -1)
+    onehot = jnp.where(ids.astype(jnp.float32) == centre, 1.0, 0.0)
+    onehot = onehot.T.astype(jnp.bfloat16)
+    return jnp.concatenate([high, high, low, onehot], axis=1)
+
+
+def network(lefts, pairs, wout):
+    t1, t2, t3, l2, l3 = pairs
+    chan = t1.shape[0] // 3
+    first = jnp.concatenate([t1[0 : 2 * chan, :], t1[0:chan, :], t1[2 * chan :, :]], axis=0)
 
     def act(x):
-        sig = 1.0 / (1.0 + jnp.exp2(x * (-LOG2E)))
+        sig = 0.5 + 0.5 * jnp.tanh(0.5 * x)
         value = x * sig
         return value, sig + value * (1.0 - sig)
 
-    def layer(pair, x):
+    def layer(x, pair):
         high, low = split2(x)
-        both = dot(pair[...], high)
         rows = pair.shape[0] // 2
-        return both[0:rows] + (both[rows:] + dot(pair[0:rows, :], low))
-
-    h1, s1 = act(first)
-    h2, s2 = act(layer(l2, h1))
-    _, s3 = act(layer(l3, h2))
-    g3 = jnp.concatenate([wout[...]] * (block // LANES), axis=1) * s3
-    g2 = layer(t3, g3) * s2
-    g1 = layer(t2, g2) * s1
-    return layer(t1, g1)
-
-
-def slot_slopes(grad, cols, kind, rates, rad, slope):
+        right = jnp.concatenate([pair[...], pair[0:rows, :]], axis=0)
+        return dot(jnp.concatenate([high, high, low], axis=1), right)
+
+    one = [act(dot(left, first)) for left in lefts]
+    two = [act(layer(h, t2)) for h, _ in one]
+    three = [act(layer(h, t3))[1] for h, _ in two]
+    back = [wout[0:1, :] * s for s in three]
+    back = [layer(g, l3) * s for g, (_, s) in zip(back, two)]
+    back = [layer(g, l2) * s for g, (_, s) in zip(back, one)]
+    last = jnp.concatenate(
+        [t1[0:chan, :], t1[chan : 2 * chan, :], t1[0:chan, :]], axis=1
+    )
+    grads = []
+    for g in back:
+        high, low = split2(g)
+        grads.append(dot_nt(last, jnp.concatenate([high, high, low], axis=1)))
+    return grads
+
+
+def slot_slopes(grad, kind, rates, rad, slope):
     slots = kind.shape[0]
     rate_count = rates.shape[0]
     octets = rate_count // 8
     grads = [
         [
-            grad[s * rate_count + 8 * o : s * rate_count + 8 * o + 8, cols]
+            grad[s * rate_count + 8 * o : s * rate_count + 8 * o + 8, :]
             * rates[8 * o : 8 * o + 8, :]
             for o in range(octets)
         ]
@@ -320,104 +335,121 @@
             out[row : row + 1, :] = out[row : row + 1, :] + both
 
 
-def inner_kernel(own, code, rates, off, kind, rad, desc, dist):
+def inner_kernel(own, code, rates, off, kind, rad, left, dist, desc):
     for i in range(kind.shape[0]):
-        cols = slice(i * LANES, (i + 1) * LANES)
         word = code[:, (i + 1) * LANES : (i + 2) * LANES]
         neighbours(own, word, i, off.at[i], kind.at[i], dist)
-        describe(kind.at[i], dist, rates, rad.at[i], desc, cols)
+        describe(kind.at[i], dist, rates, rad.at[i], desc)
+        row = 4 * (i + 1) + 3
+        left[i] = left_factor(desc, own[row : row + 1, :])
 
 
 def inner_stage(own, code, rates, count):
     slots = code.shape[0]
     rate_count = rates.shape[0]
+    chan = SPECIES * rate_count
     out_shape = [
         pltpu.VMEM((count, 3, slots, LANES), jnp.float32),
         pltpu.VMEM((count, slots, LANES), jnp.float32),
         pltpu.VMEM((count, slots * rate_count, LANES), jnp.float32),
-        pltpu.VMEM((SPECIES * rate_count, count * LANES), jnp.float32),
+        pltpu.VMEM((count, LANES, 4 * chan), jnp.bfloat16),
     ]
     return pl.pallas_call(
         inner_kernel,
         out_shape=out_shape,
         in_specs=[VMEM] * 3,
         out_specs=[VMEM] * 4,
-        scratch_shapes=[pltpu.VMEM((slots, LANES), jnp.float32)],
+        scratch_shapes=[
+            pltpu.VMEM((slots, LANES), jnp.float32),
+            pltpu.VMEM((chan, LANES), jnp.float32),
+        ],
         compiler_params=PARAMS,
         cost_estimate=cost(1.0),
         name="inner_descriptor",
     )(own, code, rates)
 
 
-def outer_kernel(inner, *refs):
-    ins = 10 + (1 if inner else 0)
-    places, code, l1, l2, l3, t1, t2, t3, rates, wout = refs[:10]
-    out = refs[ins]
-    grad_inner = refs[ins + 1] if inner else None
-    off, kind, dist, rad, desc, grad, pair, rel = refs[ins + (2 if inner else 1) :]
+def outer_kernel(direct, inner, *refs):
+    refs = list(refs)
+
+    def take(count):
+        taken = refs[:count]
+        del refs[:count]
+        return taken
+
+    blocks = take(3 if direct else 1)
+    code, *pairs, rates, wout = take(9 - 1)
+    left_inner = take(1)[0] if inner else None
+    out = take(1)[0]
+    to_inner, to_outer = take(2) if direct else (None, None)
+    grad_inner = take(1)[0] if inner else None
+    places, off, kind, dist, rad, desc, grad, pair, rel = refs
     slots, block = code.shape
     groups = block // LANES
     outer = sorted({0, groups - 1})
-    order = outer + list(range(1, groups - 1))
+    if direct:
+        own, got_outer, got_inner = blocks
+        even = at_even("space")
+        places[0:4, :] = jnp.where(even, got_outer[...], got_inner[...])
+        places[4 : 4 * groups + 4, :] = own[...]
+        places[4 * groups + 4 :, :] = jnp.where(even, got_inner[...], got_outer[...])
+    else:
+        places[...] = blocks[0][...]
     words = [code[:, g * LANES : (g + 1) * LANES] for g in outer]
+    lefts = []
     for i, g in enumerate(outer):
-        cols = slice(i * LANES, (i + 1) * LANES)
         neighbours(places, words[i], g, off.at[i], kind.at[i], dist)
-        describe(kind.at[i], dist, rates, rad.at[i], desc, cols)
-
-    kinds = lax.broadcasted_iota(jnp.int32, (16, LANES), 0)
-    kinds = jnp.where(
-        kinds < 3 * SPECIES, jnp.bitwise_and(kinds, SPECIES - 1), -1
-    ).astype(jnp.float32)
-    onehot = jnp.concatenate(
-        [
-            jnp.where(kinds == places[4 * (g + 1) + 3 : 4 * (g + 1) + 4, :], 1.0, 0.0)
-            for g in order
-        ],
-        axis=1,
-    ).astype(jnp.bfloat16)
-    whole = desc[...]
+        describe(kind.at[i], dist, rates, rad.at[i], desc.at[i])
+        row = 4 * (g + 1) + 3
+        lefts.append(left_factor(desc.at[i], places[row : row + 1, :]))
     if inner:
-        whole = jnp.concatenate([whole, refs[10][...]], axis=1)
-    slopes = network(whole, onehot, (l1, l2, l3, t1, t2, t3), wout)
-    split = len(outer) * LANES
-    grad[...] = slopes[:, :split]
-    if inner:
-        grad_inner[...] = slopes[:, split:]
+        lefts += [left_inner[i] for i in range(left_inner.shape[0])]
+    slopes = network(lefts, pairs, wout)
+    for i in range(len(outer)):
+        grad[i] = slopes[i]
+    for i in range(len(outer), len(slopes)):
+        grad_inner[i - len(outer)] = slopes[i]
 
     out[...] = jnp.zeros_like(out)
     for i, g in enumerate(outer):
-        cols = slice(i * LANES, (i + 1) * LANES)
-        slot_slopes(grad, cols, kind.at[i], rates, rad.at[i], dist)
+        slot_slopes(grad.at[i], kind.at[i], rates, rad.at[i], dist)
         centre = pair_forces(words[i], dist, off.at[i], pair, rel)
         scatter(pair, rel, slots, out, g, centre)
-
-
-def outer_stage(places, code, pairs, rates, wout, desc_inner):
+    if direct:
+        lower, upper = out[0:4, :], out[4 * groups + 4 :, :]
+        to_inner[...] = jnp.where(even, upper, lower)
+        to_outer[...] = jnp.where(even, lower, upper)
+
+
+def outer_stage(blocks, code, pairs, rates, wout, left_inner):
     slots, block = code.shape
     rate_count = rates.shape[0]
     chan = SPECIES * rate_count
     groups = block // LANES
     count = len({0, groups - 1})
     inner = groups - count
+    direct = len(blocks) > 1
     f32 = jnp.float32
     out_shape = [pltpu.VMEM((4 * (groups + 2), LANES), f32)]
-    operands = [places, code, *pairs, rates, wout]
+    operands = [*blocks, code, *pairs, rates, wout]
+    if direct:
+        out_shape += [pltpu.VMEM((4, LANES), f32)] * 2
     if inner:
-        out_shape.append(pltpu.VMEM((chan, inner * LANES), f32))
-        operands.append(desc_inner)
+        out_shape.append(pltpu.VMEM((inner, chan, LANES), f32))
+        operands.append(left_inner)
     return pl.pallas_call(
-        functools.partial(outer_kernel, inner),
+        functools.partial(outer_kernel, direct, inner),
         out_shape=out_shape,
         in_specs=[VMEM] * len(operands),
         out_specs=[VMEM] * len(out_shape),
         scratch_shapes=[
+            pltpu.VMEM((4 * (groups + 2), LANES), f32),
             pltpu.VMEM((count, 3, slots, LANES), f32),
             pltpu.VMEM((count, slots, LANES), f32),
             pltpu.VMEM((slots, LANES), f32),
             pltpu.VMEM((count, slots * rate_count, LANES), f32),
-            pltpu.VMEM((chan, count * LANES), f32),
-            pltpu.VMEM((chan, count * LANES), f32),
+            pltpu.VMEM((count, chan, LANES), f32),
+            pltpu.VMEM((count, chan, LANES), f32),
             pltpu.VMEM((6, slots, LANES), f32),
             pltpu.VMEM((2, slots, LANES), jnp.int32),
         ],
@@ -431,9 +463,8 @@
     slots = code.shape[0]
     out[...] = jnp.zeros_like(out)
     for i in range(kind.shape[0]):
-        cols = slice(i * LANES, (i + 1) * LANES)
         word = code[:, (i + 1) * LANES : (i + 2) * LANES]
-        slot_slopes(grad, cols, kind.at[i], rates, rad.at[i], slope)
+        slot_slopes(grad.at[i], kind.at[i], rates, rad.at[i], slope)
         centre = pair_forces(word, slope, off.at[i], pair, rel)
         scatter(pair, rel, slots, out, i, centre)
 
@@ -456,6 +487,30 @@
     )(code, rates, off, kind, rad, grad)
 
 
+def combine_kernel(inner, force, *refs):
+    *rest, got_outer, got_inner, out = refs
+    total = force[4 : force.shape[0] - 4, :]
+    if inner:
+        total = total + rest[0][...]
+    even = at_even("space")
+    out[...] = total
+    out[0:4, :] += jnp.where(even, got_outer[...], got_inner[...])
+    out[out.shape[0] - 4 :, :] += jnp.where(even, got_inner[...], got_outer[...])
+
+
+def combine(force, inner, got_inner, got_outer):
+    operands = [force, *inner, got_outer, got_inner]
+    return pl.pallas_call(
+        functools.partial(combine_kernel, len(inner)),
+        out_shape=pltpu.VMEM((force.shape[0] - 8, LANES), jnp.float32),
+        in_specs=[VMEM] * len(operands),
+        out_specs=VMEM,
+        compiler_params=PARAMS,
+        cost_estimate=cost(0.1),
+        name="combine",
+    )(*operands)
+
+
 def bead_rows(array):
     beads, comps, atoms = array.shape
     split = array.reshape(beads, comps, atoms // LANES, LANES)
@@ -469,29 +524,38 @@
 
 
 def contract_kernel(table, beads, *refs):
-    blocks, species, out = refs[:NC], refs[NC], refs[NC + 1]
+    blocks, species = arranged(GATHER, refs), refs[NC]
+    out, to_inner, to_outer = refs[NC + 1 :]
     tiles = species.shape[0]
     for c in range(3):
         total = None
         for r in range(NC):
             for j in range(beads):
                 rows = pl.ds(c * tiles * beads + j, tiles, stride=beads)
-                term = float(table[r, j]) * blocks[r][rows, :]
+                term = share(GATHER, r, table[r, j], table[-r % NC, j]) * blocks[r][rows, :]
                 total = term if total is None else total + term
         out[pl.ds(c, tiles, stride=4), :] = total
     out[pl.ds(3, tiles, stride=4), :] = species[...]
+    bottom, top = out[0:4, :], out[4 * tiles - 4 :, :]
+    even = at_even("space")
+    to_inner[...] = jnp.where(even, top, bottom)
+    to_outer[...] = jnp.where(even, bottom, top)
 
 
 def contract(table, beads, blocks, species):
     return pl.pallas_call(
         functools.partial(contract_kernel, table, beads),
-        out_shape=pltpu.VMEM((4 * species.shape[0], LANES), jnp.float32),
+        out_shape=[
+            pltpu.VMEM((4 * species.shape[0], LANES), jnp.float32),
+            pltpu.VMEM((4, LANES), jnp.float32),
+            pltpu.VMEM((4, LANES), jnp.float32),
+        ],
         in_specs=[VMEM] * (NC + 1),
-        out_specs=VMEM,
+        out_specs=[VMEM] * 3,
         compiler_params=PARAMS,
         cost_estimate=cost(0.2),
         name="contract",
-    )(*blocks, species)
+    )(blocks[0], *(blocks[r] for r in GATHER[1]), species)
 
 
 def masses_of(species):
@@ -505,10 +569,15 @@
     def row(ref, c, j):
         return ref[pl.ds(c * tiles * beads + j, tiles, stride=beads), :]
 
+    def side(c, j, ref, other):
+        if GATHER[0] == "turn":
+            return row(ref, c, j)
+        return jnp.where(at_even("bead"), row(other, c, j), row(ref, c, j))
+
     for c in range(3):
         for j in range(beads):
-            below = row(own, c, j - 1) if j else row(before, c, beads - 1)
-            above = row(own, c, j + 1) if j + 1 < beads else row(after, c, 0)
+            below = row(own, c, j - 1) if j else side(c, beads - 1, before, after)
+            above = row(own, c, j + 1) if j + 1 < beads else side(c, 0, after, before)
             laplace = 2.0 * row(own, c, j) - below - above
             out[pl.ds(c * tiles * beads + j, tiles, stride=beads), :] = (
                 row(momenta, c, j) - pull * laplace
@@ -528,7 +597,7 @@
 
 
 def expand_kernel(table, beads, *refs):
-    forces, kicked, species = refs[:NC], refs[NC], refs[NC + 1]
+    forces, kicked, species = arranged(SPREAD, refs), refs[NC], refs[NC + 1]
     momenta, displacement = refs[NC + 2 :]
     tiles = species.shape[0]
     scale = TIME_STEP * beads * NC / NC
@@ -539,7 +608,8 @@
             rows = pl.ds(c * tiles * beads + j, tiles, stride=beads)
             total = kicked[rows, :]
             for r in range(NC):
-                total = total + (scale * float(table[-r % NC, j])) * pulls[r]
+                weight = share(SPREAD, r, scale * table[-r % NC, j], scale * table[r, j])
+                total = total + weight * pulls[r]
             momenta[rows, :] = total
             displacement[rows, :] = drift * total
 
@@ -554,7 +624,7 @@
         compiler_params=PARAMS,
         cost_estimate=cost(0.8),
         name="expand",
-    )(*forces, kicked, species)
+    )(forces[0], *(forces[r] for r in SPREAD[1]), kicked, species)
 
 
 def swap_with_adjacent(send_inner, send_outer):
@@ -567,13 +637,27 @@
     )
 
 
-def around(block):
+def arranged(plan, refs):
+    return [refs[0]] + [refs[1 + plan[1].index(r)] for r in range(1, NC)]
+
+
+def share(plan, distance, behind, ahead):
+    behind, ahead = float(behind), float(ahead)
+    if plan[0] == "turn" or behind == ahead or distance == 0:
+        return behind
+    return jnp.where(at_even("bead"), ahead, behind)
+
+
+def around(plan, block):
     count = lax.axis_size("bead")
-    blocks = [
-        lax.ppermute(block, "bead", [(i, (i + r) % count) for i in range(count)])
-        for r in range(count - 1, 0, -1)
-    ]
-    return [block] + blocks[::-1]
+    blocks = [block]
+    for r in range(1, count):
+        if plan[0] == "turn":
+            pairs = [(i, (i + r) % count) for i in range(count)]
+        else:
+            pairs = [(i, i ^ r) for i in range(count)]
+        blocks.append(lax.ppermute(block, "bead", pairs))
+    return blocks
 
 
 def on_device(
@@ -595,8 +679,6 @@
     bead_count = bead_dev * bead_groups
     table = contraction_table(bead_count, NC)
     place = lax.axis_index("bead")
-    slab = lax.axis_index("space")
-    even = jnp.bitwise_and(slab, 1) == 0
     direct = bead_groups == NC
     block_size = atom_dev * NC // bead_groups
     tiles = atom_dev // LANES
@@ -623,8 +705,8 @@
     )
 
     if direct:
-        blocks = around(bead_rows(positions))
-        own = contract(table, bead_dev, blocks, kinds)
+        blocks = around(GATHER, bead_rows(positions))
+        own, to_inner, to_outer = contract(table, bead_dev, blocks, kinds)
     else:
         replica = place % NC
         everything = lax.all_gather(positions, "bead", axis=0, tiled=True)
@@ -633,15 +715,30 @@
         stacked = contracted.reshape(3, tiles, LANES).transpose(1, 0, 2)
         own = jnp.concatenate([stacked, kinds[:, None]], axis=1).reshape(-1, LANES)
 
+    if direct:
+        got = swap_with_adjacent(to_inner, to_outer)
+        inner_count = max(tiles - 2, 0)
+        left_inner, others = None, []
+        if inner_count:
+            off, kind, rad, left_inner = inner_stage(own, code, rates, inner_count)
+        force, to_inner, to_outer, *grad_inner = outer_stage(
+            [own, *got[::-1]], code, pairs, rates, wout, left_inner
+        )
+        got = swap_with_adjacent(to_inner, to_outer)
+        if inner_count:
+            others = [inner_forces(code, rates, off, kind, rad, *grad_inner)]
+        forces = around(SPREAD, combine(force, others, *got))
+        kicked = spring_kick(
+            bead_dev, blocks[0], blocks[1], blocks[NC - 1], bead_rows(momenta), kinds
+        )
+        moved = expand(table, bead_dev, forces, kicked, kinds)
+        return tuple(from_bead_rows(rows, positions.shape) for rows in moved)
+
+    even = at_even("space")
     bottom, top = own[:4], own[4 * tiles - 4 :]
     got_inner, got_outer = swap_with_adjacent(
         jnp.where(even, top, bottom), jnp.where(even, bottom, top)
     )
-    inner_count = max(block_size // LANES - 2, 0)
-    if inner_count:
-        off, kind, rad, desc_inner = inner_stage(own, code, rates, inner_count)
-    else:
-        desc_inner = None
     window = jnp.concatenate(
         [
             jnp.where(even, got_outer, got_inner),
@@ -650,39 +747,35 @@
         ],
         axis=0,
     )
-    if not direct:
-        first = block_start // LANES * 4
-        window = lax.dynamic_slice_in_dim(window, first, 4 * (block_size // LANES + 2), 0)
-    force, *grad_inner = outer_stage(window, code, pairs, rates, wout, desc_inner)
-
-    if not direct:
-        partial = jnp.zeros((4 * (tiles + 2), LANES), jnp.float32)
-        partial = lax.dynamic_update_slice_in_dim(partial, force, first, 0)
-        chosen = (jnp.arange(NC, dtype=jnp.int32) == replica).astype(jnp.float32)
-        force = lax.psum(chosen[:, None, None] * partial[None], "bead")
-
-    lower, middle, upper = force[..., :4, :], force[..., 4:-4, :], force[..., -4:, :]
+    first = block_start // LANES * 4
+    groups = block_size // LANES
+    window = lax.dynamic_slice_in_dim(window, first, 4 * (groups + 2), 0)
+    left_inner = None
+    if groups > 2:
+        inside = window[4 : 4 * groups + 4]
+        off, kind, rad, left_inner = inner_stage(inside, code, rates, groups - 2)
+    force, *grad_inner = outer_stage([window], code, pairs, rates, wout, left_inner)
+    if groups > 2:
+        force = force.at[4 : 4 * groups + 4].add(
+            inner_forces(code, rates, off, kind, rad, *grad_inner)
+        )
+    partial = jnp.zeros((4 * (tiles + 2), LANES), jnp.float32)
+    partial = lax.dynamic_update_slice_in_dim(partial, force, first, 0)
+    chosen = (jnp.arange(NC, dtype=jnp.int32) == replica).astype(jnp.float32)
+    force = lax.psum(chosen[:, None, None] * partial[None], "bead")
+
+    lower, middle, upper = force[:, :4], force[:, 4:-4], force[:, -4:]
     got_inner, got_outer = swap_with_adjacent(
         jnp.where(even, upper, lower), jnp.where(even, lower, upper)
     )
-    if inner_count:
-        middle = middle + inner_forces(code, rates, off, kind, rad, *grad_inner)
     middle = jnp.concatenate(
         [
-            middle[..., :4, :] + jnp.where(even, got_outer, got_inner),
-            middle[..., 4:-4, :],
-            middle[..., -4:, :] + jnp.where(even, got_inner, got_outer),
+            middle[:, :4] + jnp.where(even, got_outer, got_inner),
+            middle[:, 4:-4],
+            middle[:, -4:] + jnp.where(even, got_inner, got_outer),
         ],
-        axis=-2,
-    )
-
-    if direct:
-        forces = around(middle)
-        kicked = spring_kick(
-            bead_dev, blocks[0], blocks[1], blocks[NC - 1], bead_rows(momenta), kinds
-        )
-        moved = expand(table, bead_dev, forces, kicked, kinds)
-        return tuple(from_bead_rows(rows, positions.shape) for rows in moved)
+        axis=1,
+    )
 
     first = place * bead_dev
     below = lax.dynamic_index_in_dim(everything, (first - 1) % bead_count, 0)

time: 28.6 us -> 26.8 us (0.937)
  waiting for transfers between devices: 7.83 us -> 5.77 us
  starting transfers between devices: 12.7 us -> 13.2 us
    ppermute x6, waiting for transfers between devices: 6.42 us -> 4.57 us  [around(): blocks.append(lax.ppermute(block, 'bead', pairs))]
    ppermute x6, starting transfers between devices: 9.33 us -> 9.88 us  [around(): blocks.append(lax.ppermute(block, 'bead', pairs))]
    pallas_call x1 -> x2, Pallas kernels: 3.45 us -> 3.08 us  [the longest x1 3.07 us: outer_stage(): pl.pallas_call(functools.partial(outer_kernel, direct, inner), out_shape=...]
  transfers between devices with their start and end apart: 10 -> 10, of which waited for: 7 -> 5; matrix products, arithmetic and copies ran while one was open for 0% -> 0% of each run, Pallas kernels for 11% -> 12%
where the time goes in v3:
time: 26.8 us; the launch traced here: 26.6 us
  starting transfers between devices  13.2 us (49%)
  Pallas kernels  6.95 us (26%)
  waiting for transfers between devices  5.77 us (22%)
  between operations  0.7 us (3%)
    ppermute x6, starting transfers between devices, around(): blocks.append(lax.ppermute(block, 'bead', pairs))  9.88 us
    ppermute x6, waiting for transfers between devices, around(): blocks.append(lax.ppermute(block, 'bead', pairs))  4.57 us
    ppermute x2, starting transfers between devices, swap_with_adjacent(): lax.ppermute(send_inner, 'space', inner)  3.18 us
    pallas_call x1, Pallas kernels, outer_stage(): pl.pallas_call(functools.partial(outer_kernel, direct, inner), out_shape=...  3.07 us
    pallas_call x1, Pallas kernels, prepare(): pl.pallas_call(functools.partial(prepare_kernel, slab_atoms, block_start)...  1.59 us
    ppermute x2, waiting for transfers between devices, swap_with_adjacent(): lax.ppermute(send_outer, 'space', outer)  1.19 us
    pallas_call x1, Pallas kernels, inner_forces(): pl.pallas_call(inner_force_kernel, out_shape=pltpu.VMEM((block // LANES *...  0.84 us
    pallas_call x1, Pallas kernels, inner_stage(): pl.pallas_call(inner_kernel, out_shape=out_shape, in_specs=[VMEM] * 3, ou...  0.76 us
  transfers between devices with their start and end apart: 10, of which 5 were waited for; matrix products, arithmetic and copies ran while one was open for 0% of the time, Pallas kernels for 12%

profile of v3, /device:TPU:0, one launch (start us, length us, event | category | flops | bytes accessed | tf_op | source)
XLA Modules:
  0.0 26.6 jit_solution(12948757241711749157)
XLA Ops:
  0.6 4.1 %collective-permute-start.2 = (f32[24,128]{1,0:T(8,128)}, f32[24,128]{1,0:T(8,128)S(1)}, u32[]{:S(2)}, u32[]{:S(2)}) collective-permute-start(f32[24,128]{1,0:T(8,128)} %bitcast.25), channel_id=1, source_target_pairs={{0,8},{4,12},{8,0},{12,4},{1,9},{5,13},{9,1},{13,5},{2,10},{6,14},... | collective-permute-start | bytes 36872 | tf_op jit(solution)/shard_map/ppermute | solution.py:659
  4.7 1.3 %collective-permute-start.1 = (f32[24,128]{1,0:T(8,128)}, f32[24,128]{1,0:T(8,128)S(1)}, u32[]{:S(2)}, u32[]{:S(2)}) collective-permute-start(f32[24,128]{1,0:T(8,128)} %bitcast.26), channel_id=1, source_target_pairs={{0,12},{4,8},{8,4},{12,0},{1,13},{5,9},{9,5},{13,1},{2,14},{6,10},... | collective-permute-start | bytes 36872 | tf_op jit(solution)/shard_map/ppermute | solution.py:659
  6.1 0.2 collective-permute-start
  6.3 0.0 copy-start
  6.3 1.6 %prepare.1 = (s32[32,512]{1,0:T(8,128)S(1)}, f32[4,128]{1,0:T(4,128)S(1)}, bf16[384,256]{1,0:T(8,128)(2,1)S(1)}, bf16[512,256]{1,0:T(8,128)(2,1)S(1)}, bf16[512,...) custom-call(s32[32,512]{1,0:T(8,128)} %refs_0_.1, ...), custom_call_target="tpu_custom_call" | custom-call | bytes 3600000 | tf_op jit(solution)/shard_map/prepare/pallas_call | solution.py:156
  7.9 0.0 collective-permute-done.2.refs_3_
  7.9 2.5 %collective-permute-done.1.refs_2_.after = f32[24,128]{1,0:T(8,128)S(1)} collective-permute-done((f32[24,128]{1,0:T(8,128)}, f32[24,128]{1,0:T(8,128)S(1)}, u32[]{:S(2)}, u32[]{:S(2)}) %collective-permute-start.1) | collective-permute-done | bytes 12320 | tf_op jit(solution)/shard_map/ppermute | solution.py:659
  10.4 0.0 collective-permute-done.refs_1_.before
  10.4 0.0 copy-done
  10.5 0.1 collective-permute-start.3
  10.6 1.6 %collective-permute-start.4 = (f32[4,128]{1,0:T(4,128)S(1)}, f32[4,128]{1,0:T(4,128)S(1)}, u32[]{:S(2)}, u32[]{:S(2)}) collective-permute-start(f32[4,128]{1,0:T(4,128)S(1)} %get-tuple-element.27), channel_id=1, source_target_pairs={{0,1},{1,0},{2,3},{3,2},{4,5},{5,4},{6,7},{7,6},{8,9},{9,8},{10,11... | collective-permute-start | bytes 6152 | tf_op jit(solution)/shard_map/ppermute | solution.py:635
  12.1 0.8 %inner_descriptor.1 = (f32[2,3,32,128]{3,2,1,0:T(8,128)S(1)}, f32[2,32,128]{2,1,0:T(8,128)S(1)}, f32[2,1024,128]{2,1,0:T(8,128)S(1)}, bf16[2,128,512]{2,1,0:T(8,128)(2,1)S(1)}) custom-call(f32[16,128]{1,0:T(8,128)S(1)} %get-tuple-element.25.own.refs_0_, s32[32,512]{1,0:T(8,128)S(1)} %get-tuple-element.28.code.refs_3_, ...), custom_call_target="tpu_custom_call" | custom-call | bytes 3000000 | tf_op jit(solution)/shard_map/inner_descriptor/pallas_call | solution.py:357
  12.9 0.6 %collective-permute-done.3.refs_1_ = f32[4,128]{1,0:T(4,128)S(1)} collective-permute-done((f32[4,128]{1,0:T(4,128)S(1)}, f32[4,128]{1,0:T(4,128)S(1)}, u32[]{:S(2)}, u32[]{:S(2)}) %collective-permute-start.3) | collective-permute-done | bytes 2080 | tf_op jit(solution)/shard_map/ppermute | solution.py:636
  13.5 0.0 collective-permute-done.4.refs_2_
  13.6 3.1 %outer_forces.1 = (f32[24,128]{1,0:T(8,128)S(1)}, f32[4,128]{1,0:T(4,128)S(1)}, f32[4,128]{1,0:T(4,128)S(1)}, f32[2,128,128]{2,1,0:T(8,128)S(1)}) custom-call(f32[16,128]{1,0:T(8,128)S(1)} %get-tuple-element.25.own.refs_0_, f32[4,128]{1,0:T(4,128)S(1)} %collective-permute-done.3.refs_1_, f32[4,128]{1,0:T(4,128)S(1)} %collective-permute-done.4.refs_2_, ...), custom_call_target="tpu_custom_call" | custom-call | bytes 9000000 | tf_op jit(solution)/shard_map/outer_forces/pallas_call | solution.py:440
  16.6 0.1 collective-permute-start.5
  16.7 1.6 %collective-permute-start.6 = (f32[4,128]{1,0:T(4,128)S(1)}, f32[4,128]{1,0:T(4,128)S(1)}, u32[]{:S(2)}, u32[]{:S(2)}) collective-permute-start(f32[4,128]{1,0:T(4,128)S(1)} %get-tuple-element.43), channel_id=1, source_target_pairs={{0,1},{1,0},{2,3},{3,2},{4,5},{5,4},{6,7},{7,6},{8,9},{9,8},{10,11... | collective-permute-start | bytes 6152 | tf_op jit(solution)/shard_map/ppermute | solution.py:635
  18.3 0.8 %inner_forces.1.refs_0_ = f32[16,128]{1,0:T(8,128)S(1)} custom-call(s32[32,512]{1,0:T(8,128)S(1)} %get-tuple-element.28.code.refs_3_, f32[32,128]{1,0:T(8,128)S(1)} %get-tuple-element.34.rates.refs_9_, f32[2,3,32,128]{3,2,1,0:T(8,128)S(1)} %get-tuple-element.38.off, f32[2,32,128]{2,1,0:T(8,128)S(1)} %get-tuple-element.39.kind, ...), custom_call_target="tpu_custom_call" | custom-call | bytes 3600000 | tf_op jit(solution)/shard_map/inner_forces/pallas_call | solution.py:474
  19.1 0.6 %collective-permute-done.5.refs_1_ = f32[4,128]{1,0:T(4,128)S(1)} collective-permute-done((f32[4,128]{1,0:T(4,128)S(1)}, f32[4,128]{1,0:T(4,128)S(1)}, u32[]{:S(2)}, u32[]{:S(2)}) %collective-permute-start.5) | collective-permute-done | bytes 2080 | tf_op jit(solution)/shard_map/ppermute | solution.py:636
  19.7 0.0 collective-permute-done.6.refs_2_
  19.7 0.0 copy-start.1
  19.7 0.1 collective-permute-start.9
  19.8 2.6 %collective-permute-start.8 = (f32[16,128]{1,0:T(8,128)S(1)}, f32[16,128]{1,0:T(8,128)S(1)}, u32[]{:S(2)}, u32[]{:S(2)}) collective-permute-start(f32[16,128]{1,0:T(8,128)S(1)} %combine.1.refs_0_), channel_id=1, source_target_pairs={{0,8},{4,12},{8,0},{12,4},{1,9},{5,13},{9,1},{13,5},{2,10},{6,14},... | collective-permute-start | bytes 24584 | tf_op jit(solution)/shard_map/ppermute | solution.py:659
  22.4 1.6 %collective-permute-start.7 = (f32[16,128]{1,0:T(8,128)S(1)}, f32[16,128]{1,0:T(8,128)S(1)}, u32[]{:S(2)}, u32[]{:S(2)}) collective-permute-start(f32[16,128]{1,0:T(8,128)S(1)} %combine.1.refs_0_), channel_id=1, source_target_pairs={{0,12},{4,0},{8,4},{12,8},{1,13},{5,1},{9,5},{13,9},{2,14},{6,2},{... | collective-permute-start | bytes 24584 | tf_op jit(solution)/shard_map/ppermute | solution.py:659
  23.9 0.0 copy-done.1
  24.0 1.3 %collective-permute-done.9.refs_3_ = f32[16,128]{1,0:T(8,128)S(1)} collective-permute-done((f32[16,128]{1,0:T(8,128)S(1)}, f32[16,128]{1,0:T(8,128)S(1)}, u32[]{:S(2)}, u32[]{:S(2)}) %collective-permute-start.9) | collective-permute-done | bytes 8224 | tf_op jit(solution)/shard_map/ppermute | solution.py:659
  25.2 0.0 collective-permute-done.8.refs_2_
  25.2 0.8 %collective-permute-done.7.refs_1_ = f32[16,128]{1,0:T(8,128)S(1)} collective-permute-done((f32[16,128]{1,0:T(8,128)S(1)}, f32[16,128]{1,0:T(8,128)S(1)}, u32[]{:S(2)}, u32[]{:S(2)}) %collective-permute-start.7) | collective-permute-done | bytes 8224 | tf_op jit(solution)/shard_map/ppermute | solution.py:659
  26.0 0.6 %expand.1 = (f32[24,128]{1,0:T(8,128)}, f32[24,128]{1,0:T(8,128)}) custom-call(f32[16,128]{1,0:T(8,128)S(1)} %combine.1.refs_0_, f32[16,128]{1,0:T(8,128)S(1)} %collective-permute-done.7.refs_1_, f32[16,128]{1,0:T(8,128)S(1)} %collective-permute-done.8.refs_2_, f32[16,128]{1,0:T(8,128)S(1)} %collective-permute-done.9.refs_3_, ...), custom_call_target="tpu_custom_call" | custom-call | bytes 2400000 | tf_op jit(solution)/shard_map/expand/pallas_call | solution.py:619
  (3 shorter events, 0.1 us)
Async XLA Ops:
  0.6 7.3 %collective-permute-start.2 = (f32[24,128]{1,0:T(8,128)}, f32[24,128]{1,0:T(8,128)S(1)}, u32[]{:S(2)}, u32[]{:S(2)}) collective-permute-start(f32[24,128]{1,0:T(8,128)} %bitcast.25), channel_id=1, source_target_pairs={{0,8},{4,12},{8,0},{12,4},{1,9},{5,13},{9,1},{13,5},{2,10},{6,14},... | collective-permute-start | bytes 36872 | tf_op jit(solution)/shard_map/ppermute | solution.py:659
  4.7 5.7 %collective-permute-start.1 = (f32[24,128]{1,0:T(8,128)}, f32[24,128]{1,0:T(8,128)S(1)}, u32[]{:S(2)}, u32[]{:S(2)}) collective-permute-start(f32[24,128]{1,0:T(8,128)} %bitcast.26), channel_id=1, source_target_pairs={{0,12},{4,8},{8,4},{12,0},{1,13},{5,9},{9,5},{13,1},{2,14},{6,10},... | collective-permute-start | bytes 36872 | tf_op jit(solution)/shard_map/ppermute | solution.py:659
  6.1 4.4 %collective-permute-start = (f32[24,128]{1,0:T(8,128)}, f32[24,128]{1,0:T(8,128)S(1)}, u32[]{:S(2)}, u32[]{:S(2)}) collective-permute-start(f32[24,128]{1,0:T(8,128)} %bitcast.27), channel_id=1, source_target_pairs={{0,4},{4,0},{8,12},{12,8},{1,5},{5,1},{9,13},{13,9},{2,6},{6,2},{1... | collective-permute-start | bytes 36872 | tf_op jit(solution)/shard_map/ppermute | solution.py:659
  6.3 4.1 %copy-start = (f32[2,3,512]{2,0,1:T(2,128)S(1)}, f32[2,3,512]{2,0,1:T(2,128)}, u32[]{:S(2)}) copy-start(f32[2,3,512]{2,0,1:T(2,128)} %param.11) | copy-start | bytes 36868
  10.5 3.1 %collective-permute-start.3 = (f32[4,128]{1,0:T(4,128)S(1)}, f32[4,128]{1,0:T(4,128)S(1)}, u32[]{:S(2)}, u32[]{:S(2)}) collective-permute-start(f32[4,128]{1,0:T(4,128)S(1)} %get-tuple-element.26), channel_id=1, source_target_pairs={{0,3},{1,2},{2,1},{3,0},{4,7},{5,6},{6,5},{7,4},{8,11},{9,10},{10,... | collective-permute-start | bytes 6152 | tf_op jit(solution)/shard_map/ppermute | solution.py:636
  10.6 3.0 %collective-permute-start.4 = (f32[4,128]{1,0:T(4,128)S(1)}, f32[4,128]{1,0:T(4,128)S(1)}, u32[]{:S(2)}, u32[]{:S(2)}) collective-permute-start(f32[4,128]{1,0:T(4,128)S(1)} %get-tuple-element.27), channel_id=1, source_target_pairs={{0,1},{1,0},{2,3},{3,2},{4,5},{5,4},{6,7},{7,6},{8,9},{9,8},{10,11... | collective-permute-start | bytes 6152 | tf_op jit(solution)/shard_map/ppermute | solution.py:635
  16.6 3.1 %collective-permute-start.5 = (f32[4,128]{1,0:T(4,128)S(1)}, f32[4,128]{1,0:T(4,128)S(1)}, u32[]{:S(2)}, u32[]{:S(2)}) collective-permute-start(f32[4,128]{1,0:T(4,128)S(1)} %get-tuple-element.42), channel_id=1, source_target_pairs={{0,3},{1,2},{2,1},{3,0},{4,7},{5,6},{6,5},{7,4},{8,11},{9,10},{10,... | collective-permute-start | bytes 6152 | tf_op jit(solution)/shard_map/ppermute | solution.py:636
  16.7 3.0 %collective-permute-start.6 = (f32[4,128]{1,0:T(4,128)S(1)}, f32[4,128]{1,0:T(4,128)S(1)}, u32[]{:S(2)}, u32[]{:S(2)}) collective-permute-start(f32[4,128]{1,0:T(4,128)S(1)} %get-tuple-element.43), channel_id=1, source_target_pairs={{0,1},{1,0},{2,3},{3,2},{4,5},{5,4},{6,7},{7,6},{8,9},{9,8},{10,11... | collective-permute-start | bytes 6152 | tf_op jit(solution)/shard_map/ppermute | solution.py:635
  19.7 4.2 %copy-start.1 = (f32[2,3,512]{2,0,1:T(2,128)S(1)}, f32[2,3,512]{2,0,1:T(2,128)}, u32[]{:S(2)}) copy-start(f32[2,3,512]{2,0,1:T(2,128)} %param.12) | copy-start | bytes 36868
  19.7 5.5 %collective-permute-start.9 = (f32[16,128]{1,0:T(8,128)S(1)}, f32[16,128]{1,0:T(8,128)S(1)}, u32[]{:S(2)}, u32[]{:S(2)}) collective-permute-start(f32[16,128]{1,0:T(8,128)S(1)} %combine.1.refs_0_), channel_id=1, source_target_pairs={{0,4},{4,8},{8,12},{12,0},{1,5},{5,9},{9,13},{13,1},{2,6},{6,10},{... | collective-permute-start | bytes 24584 | tf_op jit(solution)/shard_map/ppermute | solution.py:659
  19.8 5.4 %collective-permute-start.8 = (f32[16,128]{1,0:T(8,128)S(1)}, f32[16,128]{1,0:T(8,128)S(1)}, u32[]{:S(2)}, u32[]{:S(2)}) collective-permute-start(f32[16,128]{1,0:T(8,128)S(1)} %combine.1.refs_0_), channel_id=1, source_target_pairs={{0,8},{4,12},{8,0},{12,4},{1,9},{5,13},{9,1},{13,5},{2,10},{6,14},... | collective-permute-start | bytes 24584 | tf_op jit(solution)/shard_map/ppermute | solution.py:659
  22.4 3.7 %collective-permute-start.7 = (f32[16,128]{1,0:T(8,128)S(1)}, f32[16,128]{1,0:T(8,128)S(1)}, u32[]{:S(2)}, u32[]{:S(2)}) collective-permute-start(f32[16,128]{1,0:T(8,128)S(1)} %combine.1.refs_0_), channel_id=1, source_target_pairs={{0,12},{4,0},{8,4},{12,8},{1,13},{5,1},{9,5},{13,9},{2,14},{6,2},{... | collective-permute-start | bytes 24584 | tf_op jit(solution)/shard_map/ppermute | solution.py:659

commit v4 on v3

--- a/solution.py
+++ b/solution.py
@@ -330,7 +330,7 @@
             both = jnp.concatenate(
                 [merged[2 * q : 2 * q + 1, :], merged[2 * q + 1 : 2 * q + 2, :]], axis=1
             )
-            if q == 1:
+            if q == 1 and centre is not None:
                 both = both - centre[c]
             out[row : row + 1, :] = out[row : row + 1, :] + both
 
@@ -381,44 +381,57 @@
     code, *pairs, rates, wout = take(9 - 1)
     left_inner = take(1)[0] if inner else None
     out = take(1)[0]
-    to_inner, to_outer = take(2) if direct else (None, None)
+    to_inner = take(1)[0] if direct else None
     grad_inner = take(1)[0] if inner else None
-    places, off, kind, dist, rad, desc, grad, pair, rel = refs
+    places, off, kind, dist, rad, desc, grad, pair, rel, beyond, pulled = refs
     slots, block = code.shape
     groups = block // LANES
-    outer = sorted({0, groups - 1})
+    stages = [
+        (code[:, g * LANES : (g + 1) * LANES], places, g, out)
+        for g in sorted({0, groups - 1})
+    ]
     if direct:
         own, got_outer, got_inner = blocks
         even = at_even("space")
-        places[0:4, :] = jnp.where(even, got_outer[...], got_inner[...])
+        first, last = own[0:4, :], own[4 * groups - 4 :, :]
+        near, far = got_outer[0:4, :], got_outer[4:8, :]
+        places[0:4, :] = jnp.where(even, far, got_inner[...])
         places[4 : 4 * groups + 4, :] = own[...]
-        places[4 * groups + 4 :, :] = jnp.where(even, got_inner[...], got_outer[...])
+        places[4 * groups + 4 :, :] = jnp.where(even, got_inner[...], near)
+        beyond[0:4, :] = jnp.where(even, near, last)
+        beyond[4:8, :] = jnp.where(even, far, near)
+        beyond[8:12, :] = jnp.where(even, first, far)
+        slab = lax.axis_index("space")
+        at_end = (slab == 0) | (slab == lax.axis_size("space") - 1)
+        word = got_outer[8:, :].astype(jnp.int32)
+        word = jnp.where(at_end, jnp.bitwise_or(word, DEAD), word)
+        stages.append((word, beyond, 0, pulled))
+        pulled[...] = jnp.zeros_like(pulled)
     else:
         places[...] = blocks[0][...]
-    words = [code[:, g * LANES : (g + 1) * LANES] for g in outer]
     lefts = []
-    for i, g in enumerate(outer):
-        neighbours(places, words[i], g, off.at[i], kind.at[i], dist)
+    for i, (word, rows, g, _) in enumerate(stages):
+        neighbours(rows, word, g, off.at[i], kind.at[i], dist)
         describe(kind.at[i], dist, rates, rad.at[i], desc.at[i])
         row = 4 * (g + 1) + 3
-        lefts.append(left_factor(desc.at[i], places[row : row + 1, :]))
+        lefts.append(left_factor(desc.at[i], rows[row : row + 1, :]))
     if inner:
         lefts += [left_inner[i] for i in range(left_inner.shape[0])]
     slopes = network(lefts, pairs, wout)
-    for i in range(len(outer)):
+    for i in range(len(stages)):
         grad[i] = slopes[i]
-    for i in range(len(outer), len(slopes)):
-        grad_inner[i - len(outer)] = slopes[i]
+    for i in range(len(stages), len(slopes)):
+        grad_inner[i - len(stages)] = slopes[i]
 
     out[...] = jnp.zeros_like(out)
-    for i, g in enumerate(outer):
+    for i, (word, rows, g, target) in enumerate(stages):
         slot_slopes(grad.at[i], kind.at[i], rates, rad.at[i], dist)
-        centre = pair_forces(words[i], dist, off.at[i], pair, rel)
-        scatter(pair, rel, slots, out, g, centre)
+        centre = pair_forces(word, dist, off.at[i], pair, rel)
+        scatter(pair, rel, slots, target, g, None if rows is beyond else centre)
     if direct:
-        lower, upper = out[0:4, :], out[4 * groups + 4 :, :]
-        to_inner[...] = jnp.where(even, upper, lower)
-        to_outer[...] = jnp.where(even, lower, upper)
+        out[4:8, :] += jnp.where(even, pulled[8:12, :], 0.0)
+        out[4 * groups : 4 * groups + 4, :] += jnp.where(even, 0.0, pulled[0:4, :])
+        to_inner[...] = jnp.where(even, out[4 * groups + 4 :, :], out[0:4, :])
 
 
 def outer_stage(blocks, code, pairs, rates, wout, left_inner):
@@ -433,7 +446,8 @@
     out_shape = [pltpu.VMEM((4 * (groups + 2), LANES), f32)]
     operands = [*blocks, code, *pairs, rates, wout]
     if direct:
-        out_shape += [pltpu.VMEM((4, LANES), f32)] * 2
+        out_shape.append(pltpu.VMEM((4, LANES), f32))
+        count += 1
     if inner:
         out_shape.append(pltpu.VMEM((inner, chan, LANES), f32))
         operands.append(left_inner)
@@ -452,6 +466,8 @@
             pltpu.VMEM((count, chan, LANES), f32),
             pltpu.VMEM((6, slots, LANES), f32),
             pltpu.VMEM((2, slots, LANES), jnp.int32),
+            pltpu.VMEM((12, LANES), f32),
+            pltpu.VMEM((12, LANES), f32),
         ],
         compiler_params=PARAMS,
         cost_estimate=cost(3.0),
@@ -488,18 +504,18 @@
 
 
 def combine_kernel(inner, force, *refs):
-    *rest, got_outer, got_inner, out = refs
+    *rest, got_inner, out = refs
     total = force[4 : force.shape[0] - 4, :]
     if inner:
         total = total + rest[0][...]
     even = at_even("space")
     out[...] = total
-    out[0:4, :] += jnp.where(even, got_outer[...], got_inner[...])
-    out[out.shape[0] - 4 :, :] += jnp.where(even, got_inner[...], got_outer[...])
-
-
-def combine(force, inner, got_inner, got_outer):
-    operands = [force, *inner, got_outer, got_inner]
+    out[0:4, :] += jnp.where(even, 0.0, got_inner[...])
+    out[out.shape[0] - 4 :, :] += jnp.where(even, got_inner[...], 0.0)
+
+
+def combine(force, inner, got_inner):
+    operands = [force, *inner, got_inner]
     return pl.pallas_call(
         functools.partial(combine_kernel, len(inner)),
         out_shape=pltpu.VMEM((force.shape[0] - 8, LANES), jnp.float32),
@@ -524,8 +540,8 @@
 
 
 def contract_kernel(table, beads, *refs):
-    blocks, species = arranged(GATHER, refs), refs[NC]
-    out, to_inner, to_outer = refs[NC + 1 :]
+    blocks, species, code = arranged(GATHER, refs), refs[NC], refs[NC + 1]
+    out, to_inner, to_outer = refs[NC + 2 :]
     tiles = species.shape[0]
     for c in range(3):
         total = None
@@ -536,26 +552,27 @@
                 total = term if total is None else total + term
         out[pl.ds(c, tiles, stride=4), :] = total
     out[pl.ds(3, tiles, stride=4), :] = species[...]
-    bottom, top = out[0:4, :], out[4 * tiles - 4 :, :]
     even = at_even("space")
-    to_inner[...] = jnp.where(even, top, bottom)
-    to_outer[...] = jnp.where(even, bottom, top)
-
-
-def contract(table, beads, blocks, species):
+    last = code.shape[1] - LANES
+    to_inner[...] = jnp.where(even, out[4 * tiles - 4 :, :], out[0:4, :])
+    to_outer[0:8, :] = jnp.where(even, out[0:8, :], out[4 * tiles - 8 :, :])
+    to_outer[8:, :] = jnp.where(even, code[:, 0:LANES], code[:, last:]).astype(jnp.float32)
+
+
+def contract(table, beads, blocks, species, code):
     return pl.pallas_call(
         functools.partial(contract_kernel, table, beads),
         out_shape=[
             pltpu.VMEM((4 * species.shape[0], LANES), jnp.float32),
             pltpu.VMEM((4, LANES), jnp.float32),
-            pltpu.VMEM((4, LANES), jnp.float32),
+            pltpu.VMEM((8 + code.shape[0], LANES), jnp.float32),
         ],
-        in_specs=[VMEM] * (NC + 1),
+        in_specs=[VMEM] * (NC + 2),
         out_specs=[VMEM] * 3,
         compiler_params=PARAMS,
         cost_estimate=cost(0.2),
         name="contract",
-    )(blocks[0], *(blocks[r] for r in GATHER[1]), species)
+    )(blocks[0], *(blocks[r] for r in GATHER[1]), species, code)
 
 
 def masses_of(species):
@@ -627,14 +644,15 @@
     )(forces[0], *(forces[r] for r in SPREAD[1]), kicked, species)
 
 
-def swap_with_adjacent(send_inner, send_outer):
+def swap_inner(block):
     count = lax.axis_size("space")
-    inner = [(i, i ^ 1) for i in range(count)]
-    outer = [(i, (i + 1) % count if i % 2 else (i - 1) % count) for i in range(count)]
-    return (
-        lax.ppermute(send_inner, "space", inner),
-        lax.ppermute(send_outer, "space", outer),
-    )
+    return lax.ppermute(block, "space", [(i, i ^ 1) for i in range(count)])
+
+
+def swap_outer(block):
+    count = lax.axis_size("space")
+    pairs = [(i, (i + 1) % count if i % 2 else (i - 1) % count) for i in range(count)]
+    return lax.ppermute(block, "space", pairs)
 
 
 def arranged(plan, refs):
@@ -679,9 +697,9 @@
     bead_count = bead_dev * bead_groups
     table = contraction_table(bead_count, NC)
     place = lax.axis_index("bead")
-    direct = bead_groups == NC
+    tiles = atom_dev // LANES
+    direct = bead_groups == NC and tiles > 1
     block_size = atom_dev * NC // bead_groups
-    tiles = atom_dev // LANES
 
     if direct:
         block_start = 0
@@ -706,7 +724,7 @@
 
     if direct:
         blocks = around(GATHER, bead_rows(positions))
-        own, to_inner, to_outer = contract(table, bead_dev, blocks, kinds)
+        own, to_inner, to_outer = contract(table, bead_dev, blocks, kinds, code)
     else:
         replica = place % NC
         everything = lax.all_gather(positions, "bead", axis=0, tiled=True)
@@ -716,18 +734,18 @@
         own = jnp.concatenate([stacked, kinds[:, None]], axis=1).reshape(-1, LANES)
 
     if direct:
-        got = swap_with_adjacent(to_inner, to_outer)
+        got_outer, got_inner = swap_outer(to_outer), swap_inner(to_inner)
         inner_count = max(tiles - 2, 0)
         left_inner, others = None, []
         if inner_count:
             off, kind, rad, left_inner = inner_stage(own, code, rates, inner_count)
-        force, to_inner, to_outer, *grad_inner = outer_stage(
-            [own, *got[::-1]], code, pairs, rates, wout, left_inner
+        force, to_inner, *grad_inner = outer_stage(
+            [own, got_outer, got_inner], code, pairs, rates, wout, left_inner
         )
-        got = swap_with_adjacent(to_inner, to_outer)
+        got_inner = swap_inner(to_inner)
         if inner_count:
             others = [inner_forces(code, rates, off, kind, rad, *grad_inner)]
-        forces = around(SPREAD, combine(force, others, *got))
+        forces = around(SPREAD, combine(force, others, got_inner))
         kicked = spring_kick(
             bead_dev, blocks[0], blocks[1], blocks[NC - 1], bead_rows(momenta), kinds
         )
@@ -736,9 +754,8 @@
 
     even = at_even("space")
     bottom, top = own[:4], own[4 * tiles - 4 :]
-    got_inner, got_outer = swap_with_adjacent(
-        jnp.where(even, top, bottom), jnp.where(even, bottom, top)
-    )
+    got_inner = swap_inner(jnp.where(even, top, bottom))
+    got_outer = swap_outer(jnp.where(even, bottom, top))
     window = jnp.concatenate(
         [
             jnp.where(even, got_outer, got_inner),
@@ -765,9 +782,8 @@
     force = lax.psum(chosen[:, None, None] * partial[None], "bead")
 
     lower, middle, upper = force[:, :4], force[:, 4:-4], force[:, -4:]
-    got_inner, got_outer = swap_with_adjacent(
-        jnp.where(even, upper, lower), jnp.where(even, lower, upper)
-    )
+    got_inner = swap_inner(jnp.where(even, upper, lower))
+    got_outer = swap_outer(jnp.where(even, lower, upper))
     middle = jnp.concatenate(
         [
             middle[:, :4] + jnp.where(even, got_outer, got_inner),

time: 26.8 us -> 26 us (0.970)
  starting transfers between devices: 13.2 us -> 11.7 us
  Pallas kernels: 6.95 us -> 7.67 us
    ppermute x4 -> x3, starting transfers between devices: 3.32 us -> 1.84 us  [the longest x2 1.77 us: swap_inner(): return lax.ppermute(block, 'space', [(i, i ^ 1) for i in range(count)])]
    pallas_call x1, Pallas kernels: 3.07 us -> 3.82 us  [outer_stage(): pl.pallas_call(functools.partial(outer_kernel, direct, inner), out_shape=...]
    ppermute x4 -> x3, waiting for transfers between devices: 1.2 us -> 1.23 us  [the longest x1 0.95 us: swap_outer(): return lax.ppermute(block, 'space', pairs)]
  transfers between devices with their start and end apart: 10 -> 9, of which waited for: 5 -> 6; matrix products, arithmetic and copies ran while one was open for 0% -> 0% of each run, Pallas kernels for 12% -> 12%
where the time goes in v4:
time: 26 us; the launch traced here: 25.9 us
  starting transfers between devices  11.7 us (45%)
  Pallas kernels  7.67 us (30%)
  waiting for transfers between devices  5.8 us (22%)
  between operations  0.7 us (3%)
    ppermute x6, starting transfers between devices, around(): blocks.append(lax.ppermute(block, 'bead', pairs))  9.87 us
    ppermute x6, waiting for transfers between devices, around(): blocks.append(lax.ppermute(block, 'bead', pairs))  4.57 us
    pallas_call x1, Pallas kernels, outer_stage(): pl.pallas_call(functools.partial(outer_kernel, direct, inner), out_shape=...  3.82 us
    ppermute x2, starting transfers between devices, swap_inner(): return lax.ppermute(block, 'space', [(i, i ^ 1) for i in range(count)])  1.77 us
    pallas_call x1, Pallas kernels, prepare(): pl.pallas_call(functools.partial(prepare_kernel, slab_atoms, block_start)...  1.59 us
    ppermute x1, waiting for transfers between devices, swap_outer(): return lax.ppermute(block, 'space', pairs)  0.95 us
    pallas_call x1, Pallas kernels, inner_forces(): pl.pallas_call(inner_force_kernel, out_shape=pltpu.VMEM((block // LANES *...  0.84 us
    pallas_call x1, Pallas kernels, inner_stage(): pl.pallas_call(inner_kernel, out_shape=out_shape, in_specs=[VMEM] * 3, ou...  0.74 us
  transfers between devices with their start and end apart: 9, of which 6 were waited for; matrix products, arithmetic and copies ran while one was open for 0% of the time, Pallas kernels for 12%

profile of v4, /device:TPU:0, one launch (start us, length us, event | category | flops | bytes accessed | tf_op | source)
XLA Modules:
  0.0 25.9 jit_solution(12819336122857384597)
XLA Ops:
  0.6 4.1 %collective-permute-start.2 = (f32[24,128]{1,0:T(8,128)}, f32[24,128]{1,0:T(8,128)S(1)}, u32[]{:S(2)}, u32[]{:S(2)}) collective-permute-start(f32[24,128]{1,0:T(8,128)} %bitcast.25), channel_id=1, source_target_pairs={{0,8},{4,12},{8,0},{12,4},{1,9},{5,13},{9,1},{13,5},{2,10},{6,14},... | collective-permute-start | bytes 36872 | tf_op jit(solution)/shard_map/ppermute | solution.py:677
  4.7 1.3 %collective-permute-start.1 = (f32[24,128]{1,0:T(8,128)}, f32[24,128]{1,0:T(8,128)S(1)}, u32[]{:S(2)}, u32[]{:S(2)}) collective-permute-start(f32[24,128]{1,0:T(8,128)} %bitcast.26), channel_id=1, source_target_pairs={{0,12},{4,8},{8,4},{12,0},{1,13},{5,9},{9,5},{13,1},{2,14},{6,10},... | collective-permute-start | bytes 36872 | tf_op jit(solution)/shard_map/ppermute | solution.py:677
  6.1 0.2 collective-permute-start
  6.3 0.0 copy-start
  6.3 1.6 %prepare.1 = (s32[32,512]{1,0:T(8,128)S(1)}, f32[4,128]{1,0:T(4,128)S(1)}, bf16[384,256]{1,0:T(8,128)(2,1)S(1)}, bf16[512,256]{1,0:T(8,128)(2,1)S(1)}, bf16[512,...) custom-call(s32[32,512]{1,0:T(8,128)} %refs_0_.1, ...), custom_call_target="tpu_custom_call" | custom-call | bytes 3600000 | tf_op jit(solution)/shard_map/prepare/pallas_call | solution.py:156
  7.9 0.0 collective-permute-done.2.refs_3_
  7.9 2.5 %collective-permute-done.1.refs_2_.after = f32[24,128]{1,0:T(8,128)S(1)} collective-permute-done((f32[24,128]{1,0:T(8,128)}, f32[24,128]{1,0:T(8,128)S(1)}, u32[]{:S(2)}, u32[]{:S(2)}) %collective-permute-start.1) | collective-permute-done | bytes 12320 | tf_op jit(solution)/shard_map/ppermute | solution.py:677
  10.4 0.0 collective-permute-done.refs_1_.before
  10.4 0.0 copy-done
  10.5 0.1 collective-permute-start.3
  10.6 1.6 %collective-permute-start.4 = (f32[4,128]{1,0:T(4,128)S(1)}, f32[4,128]{1,0:T(4,128)S(1)}, u32[]{:S(2)}, u32[]{:S(2)}) collective-permute-start(f32[4,128]{1,0:T(4,128)S(1)} %get-tuple-element.27), channel_id=1, source_target_pairs={{0,1},{1,0},{2,3},{3,2},{4,5},{5,4},{6,7},{7,6},{8,9},{9,8},{10,11... | collective-permute-start | bytes 6152 | tf_op jit(solution)/shard_map/ppermute | solution.py:649
  12.1 0.7 %inner_descriptor.1 = (f32[2,3,32,128]{3,2,1,0:T(8,128)S(1)}, f32[2,32,128]{2,1,0:T(8,128)S(1)}, f32[2,1024,128]{2,1,0:T(8,128)S(1)}, bf16[2,128,512]{2,1,0:T(8,128)(2,1)S(1)}) custom-call(f32[16,128]{1,0:T(8,128)S(1)} %get-tuple-element.25.own.refs_0_, s32[32,512]{1,0:T(8,128)S(1)} %get-tuple-element.24.refs_5_.code.refs_3_, ...), custom_call_target="tpu_custom_call" | custom-call | bytes 3000000 | tf_op jit(solution)/shard_map/inner_descriptor/pallas_call | solution.py:357
  12.9 0.1 collective-permute-done.4.refs_2_
  13.0 0.9 %collective-permute-done.3.refs_1_ = f32[40,128]{1,0:T(8,128)S(1)} collective-permute-done((f32[40,128]{1,0:T(8,128)S(1)}, f32[40,128]{1,0:T(8,128)S(1)}, u32[]{:S(2)}, u32[]{:S(2)}) %collective-permute-start.3) | collective-permute-done | bytes 20512 | tf_op jit(solution)/shard_map/ppermute | solution.py:655
  13.9 3.8 %outer_forces.1 = (f32[24,128]{1,0:T(8,128)S(1)}, f32[4,128]{1,0:T(4,128)S(1)}, f32[2,128,128]{2,1,0:T(8,128)S(1)}) custom-call(f32[16,128]{1,0:T(8,128)S(1)} %get-tuple-element.25.own.refs_0_, f32[40,128]{1,0:T(8,128)S(1)} %collective-permute-done.3.refs_1_, f32[4,128]{1,0:T(4,128)S(1)} %collective-permute-done.4.refs_2_, ...), custom_call_target="tpu_custom_call" | custom-call | bytes 9000000 | tf_op jit(solution)/shard_map/outer_forces/pallas_call | solution.py:454
  17.7 0.2 collective-permute-start.5
  17.9 0.8 %inner_forces.1.refs_0_ = f32[16,128]{1,0:T(8,128)S(1)} custom-call(s32[32,512]{1,0:T(8,128)S(1)} %get-tuple-element.24.refs_5_.code.refs_3_, f32[32,128]{1,0:T(8,128)S(1)} %get-tuple-element.33.rates.refs_9_, f32[2,3,32,128]{3,2,1,0:T(8,128)S(1)} %get-tuple-element.37.off, f32[2,32,128]{2,1,0:T(8,128)S(1)} %get-tuple-element.38.kind, ...), custom_call_target="tpu_custom_call" | custom-call | bytes 3600000 | tf_op jit(solution)/shard_map/inner_forces/pallas_call | solution.py:490
  18.8 0.2 collective-permute-done.5.refs_1_
  19.0 0.0 copy-start.1
  19.0 0.1 collective-permute-start.8
  19.0 2.6 %collective-permute-start.7 = (f32[16,128]{1,0:T(8,128)S(1)}, f32[16,128]{1,0:T(8,128)S(1)}, u32[]{:S(2)}, u32[]{:S(2)}) collective-permute-start(f32[16,128]{1,0:T(8,128)S(1)} %combine.1.refs_0_), channel_id=1, source_target_pairs={{0,8},{4,12},{8,0},{12,4},{1,9},{5,13},{9,1},{13,5},{2,10},{6,14},... | collective-permute-start | bytes 24584 | tf_op jit(solution)/shard_map/ppermute | solution.py:677
  21.6 1.6 %collective-permute-start.6 = (f32[16,128]{1,0:T(8,128)S(1)}, f32[16,128]{1,0:T(8,128)S(1)}, u32[]{:S(2)}, u32[]{:S(2)}) collective-permute-start(f32[16,128]{1,0:T(8,128)S(1)} %combine.1.refs_0_), channel_id=1, source_target_pairs={{0,12},{4,0},{8,4},{12,8},{1,13},{5,1},{9,5},{13,9},{2,14},{6,2},{... | collective-permute-start | bytes 24584 | tf_op jit(solution)/shard_map/ppermute | solution.py:677
  23.2 0.0 copy-done.1
  23.2 1.3 %collective-permute-done.8.refs_3_ = f32[16,128]{1,0:T(8,128)S(1)} collective-permute-done((f32[16,128]{1,0:T(8,128)S(1)}, f32[16,128]{1,0:T(8,128)S(1)}, u32[]{:S(2)}, u32[]{:S(2)}) %collective-permute-start.8) | collective-permute-done | bytes 8224 | tf_op jit(solution)/shard_map/ppermute | solution.py:677
  24.5 0.0 collective-permute-done.7.refs_2_
  24.5 0.8 %collective-permute-done.6.refs_1_ = f32[16,128]{1,0:T(8,128)S(1)} collective-permute-done((f32[16,128]{1,0:T(8,128)S(1)}, f32[16,128]{1,0:T(8,128)S(1)}, u32[]{:S(2)}, u32[]{:S(2)}) %collective-permute-start.6) | collective-permute-done | bytes 8224 | tf_op jit(solution)/shard_map/ppermute | solution.py:677
  25.3 0.6 %expand.1 = (f32[24,128]{1,0:T(8,128)}, f32[24,128]{1,0:T(8,128)}) custom-call(f32[16,128]{1,0:T(8,128)S(1)} %combine.1.refs_0_, f32[16,128]{1,0:T(8,128)S(1)} %collective-permute-done.6.refs_1_, f32[16,128]{1,0:T(8,128)S(1)} %collective-permute-done.7.refs_2_, f32[16,128]{1,0:T(8,128)S(1)} %collective-permute-done.8.refs_3_, ...), custom_call_target="tpu_custom_call" | custom-call | bytes 2400000 | tf_op jit(solution)/shard_map/expand/pallas_call | solution.py:636
  (3 shorter events, 0.1 us)
Async XLA Ops:
  0.6 7.3 %collective-permute-start.2 = (f32[24,128]{1,0:T(8,128)}, f32[24,128]{1,0:T(8,128)S(1)}, u32[]{:S(2)}, u32[]{:S(2)}) collective-permute-start(f32[24,128]{1,0:T(8,128)} %bitcast.25), channel_id=1, source_target_pairs={{0,8},{4,12},{8,0},{12,4},{1,9},{5,13},{9,1},{13,5},{2,10},{6,14},... | collective-permute-start | bytes 36872 | tf_op jit(solution)/shard_map/ppermute | solution.py:677
  4.7 5.7 %collective-permute-start.1 = (f32[24,128]{1,0:T(8,128)}, f32[24,128]{1,0:T(8,128)S(1)}, u32[]{:S(2)}, u32[]{:S(2)}) collective-permute-start(f32[24,128]{1,0:T(8,128)} %bitcast.26), channel_id=1, source_target_pairs={{0,12},{4,8},{8,4},{12,0},{1,13},{5,9},{9,5},{13,1},{2,14},{6,10},... | collective-permute-start | bytes 36872 | tf_op jit(solution)/shard_map/ppermute | solution.py:677
  6.1 4.4 %collective-permute-start = (f32[24,128]{1,0:T(8,128)}, f32[24,128]{1,0:T(8,128)S(1)}, u32[]{:S(2)}, u32[]{:S(2)}) collective-permute-start(f32[24,128]{1,0:T(8,128)} %bitcast.27), channel_id=1, source_target_pairs={{0,4},{4,0},{8,12},{12,8},{1,5},{5,1},{9,13},{13,9},{2,6},{6,2},{1... | collective-permute-start | bytes 36872 | tf_op jit(solution)/shard_map/ppermute | solution.py:677
  6.3 4.1 %copy-start = (f32[2,3,512]{2,0,1:T(2,128)S(1)}, f32[2,3,512]{2,0,1:T(2,128)}, u32[]{:S(2)}) copy-start(f32[2,3,512]{2,0,1:T(2,128)} %param.11) | copy-start | bytes 36868
  10.5 3.4 %collective-permute-start.3 = (f32[40,128]{1,0:T(8,128)S(1)}, f32[40,128]{1,0:T(8,128)S(1)}, u32[]{:S(2)}, u32[]{:S(2)}) collective-permute-start(f32[40,128]{1,0:T(8,128)S(1)} %get-tuple-element.26), channel_id=1, source_target_pairs={{0,3},{1,2},{2,1},{3,0},{4,7},{5,6},{6,5},{7,4},{8,11},{9,10},{10,... | collective-permute-start | bytes 61448 | tf_op jit(solution)/shard_map/ppermute | solution.py:655
  10.6 2.4 %collective-permute-start.4 = (f32[4,128]{1,0:T(4,128)S(1)}, f32[4,128]{1,0:T(4,128)S(1)}, u32[]{:S(2)}, u32[]{:S(2)}) collective-permute-start(f32[4,128]{1,0:T(4,128)S(1)} %get-tuple-element.27), channel_id=1, source_target_pairs={{0,1},{1,0},{2,3},{3,2},{4,5},{5,4},{6,7},{7,6},{8,9},{9,8},{10,11... | collective-permute-start | bytes 6152 | tf_op jit(solution)/shard_map/ppermute | solution.py:649
  17.7 1.2 %collective-permute-start.5 = (f32[4,128]{1,0:T(4,128)S(1)}, f32[4,128]{1,0:T(4,128)S(1)}, u32[]{:S(2)}, u32[]{:S(2)}) collective-permute-start(f32[4,128]{1,0:T(4,128)S(1)} %get-tuple-element.41), channel_id=1, source_target_pairs={{0,1},{1,0},{2,3},{3,2},{4,5},{5,4},{6,7},{7,6},{8,9},{9,8},{10,11... | collective-permute-start | bytes 6152 | tf_op jit(solution)/shard_map/ppermute | solution.py:649
  19.0 4.2 %copy-start.1 = (f32[2,3,512]{2,0,1:T(2,128)S(1)}, f32[2,3,512]{2,0,1:T(2,128)}, u32[]{:S(2)}) copy-start(f32[2,3,512]{2,0,1:T(2,128)} %param.12) | copy-start | bytes 36868
  19.0 5.5 %collective-permute-start.8 = (f32[16,128]{1,0:T(8,128)S(1)}, f32[16,128]{1,0:T(8,128)S(1)}, u32[]{:S(2)}, u32[]{:S(2)}) collective-permute-start(f32[16,128]{1,0:T(8,128)S(1)} %combine.1.refs_0_), channel_id=1, source_target_pairs={{0,4},{4,8},{8,12},{12,0},{1,5},{5,9},{9,13},{13,1},{2,6},{6,10},{... | collective-permute-start | bytes 24584 | tf_op jit(solution)/shard_map/ppermute | solution.py:677
  19.0 5.4 %collective-permute-start.7 = (f32[16,128]{1,0:T(8,128)S(1)}, f32[16,128]{1,0:T(8,128)S(1)}, u32[]{:S(2)}, u32[]{:S(2)}) collective-permute-start(f32[16,128]{1,0:T(8,128)S(1)} %combine.1.refs_0_), channel_id=1, source_target_pairs={{0,8},{4,12},{8,0},{12,4},{1,9},{5,13},{9,1},{13,5},{2,10},{6,14},... | collective-permute-start | bytes 24584 | tf_op jit(solution)/shard_map/ppermute | solution.py:677
  21.6 3.7 %collective-permute-start.6 = (f32[16,128]{1,0:T(8,128)S(1)}, f32[16,128]{1,0:T(8,128)S(1)}, u32[]{:S(2)}, u32[]{:S(2)}) collective-permute-start(f32[16,128]{1,0:T(8,128)S(1)} %combine.1.refs_0_), channel_id=1, source_target_pairs={{0,12},{4,0},{8,4},{12,8},{1,13},{5,1},{9,5},{13,9},{2,14},{6,2},{... | collective-permute-start | bytes 24584 | tf_op jit(solution)/shard_map/ppermute | solution.py:677

commit v5 on v4

--- a/solution.py
+++ b/solution.py
@@ -229,8 +229,15 @@
     return jnp.concatenate([high, high, low, onehot], axis=1)
 
 
-def network(lefts, pairs, wout):
-    t1, t2, t3, l2, l3 = pairs
+def dense(x, pair):
+    high, low = split2(x)
+    rows = pair.shape[0] // 2
+    right = jnp.concatenate([pair[...], pair[0:rows, :]], axis=0)
+    return dot(jnp.concatenate([high, high, low], axis=1), right)
+
+
+def forward(lefts, pairs, wout):
+    t1, t2, t3 = pairs
     chan = t1.shape[0] // 3
     first = jnp.concatenate([t1[0 : 2 * chan, :], t1[0:chan, :], t1[2 * chan :, :]], axis=0)
 
@@ -239,18 +246,17 @@
         value = x * sig
         return value, sig + value * (1.0 - sig)
 
-    def layer(x, pair):
-        high, low = split2(x)
-        rows = pair.shape[0] // 2
-        right = jnp.concatenate([pair[...], pair[0:rows, :]], axis=0)
-        return dot(jnp.concatenate([high, high, low], axis=1), right)
-
     one = [act(dot(left, first)) for left in lefts]
-    two = [act(layer(h, t2)) for h, _ in one]
-    three = [act(layer(h, t3))[1] for h, _ in two]
-    back = [wout[0:1, :] * s for s in three]
-    back = [layer(g, l3) * s for g, (_, s) in zip(back, two)]
-    back = [layer(g, l2) * s for g, (_, s) in zip(back, one)]
+    two = [act(dense(h, t2)) for h, _ in one]
+    three = [wout[0:1, :] * act(dense(h, t3))[1] for h, _ in two]
+    return [(s1, s2, g3) for (_, s1), (_, s2), g3 in zip(one, two, three, strict=True)]
+
+
+def backward(states, pairs):
+    t1, l2, l3 = pairs
+    chan = t1.shape[0] // 3
+    back = [dense(g3, l3) * s2 for _, s2, g3 in states]
+    back = [dense(g, l2) * s1 for g, (s1, _, _) in zip(back, states, strict=True)]
     last = jnp.concatenate(
         [t1[0:chan, :], t1[chan : 2 * chan, :], t1[0:chan, :]], axis=1
     )
@@ -292,8 +298,8 @@
     for o in range(word.shape[0] // 8):
         rows = slice(8 * o, 8 * o + 8)
         part = jnp.bitwise_and(word[rows, :], DEAD - 1)
-        rel[0, rows, :] = jnp.bitwise_and(part, 63)
-        rel[1, rows, :] = jnp.right_shift(part, 6)
+        rel[0, rows, :] = jnp.bitwise_and(part, 63).astype(jnp.float32)
+        rel[1, rows, :] = jnp.right_shift(part, 6).astype(jnp.float32)
         twice = jnp.where(word[rows, :] >= DEAD, 0.0, 2.0 * slope[rows, :])
         for c in range(3):
             force = twice * off[c, rows, :]
@@ -305,21 +311,28 @@
 
 
 def scatter(pair, rel, slots, out, block0, centre):
-    low_ids = lax.broadcasted_iota(jnp.int32, (64, LANES), 0)
-    high_ids = lax.broadcasted_iota(jnp.int32, (8, LANES), 0)
+    half = jnp.bfloat16
+    low_ids = lax.broadcasted_iota(jnp.int32, (64, LANES), 0).astype(half)
+    high_ids = lax.broadcasted_iota(jnp.int32, (16, LANES), 0)
+    high_ids = jnp.bitwise_and(high_ids, 7).astype(half)
+    ones, zeros = jnp.ones((64, LANES), half), jnp.zeros((64, LANES), half)
     total = jnp.zeros((48, 64), jnp.float32)
     for n in range(0, slots, 2):
         lefts, rights = [], []
         for k in (n, n + 1):
-            low = rel[0, k : k + 1, :]
-            high = jnp.broadcast_to(rel[1, k : k + 1, :], (8, LANES))
-            rights.append(jnp.where(low_ids == low, 1.0, 0.0).astype(jnp.bfloat16))
+            low = jnp.broadcast_to(rel[0, k : k + 1, :], (16, LANES)).astype(half)
+            high = jnp.broadcast_to(rel[1, k : k + 1, :], (16, LANES)).astype(half)
+            low = jnp.concatenate([low] * 4, axis=0)
+            rights.append(jnp.where(low_ids == low, ones, zeros))
             hit = high_ids == high
-            picked = [
-                jnp.where(hit, jnp.broadcast_to(pair[c, k : k + 1, :], (8, LANES)), 0.0)
-                for c in range(6)
-            ]
-            lefts.append(jnp.concatenate(picked, axis=0).astype(jnp.bfloat16))
+            for c in range(3):
+                terms = [
+                    jnp.broadcast_to(pair[2 * c + i, k : k + 1, :], (8, LANES))
+                    for i in range(2)
+                ]
+                terms = jnp.concatenate(terms, axis=0).astype(half)
+                lefts.append(jnp.where(hit, terms, zeros[0:16]))
+        lefts = [jnp.concatenate(lefts[0:3], axis=0), jnp.concatenate(lefts[3:6], axis=0)]
         total = total + dot_nt(
             jnp.concatenate(lefts, axis=1), jnp.concatenate(rights, axis=1)
         )
@@ -335,16 +348,20 @@
             out[row : row + 1, :] = out[row : row + 1, :] + both
 
 
-def inner_kernel(own, code, rates, off, kind, rad, left, dist, desc):
+def inner_kernel(own, code, rates, t1, t2, t3, wout, off, kind, rad, state, dist, desc):
+    lefts = []
     for i in range(kind.shape[0]):
         word = code[:, (i + 1) * LANES : (i + 2) * LANES]
-        neighbours(own, word, i, off.at[i], kind.at[i], dist)
-        describe(kind.at[i], dist, rates, rad.at[i], desc)
+        neighbours(own, word, i, off.at[i], kind.at[i], dist.at[i])
+        describe(kind.at[i], dist.at[i], rates, rad.at[i], desc.at[i])
         row = 4 * (i + 1) + 3
-        left[i] = left_factor(desc, own[row : row + 1, :])
-
-
-def inner_stage(own, code, rates, count):
+        lefts.append(left_factor(desc.at[i], own[row : row + 1, :]))
+    for i, values in enumerate(forward(lefts, (t1, t2, t3), wout)):
+        for j, value in enumerate(values):
+            state[i, j] = value
+
+
+def inner_stage(own, code, rates, pairs, wout, count):
     slots = code.shape[0]
     rate_count = rates.shape[0]
     chan = SPECIES * rate_count
@@ -352,21 +369,21 @@
         pltpu.VMEM((count, 3, slots, LANES), jnp.float32),
         pltpu.VMEM((count, slots, LANES), jnp.float32),
         pltpu.VMEM((count, slots * rate_count, LANES), jnp.float32),
-        pltpu.VMEM((count, LANES, 4 * chan), jnp.bfloat16),
+        pltpu.VMEM((count, 3, LANES, wout.shape[1]), jnp.float32),
     ]
     return pl.pallas_call(
         inner_kernel,
         out_shape=out_shape,
-        in_specs=[VMEM] * 3,
+        in_specs=[VMEM] * 7,
         out_specs=[VMEM] * 4,
         scratch_shapes=[
-            pltpu.VMEM((slots, LANES), jnp.float32),
-            pltpu.VMEM((chan, LANES), jnp.float32),
+            pltpu.VMEM((count, slots, LANES), jnp.float32),
+            pltpu.VMEM((count, chan, LANES), jnp.float32),
         ],
         compiler_params=PARAMS,
         cost_estimate=cost(1.0),
-        name="inner_descriptor",
-    )(own, code, rates)
+        name="inner_forward",
+    )(own, code, rates, *pairs[:3], wout)
 
 
 def outer_kernel(direct, inner, *refs):
@@ -379,7 +396,7 @@
 
     blocks = take(3 if direct else 1)
     code, *pairs, rates, wout = take(9 - 1)
-    left_inner = take(1)[0] if inner else None
+    state_inner = take(1)[0] if inner else None
     out = take(1)[0]
     to_inner = take(1)[0] if direct else None
     grad_inner = take(1)[0] if inner else None
@@ -411,13 +428,15 @@
         places[...] = blocks[0][...]
     lefts = []
     for i, (word, rows, g, _) in enumerate(stages):
-        neighbours(rows, word, g, off.at[i], kind.at[i], dist)
-        describe(kind.at[i], dist, rates, rad.at[i], desc.at[i])
+        neighbours(rows, word, g, off.at[i], kind.at[i], dist.at[i])
+        describe(kind.at[i], dist.at[i], rates, rad.at[i], desc.at[i])
         row = 4 * (g + 1) + 3
         lefts.append(left_factor(desc.at[i], rows[row : row + 1, :]))
+    t1, t2, t3, l2, l3 = pairs
+    states = forward(lefts, (t1, t2, t3), wout)
     if inner:
-        lefts += [left_inner[i] for i in range(left_inner.shape[0])]
-    slopes = network(lefts, pairs, wout)
+        states += [[state_inner[i, j] for j in range(3)] for i in range(inner)]
+    slopes = backward(states, (t1, l2, l3))
     for i in range(len(stages)):
         grad[i] = slopes[i]
     for i in range(len(stages), len(slopes)):
@@ -425,16 +444,18 @@
 
     out[...] = jnp.zeros_like(out)
     for i, (word, rows, g, target) in enumerate(stages):
-        slot_slopes(grad.at[i], kind.at[i], rates, rad.at[i], dist)
-        centre = pair_forces(word, dist, off.at[i], pair, rel)
-        scatter(pair, rel, slots, target, g, None if rows is beyond else centre)
+        slope = dist.at[i]
+        slot_slopes(grad.at[i], kind.at[i], rates, rad.at[i], slope)
+        centre = pair_forces(word, slope, off.at[i], pair.at[i], rel.at[i])
+        centre = None if rows is beyond else centre
+        scatter(pair.at[i], rel.at[i], slots, target, g, centre)
     if direct:
         out[4:8, :] += jnp.where(even, pulled[8:12, :], 0.0)
         out[4 * groups : 4 * groups + 4, :] += jnp.where(even, 0.0, pulled[0:4, :])
         to_inner[...] = jnp.where(even, out[4 * groups + 4 :, :], out[0:4, :])
 
 
-def outer_stage(blocks, code, pairs, rates, wout, left_inner):
+def outer_stage(blocks, code, pairs, rates, wout, state_inner):
     slots, block = code.shape
     rate_count = rates.shape[0]
     chan = SPECIES * rate_count
@@ -450,7 +471,7 @@
         count += 1
     if inner:
         out_shape.append(pltpu.VMEM((inner, chan, LANES), f32))
-        operands.append(left_inner)
+        operands.append(state_inner)
     return pl.pallas_call(
         functools.partial(outer_kernel, direct, inner),
         out_shape=out_shape,
@@ -460,12 +481,12 @@
             pltpu.VMEM((4 * (groups + 2), LANES), f32),
             pltpu.VMEM((count, 3, slots, LANES), f32),
             pltpu.VMEM((count, slots, LANES), f32),
-            pltpu.VMEM((slots, LANES), f32),
+            pltpu.VMEM((count, slots, LANES), f32),
             pltpu.VMEM((count, slots * rate_count, LANES), f32),
             pltpu.VMEM((count, chan, LANES), f32),
             pltpu.VMEM((count, chan, LANES), f32),
-            pltpu.VMEM((6, slots, LANES), f32),
-            pltpu.VMEM((2, slots, LANES), jnp.int32),
+            pltpu.VMEM((count, 6, slots, LANES), f32),
+            pltpu.VMEM((count, 2, slots, LANES), jnp.float32),
             pltpu.VMEM((12, LANES), f32),
             pltpu.VMEM((12, LANES), f32),
         ],
@@ -480,22 +501,23 @@
     out[...] = jnp.zeros_like(out)
     for i in range(kind.shape[0]):
         word = code[:, (i + 1) * LANES : (i + 2) * LANES]
-        slot_slopes(grad.at[i], kind.at[i], rates, rad.at[i], slope)
-        centre = pair_forces(word, slope, off.at[i], pair, rel)
-        scatter(pair, rel, slots, out, i, centre)
+        slot_slopes(grad.at[i], kind.at[i], rates, rad.at[i], slope.at[i])
+        centre = pair_forces(word, slope.at[i], off.at[i], pair.at[i], rel.at[i])
+        scatter(pair.at[i], rel.at[i], slots, out, i, centre)
 
 
 def inner_forces(code, rates, off, kind, rad, grad):
     slots, block = code.shape
+    count = kind.shape[0]
     return pl.pallas_call(
         inner_force_kernel,
         out_shape=pltpu.VMEM((block // LANES * 4, LANES), jnp.float32),
         in_specs=[VMEM] * 6,
         out_specs=VMEM,
         scratch_shapes=[
-            pltpu.VMEM((slots, LANES), jnp.float32),
-            pltpu.VMEM((6, slots, LANES), jnp.float32),
-            pltpu.VMEM((2, slots, LANES), jnp.int32),
+            pltpu.VMEM((count, slots, LANES), jnp.float32),
+            pltpu.VMEM((count, 6, slots, LANES), jnp.float32),
+            pltpu.VMEM((count, 2, slots, LANES), jnp.float32),
         ],
         compiler_params=PARAMS,
         cost_estimate=cost(1.2),
@@ -736,11 +758,13 @@
     if direct:
         got_outer, got_inner = swap_outer(to_outer), swap_inner(to_inner)
         inner_count = max(tiles - 2, 0)
-        left_inner, others = None, []
+        state_inner, others = None, []
         if inner_count:
-            off, kind, rad, left_inner = inner_stage(own, code, rates, inner_count)
+            off, kind, rad, state_inner = inner_stage(
+                own, code, rates, pairs, wout, inner_count
+            )
         force, to_inner, *grad_inner = outer_stage(
-            [own, got_outer, got_inner], code, pairs, rates, wout, left_inner
+            [own, got_outer, got_inner], code, pairs, rates, wout, state_inner
         )
         got_inner = swap_inner(to_inner)
         if inner_count:
@@ -767,11 +791,13 @@
     first = block_start // LANES * 4
     groups = block_size // LANES
     window = lax.dynamic_slice_in_dim(window, first, 4 * (groups + 2), 0)
-    left_inner = None
+    state_inner = None
     if groups > 2:
         inside = window[4 : 4 * groups + 4]
-        off, kind, rad, left_inner = inner_stage(inside, code, rates, groups - 2)
-    force, *grad_inner = outer_stage([window], code, pairs, rates, wout, left_inner)
+        off, kind, rad, state_inner = inner_stage(
+            inside, code, rates, pairs, wout, groups - 2
+        )
+    force, *grad_inner = outer_stage([window], code, pairs, rates, wout, state_inner)
     if groups > 2:
         force = force.at[4 : 4 * groups + 4].add(
             inner_forces(code, rates, off, kind, rad, *grad_inner)

time: 26 us -> 25.8 us (level)
  waiting for transfers between devices: 5.8 us -> 5.25 us
  Pallas kernels: 7.67 us -> 7.95 us
    pallas_call x1, Pallas kernels: 0.74 us -> 1.38 us  [inner_stage(): pl.pallas_call(inner_kernel, out_shape=out_shape, in_specs=[VMEM] * 7, ou...]
    ppermute x1, waiting for transfers between devices: 0.95 us -> 0.37 us  [swap_outer(): return lax.ppermute(block, 'space', pairs)]
  transfers between devices with their start and end apart: 9 -> 9, of which waited for: 6 -> 5; matrix products, arithmetic and copies ran while one was open for 0% -> 0% of each run, Pallas kernels for 12% -> 14%
where the time goes in v5:
time: 25.8 us; the launch traced here: 25.7 us
  starting transfers between devices  11.7 us (45%)
  Pallas kernels  7.95 us (31%)
  waiting for transfers between devices  5.25 us (20%)
  between operations  0.71 us (3%)
    ppermute x6, starting transfers between devices, around(): blocks.append(lax.ppermute(block, 'bead', pairs))  9.89 us
    ppermute x6, waiting for transfers between devices, around(): blocks.append(lax.ppermute(block, 'bead', pairs))  4.56 us
    pallas_call x1, Pallas kernels, outer_stage(): pl.pallas_call(functools.partial(outer_kernel, direct, inner), out_shape=...  3.58 us
    ppermute x2, starting transfers between devices, swap_inner(): return lax.ppermute(block, 'space', [(i, i ^ 1) for i in range(count)])  1.77 us
    pallas_call x1, Pallas kernels, prepare(): pl.pallas_call(functools.partial(prepare_kernel, slab_atoms, block_start)...  1.59 us
    pallas_call x1, Pallas kernels, inner_stage(): pl.pallas_call(inner_kernel, out_shape=out_shape, in_specs=[VMEM] * 7, ou...  1.38 us
    pallas_call x1, Pallas kernels, inner_forces(): pl.pallas_call(inner_force_kernel, out_shape=pltpu.VMEM((block // LANES *...  0.72 us
    pallas_call x1, Pallas kernels, expand(): pl.pallas_call(functools.partial(expand_kernel, table, beads), out_shape=...  0.62 us
  transfers between devices with their start and end apart: 9, of which 5 were waited for; matrix products, arithmetic and copies ran while one was open for 0% of the time, Pallas kernels for 14%

profile of v5, /device:TPU:0, one launch (start us, length us, event | category | flops | bytes accessed | tf_op | source)
XLA Modules:
  0.0 25.7 jit_solution(12341150142232304673)
XLA Ops:
  0.6 4.1 %collective-permute-start.2 = (f32[24,128]{1,0:T(8,128)}, f32[24,128]{1,0:T(8,128)S(1)}, u32[]{:S(2)}, u32[]{:S(2)}) collective-permute-start(f32[24,128]{1,0:T(8,128)} %bitcast.25), channel_id=1, source_target_pairs={{0,8},{4,12},{8,0},{12,4},{1,9},{5,13},{9,1},{13,5},{2,10},{6,14},... | collective-permute-start | bytes 36872 | tf_op jit(solution)/shard_map/ppermute | solution.py:699
  4.7 1.3 %collective-permute-start.1 = (f32[24,128]{1,0:T(8,128)}, f32[24,128]{1,0:T(8,128)S(1)}, u32[]{:S(2)}, u32[]{:S(2)}) collective-permute-start(f32[24,128]{1,0:T(8,128)} %bitcast.26), channel_id=1, source_target_pairs={{0,12},{4,8},{8,4},{12,0},{1,13},{5,9},{9,5},{13,1},{2,14},{6,10},... | collective-permute-start | bytes 36872 | tf_op jit(solution)/shard_map/ppermute | solution.py:699
  6.1 0.2 collective-permute-start
  6.3 0.0 copy-start
  6.3 1.6 %prepare.1 = (s32[32,512]{1,0:T(8,128)S(1)}, f32[4,128]{1,0:T(4,128)S(1)}, bf16[384,256]{1,0:T(8,128)(2,1)S(1)}, bf16[512,256]{1,0:T(8,128)(2,1)S(1)}, bf16[512,...) custom-call(s32[32,512]{1,0:T(8,128)} %refs_0_.1, ...), custom_call_target="tpu_custom_call" | custom-call | bytes 3600000 | tf_op jit(solution)/shard_map/prepare/pallas_call | solution.py:156
  7.9 0.0 collective-permute-done.2.refs_3_
  7.9 2.5 %collective-permute-done.1.refs_2_.after = f32[24,128]{1,0:T(8,128)S(1)} collective-permute-done((f32[24,128]{1,0:T(8,128)}, f32[24,128]{1,0:T(8,128)S(1)}, u32[]{:S(2)}, u32[]{:S(2)}) %collective-permute-start.1) | collective-permute-done | bytes 12320 | tf_op jit(solution)/shard_map/ppermute | solution.py:699
  10.4 0.0 collective-permute-done.refs_1_.before
  10.4 0.0 copy-done
  10.5 0.1 collective-permute-start.3
  10.6 1.6 %collective-permute-start.4 = (f32[4,128]{1,0:T(4,128)S(1)}, f32[4,128]{1,0:T(4,128)S(1)}, u32[]{:S(2)}, u32[]{:S(2)}) collective-permute-start(f32[4,128]{1,0:T(4,128)S(1)} %get-tuple-element.27), channel_id=1, source_target_pairs={{0,1},{1,0},{2,3},{3,2},{4,5},{5,4},{6,7},{7,6},{8,9},{9,8},{10,11... | collective-permute-start | bytes 6152 | tf_op jit(solution)/shard_map/ppermute | solution.py:671
  12.1 1.4 %inner_forward.1 = (f32[2,3,32,128]{3,2,1,0:T(8,128)S(1)}, f32[2,32,128]{2,1,0:T(8,128)S(1)}, f32[2,1024,128]{2,1,0:T(8,128)S(1)}, f32[2,3,128,256]{3,2,1,0:T(8,128)S(1)}) custom-call(f32[16,128]{1,0:T(8,128)S(1)} %get-tuple-element.25.own.refs_0_, s32[32,512]{1,0:T(8,128)S(1)} %get-tuple-element.24.refs_5_.code.refs_3_, ...), custom_call_target="tpu_custom_call" | custom-call | bytes 3000000 | tf_op jit(solution)/shard_map/inner_forward/pallas_call | solution.py:374
  13.5 0.0 collective-permute-done.4.refs_2_
  13.5 0.4 %collective-permute-done.3.refs_1_ = f32[40,128]{1,0:T(8,128)S(1)} collective-permute-done((f32[40,128]{1,0:T(8,128)S(1)}, f32[40,128]{1,0:T(8,128)S(1)}, u32[]{:S(2)}, u32[]{:S(2)}) %collective-permute-start.3) | collective-permute-done | bytes 20512 | tf_op jit(solution)/shard_map/ppermute | solution.py:677
  13.9 3.6 %outer_forces.1 = (f32[24,128]{1,0:T(8,128)S(1)}, f32[4,128]{1,0:T(4,128)S(1)}, f32[2,128,128]{2,1,0:T(8,128)S(1)}) custom-call(f32[16,128]{1,0:T(8,128)S(1)} %get-tuple-element.25.own.refs_0_, f32[40,128]{1,0:T(8,128)S(1)} %collective-permute-done.3.refs_1_, f32[4,128]{1,0:T(4,128)S(1)} %collective-permute-done.4.refs_2_, ...), custom_call_target="tpu_custom_call" | custom-call | bytes 9000000 | tf_op jit(solution)/shard_map/outer_forces/pallas_call | solution.py:475
  17.5 0.2 collective-permute-start.5
  17.7 0.7 %inner_forces.1.refs_0_ = f32[16,128]{1,0:T(8,128)S(1)} custom-call(s32[32,512]{1,0:T(8,128)S(1)} %get-tuple-element.24.refs_5_.code.refs_3_, f32[32,128]{1,0:T(8,128)S(1)} %get-tuple-element.33.rates.refs_9_, f32[2,3,32,128]{3,2,1,0:T(8,128)S(1)} %get-tuple-element.37.off, f32[2,32,128]{2,1,0:T(8,128)S(1)} %get-tuple-element.38.kind, ...), custom_call_target="tpu_custom_call" | custom-call | bytes 3600000 | tf_op jit(solution)/shard_map/inner_forces/pallas_call | solution.py:512
  18.4 0.3 %collective-permute-done.5.refs_1_ = f32[4,128]{1,0:T(4,128)S(1)} collective-permute-done((f32[4,128]{1,0:T(4,128)S(1)}, f32[4,128]{1,0:T(4,128)S(1)}, u32[]{:S(2)}, u32[]{:S(2)}) %collective-permute-start.5) | collective-permute-done | bytes 2080 | tf_op jit(solution)/shard_map/ppermute | solution.py:671
  18.7 0.0 copy-start.1
  18.7 0.1 collective-permute-start.8
  18.8 2.6 %collective-permute-start.7 = (f32[16,128]{1,0:T(8,128)S(1)}, f32[16,128]{1,0:T(8,128)S(1)}, u32[]{:S(2)}, u32[]{:S(2)}) collective-permute-start(f32[16,128]{1,0:T(8,128)S(1)} %combine.1.refs_0_), channel_id=1, source_target_pairs={{0,8},{4,12},{8,0},{12,4},{1,9},{5,13},{9,1},{13,5},{2,10},{6,14},... | collective-permute-start | bytes 24584 | tf_op jit(solution)/shard_map/ppermute | solution.py:699
  21.4 1.6 %collective-permute-start.6 = (f32[16,128]{1,0:T(8,128)S(1)}, f32[16,128]{1,0:T(8,128)S(1)}, u32[]{:S(2)}, u32[]{:S(2)}) collective-permute-start(f32[16,128]{1,0:T(8,128)S(1)} %combine.1.refs_0_), channel_id=1, source_target_pairs={{0,12},{4,0},{8,4},{12,8},{1,13},{5,1},{9,5},{13,9},{2,14},{6,2},{... | collective-permute-start | bytes 24584 | tf_op jit(solution)/shard_map/ppermute | solution.py:699
  23.0 0.0 copy-done.1
  23.0 1.3 %collective-permute-done.8.refs_3_ = f32[16,128]{1,0:T(8,128)S(1)} collective-permute-done((f32[16,128]{1,0:T(8,128)S(1)}, f32[16,128]{1,0:T(8,128)S(1)}, u32[]{:S(2)}, u32[]{:S(2)}) %collective-permute-start.8) | collective-permute-done | bytes 8224 | tf_op jit(solution)/shard_map/ppermute | solution.py:699
  24.2 0.0 collective-permute-done.7.refs_2_
  24.2 0.8 %collective-permute-done.6.refs_1_ = f32[16,128]{1,0:T(8,128)S(1)} collective-permute-done((f32[16,128]{1,0:T(8,128)S(1)}, f32[16,128]{1,0:T(8,128)S(1)}, u32[]{:S(2)}, u32[]{:S(2)}) %collective-permute-start.6) | collective-permute-done | bytes 8224 | tf_op jit(solution)/shard_map/ppermute | solution.py:699
  25.0 0.6 %expand.1 = (f32[24,128]{1,0:T(8,128)}, f32[24,128]{1,0:T(8,128)}) custom-call(f32[16,128]{1,0:T(8,128)S(1)} %combine.1.refs_0_, f32[16,128]{1,0:T(8,128)S(1)} %collective-permute-done.6.refs_1_, f32[16,128]{1,0:T(8,128)S(1)} %collective-permute-done.7.refs_2_, f32[16,128]{1,0:T(8,128)S(1)} %collective-permute-done.8.refs_3_, ...), custom_call_target="tpu_custom_call" | custom-call | bytes 2400000 | tf_op jit(solution)/shard_map/expand/pallas_call | solution.py:658
  (3 shorter events, 0.1 us)
Async XLA Ops:
  0.6 7.3 %collective-permute-start.2 = (f32[24,128]{1,0:T(8,128)}, f32[24,128]{1,0:T(8,128)S(1)}, u32[]{:S(2)}, u32[]{:S(2)}) collective-permute-start(f32[24,128]{1,0:T(8,128)} %bitcast.25), channel_id=1, source_target_pairs={{0,8},{4,12},{8,0},{12,4},{1,9},{5,13},{9,1},{13,5},{2,10},{6,14},... | collective-permute-start | bytes 36872 | tf_op jit(solution)/shard_map/ppermute | solution.py:699
  4.7 5.7 %collective-permute-start.1 = (f32[24,128]{1,0:T(8,128)}, f32[24,128]{1,0:T(8,128)S(1)}, u32[]{:S(2)}, u32[]{:S(2)}) collective-permute-start(f32[24,128]{1,0:T(8,128)} %bitcast.26), channel_id=1, source_target_pairs={{0,12},{4,8},{8,4},{12,0},{1,13},{5,9},{9,5},{13,1},{2,14},{6,10},... | collective-permute-start | bytes 36872 | tf_op jit(solution)/shard_map/ppermute | solution.py:699
  6.1 4.4 %collective-permute-start = (f32[24,128]{1,0:T(8,128)}, f32[24,128]{1,0:T(8,128)S(1)}, u32[]{:S(2)}, u32[]{:S(2)}) collective-permute-start(f32[24,128]{1,0:T(8,128)} %bitcast.27), channel_id=1, source_target_pairs={{0,4},{4,0},{8,12},{12,8},{1,5},{5,1},{9,13},{13,9},{2,6},{6,2},{1... | collective-permute-start | bytes 36872 | tf_op jit(solution)/shard_map/ppermute | solution.py:699
  6.3 4.1 %copy-start = (f32[2,3,512]{2,0,1:T(2,128)S(1)}, f32[2,3,512]{2,0,1:T(2,128)}, u32[]{:S(2)}) copy-start(f32[2,3,512]{2,0,1:T(2,128)} %param.11) | copy-start | bytes 36868
  10.5 3.4 %collective-permute-start.3 = (f32[40,128]{1,0:T(8,128)S(1)}, f32[40,128]{1,0:T(8,128)S(1)}, u32[]{:S(2)}, u32[]{:S(2)}) collective-permute-start(f32[40,128]{1,0:T(8,128)S(1)} %get-tuple-element.26), channel_id=1, source_target_pairs={{0,3},{1,2},{2,1},{3,0},{4,7},{5,6},{6,5},{7,4},{8,11},{9,10},{10,... | collective-permute-start | bytes 61448 | tf_op jit(solution)/shard_map/ppermute | solution.py:677
  10.6 3.0 %collective-permute-start.4 = (f32[4,128]{1,0:T(4,128)S(1)}, f32[4,128]{1,0:T(4,128)S(1)}, u32[]{:S(2)}, u32[]{:S(2)}) collective-permute-start(f32[4,128]{1,0:T(4,128)S(1)} %get-tuple-element.27), channel_id=1, source_target_pairs={{0,1},{1,0},{2,3},{3,2},{4,5},{5,4},{6,7},{7,6},{8,9},{9,8},{10,11... | collective-permute-start | bytes 6152 | tf_op jit(solution)/shard_map/ppermute | solution.py:671
  17.5 1.2 %collective-permute-start.5 = (f32[4,128]{1,0:T(4,128)S(1)}, f32[4,128]{1,0:T(4,128)S(1)}, u32[]{:S(2)}, u32[]{:S(2)}) collective-permute-start(f32[4,128]{1,0:T(4,128)S(1)} %get-tuple-element.41), channel_id=1, source_target_pairs={{0,1},{1,0},{2,3},{3,2},{4,5},{5,4},{6,7},{7,6},{8,9},{9,8},{10,11... | collective-permute-start | bytes 6152 | tf_op jit(solution)/shard_map/ppermute | solution.py:671
  18.7 4.2 %copy-start.1 = (f32[2,3,512]{2,0,1:T(2,128)S(1)}, f32[2,3,512]{2,0,1:T(2,128)}, u32[]{:S(2)}) copy-start(f32[2,3,512]{2,0,1:T(2,128)} %param.12) | copy-start | bytes 36868
  18.7 5.5 %collective-permute-start.8 = (f32[16,128]{1,0:T(8,128)S(1)}, f32[16,128]{1,0:T(8,128)S(1)}, u32[]{:S(2)}, u32[]{:S(2)}) collective-permute-start(f32[16,128]{1,0:T(8,128)S(1)} %combine.1.refs_0_), channel_id=1, source_target_pairs={{0,4},{4,8},{8,12},{12,0},{1,5},{5,9},{9,13},{13,1},{2,6},{6,10},{... | collective-permute-start | bytes 24584 | tf_op jit(solution)/shard_map/ppermute | solution.py:699
  18.8 5.4 %collective-permute-start.7 = (f32[16,128]{1,0:T(8,128)S(1)}, f32[16,128]{1,0:T(8,128)S(1)}, u32[]{:S(2)}, u32[]{:S(2)}) collective-permute-start(f32[16,128]{1,0:T(8,128)S(1)} %combine.1.refs_0_), channel_id=1, source_target_pairs={{0,8},{4,12},{8,0},{12,4},{1,9},{5,13},{9,1},{13,5},{2,10},{6,14},... | collective-permute-start | bytes 24584 | tf_op jit(solution)/shard_map/ppermute | solution.py:699
  21.4 3.7 %collective-permute-start.6 = (f32[16,128]{1,0:T(8,128)S(1)}, f32[16,128]{1,0:T(8,128)S(1)}, u32[]{:S(2)}, u32[]{:S(2)}) collective-permute-start(f32[16,128]{1,0:T(8,128)S(1)} %combine.1.refs_0_), channel_id=1, source_target_pairs={{0,12},{4,0},{8,4},{12,8},{1,13},{5,1},{9,5},{13,9},{2,14},{6,2},{... | collective-permute-start | bytes 24584 | tf_op jit(solution)/shard_map/ppermute | solution.py:699

commit v6 on v5

--- a/solution.py
+++ b/solution.py
@@ -236,35 +236,57 @@
     return dot(jnp.concatenate([high, high, low], axis=1), right)
 
 
-def forward(lefts, pairs, wout):
+def act(x):
+    sig = 0.5 + 0.5 * jnp.tanh(0.5 * x)
+    value = x * sig
+    return value, sig + value * (1.0 - sig)
+
+
+def forward_layers(pairs, wout):
     t1, t2, t3 = pairs
     chan = t1.shape[0] // 3
     first = jnp.concatenate([t1[0 : 2 * chan, :], t1[0:chan, :], t1[2 * chan :, :]], axis=0)
 
-    def act(x):
-        sig = 0.5 + 0.5 * jnp.tanh(0.5 * x)
-        value = x * sig
-        return value, sig + value * (1.0 - sig)
-
-    one = [act(dot(left, first)) for left in lefts]
-    two = [act(dense(h, t2)) for h, _ in one]
-    three = [wout[0:1, :] * act(dense(h, t3))[1] for h, _ in two]
-    return [(s1, s2, g3) for (_, s1), (_, s2), g3 in zip(one, two, three, strict=True)]
-
-
-def backward(states, pairs):
+    def one(left):
+        return act(dot(left, first))
+
+    def two(state):
+        value, s1 = state
+        return act(dense(value, t2)), s1
+
+    def three(state):
+        (value, s2), s1 = state
+        return s1, s2, wout[0:1, :] * act(dense(value, t3))[1]
+
+    return one, two, three
+
+
+def backward_layers(pairs):
     t1, l2, l3 = pairs
     chan = t1.shape[0] // 3
-    back = [dense(g3, l3) * s2 for _, s2, g3 in states]
-    back = [dense(g, l2) * s1 for g, (s1, _, _) in zip(back, states, strict=True)]
-    last = jnp.concatenate(
-        [t1[0:chan, :], t1[chan : 2 * chan, :], t1[0:chan, :]], axis=1
-    )
-    grads = []
-    for g in back:
-        high, low = split2(g)
-        grads.append(dot_nt(last, jnp.concatenate([high, high, low], axis=1)))
-    return grads
+
+    def three(state):
+        s1, s2, grad = state
+        return s1, dense(grad, l3) * s2
+
+    def two(state):
+        s1, grad = state
+        return dense(grad, l2) * s1
+
+    def one(grad):
+        high, low = split2(grad)
+        last = [t1[0:chan, :], t1[chan : 2 * chan, :], t1[0:chan, :]]
+        return dot_nt(
+            jnp.concatenate(last, axis=1), jnp.concatenate([high, high, low], axis=1)
+        )
+
+    return three, two, one
+
+
+def through(layers, states):
+    for layer in layers:
+        states = [layer(state) for state in states]
+    return states
 
 
 def slot_slopes(grad, kind, rates, rad, slope):
@@ -356,7 +378,8 @@
         describe(kind.at[i], dist.at[i], rates, rad.at[i], desc.at[i])
         row = 4 * (i + 1) + 3
         lefts.append(left_factor(desc.at[i], own[row : row + 1, :]))
-    for i, values in enumerate(forward(lefts, (t1, t2, t3), wout)):
+    states = through(forward_layers((t1, t2, t3), wout), lefts)
+    for i, values in enumerate(states):
         for j, value in enumerate(values):
             state[i, j] = value
 
@@ -426,17 +449,20 @@
         pulled[...] = jnp.zeros_like(pulled)
     else:
         places[...] = blocks[0][...]
-    lefts = []
-    for i, (word, rows, g, _) in enumerate(stages):
+    def describe_group(i):
+        word, rows, g, _ = stages[i]
         neighbours(rows, word, g, off.at[i], kind.at[i], dist.at[i])
         describe(kind.at[i], dist.at[i], rates, rad.at[i], desc.at[i])
         row = 4 * (g + 1) + 3
-        lefts.append(left_factor(desc.at[i], rows[row : row + 1, :]))
+        return left_factor(desc.at[i], rows[row : row + 1, :])
+
     t1, t2, t3, l2, l3 = pairs
-    states = forward(lefts, (t1, t2, t3), wout)
+    layers = forward_layers((t1, t2, t3), wout)
+    states = through(layers, [describe_group(i) for i in range(len(stages))])
+    layers = backward_layers((t1, l2, l3))
     if inner:
         states += [[state_inner[i, j] for j in range(3)] for i in range(inner)]
-    slopes = backward(states, (t1, l2, l3))
+    slopes = through(layers, states)
     for i in range(len(stages)):
         grad[i] = slopes[i]
     for i in range(len(stages), len(slopes)):
@@ -487,8 +513,8 @@
             pltpu.VMEM((count, chan, LANES), f32),
             pltpu.VMEM((count, 6, slots, LANES), f32),
             pltpu.VMEM((count, 2, slots, LANES), jnp.float32),
-            pltpu.VMEM((12, LANES), f32),
-            pltpu.VMEM((12, LANES), f32),
+            pltpu.VMEM((16, LANES), f32),
+            pltpu.VMEM((16, LANES), f32),
         ],
         compiler_params=PARAMS,
         cost_estimate=cost(3.0),
@@ -565,15 +591,20 @@
     blocks, species, code = arranged(GATHER, refs), refs[NC], refs[NC + 1]
     out, to_inner, to_outer = refs[NC + 2 :]
     tiles = species.shape[0]
-    for c in range(3):
-        total = None
-        for r in range(NC):
-            for j in range(beads):
-                rows = pl.ds(c * tiles * beads + j, tiles, stride=beads)
-                term = share(GATHER, r, table[r, j], table[-r % NC, j]) * blocks[r][rows, :]
-                total = term if total is None else total + term
-        out[pl.ds(c, tiles, stride=4), :] = total
-    out[pl.ds(3, tiles, stride=4), :] = species[...]
+    weights = [
+        [share(GATHER, r, table[r, j], table[-r % NC, j]) for j in range(beads)]
+        for r in range(NC)
+    ]
+    for t in range(tiles):
+        for c in range(3):
+            total = None
+            for r in range(NC):
+                for j in range(beads):
+                    row = (c * tiles + t) * beads + j
+                    term = weights[r][j] * blocks[r][row : row + 1, :]
+                    total = term if total is None else total + term
+            out[4 * t + c : 4 * t + c + 1, :] = total
+        out[4 * t + 3 : 4 * t + 4, :] = species[t : t + 1, :]
     even = at_even("space")
     last = code.shape[1] - LANES
     to_inner[...] = jnp.where(even, out[4 * tiles - 4 :, :], out[0:4, :])
@@ -605,22 +636,26 @@
     tiles = species.shape[0]
     pull = TIME_STEP * SPRING_RATE * masses_of(species[...])
 
-    def row(ref, c, j):
-        return ref[pl.ds(c * tiles * beads + j, tiles, stride=beads), :]
-
-    def side(c, j, ref, other):
+    def side(row, ref, other):
+        taken = ref[row : row + 1, :]
         if GATHER[0] == "turn":
-            return row(ref, c, j)
-        return jnp.where(at_even("bead"), row(other, c, j), row(ref, c, j))
-
-    for c in range(3):
-        for j in range(beads):
-            below = row(own, c, j - 1) if j else side(c, beads - 1, before, after)
-            above = row(own, c, j + 1) if j + 1 < beads else side(c, 0, after, before)
-            laplace = 2.0 * row(own, c, j) - below - above
-            out[pl.ds(c * tiles * beads + j, tiles, stride=beads), :] = (
-                row(momenta, c, j) - pull * laplace
-            )
+            return taken
+        return jnp.where(at_even("bead"), other[row : row + 1, :], taken)
+
+    for m in range(3 * tiles):
+        t, first, last = m % tiles, m * beads, m * beads + beads - 1
+        for row in range(first, last + 1):
+            here = own[row : row + 1, :]
+            if row > first:
+                below = own[row - 1 : row, :]
+            else:
+                below = side(last, before, after)
+            if row < last:
+                above = own[row + 1 : row + 2, :]
+            else:
+                above = side(first, after, before)
+            laplace = 2.0 * here - below - above
+            out[row : row + 1, :] = momenta[row : row + 1, :] - pull[t : t + 1, :] * laplace
 
 
 def spring_kick(beads, own, before, after, momenta, species):
@@ -640,17 +675,24 @@
     momenta, displacement = refs[NC + 2 :]
     tiles = species.shape[0]
     scale = TIME_STEP * beads * NC / NC
+    weights = [
+        [
+            share(SPREAD, r, scale * table[-r % NC, j], scale * table[r, j])
+            for j in range(beads)
+        ]
+        for r in range(NC)
+    ]
     drift = per_species(species[...], [TIME_STEP / m for m in MASS_TABLE])
     for c in range(3):
-        pulls = [force[pl.ds(c, tiles, stride=4), :] for force in forces]
-        for j in range(beads):
-            rows = pl.ds(c * tiles * beads + j, tiles, stride=beads)
-            total = kicked[rows, :]
-            for r in range(NC):
-                weight = share(SPREAD, r, scale * table[-r % NC, j], scale * table[r, j])
-                total = total + weight * pulls[r]
-            momenta[rows, :] = total
-            displacement[rows, :] = drift * total
+        for t in range(tiles):
+            pulls = [force[4 * t + c : 4 * t + c + 1, :] for force in forces]
+            for j in range(beads):
+                row = (c * tiles + t) * beads + j
+                total = kicked[row : row + 1, :]
+                for r in range(NC):
+                    total = total + weights[r][j] * pulls[r]
+                momenta[row : row + 1, :] = total
+                displacement[row : row + 1, :] = drift[t : t + 1, :] * total
 
 
 def expand(table, beads, forces, kicked, species):

time: 25.8 us -> 25.8 us (level)
  no operation moved by 1% of the time
where the time goes in v6:
time: 25.8 us; the launch traced here: 25.7 us
  starting transfers between devices  11.7 us (45%)
  Pallas kernels  8.01 us (31%)
  waiting for transfers between devices  5.23 us (20%)
  between operations  0.71 us (3%)
    ppermute x6, starting transfers between devices, around(): blocks.append(lax.ppermute(block, 'bead', pairs))  9.89 us
    ppermute x6, waiting for transfers between devices, around(): blocks.append(lax.ppermute(block, 'bead', pairs))  4.54 us
    pallas_call x1, Pallas kernels, outer_stage(): pl.pallas_call(functools.partial(outer_kernel, direct, inner), out_shape=...  3.58 us
    ppermute x2, starting transfers between devices, swap_inner(): return lax.ppermute(block, 'space', [(i, i ^ 1) for i in range(count)])  1.77 us
    pallas_call x1, Pallas kernels, prepare(): pl.pallas_call(functools.partial(prepare_kernel, slab_atoms, block_start)...  1.59 us
    pallas_call x1, Pallas kernels, inner_stage(): pl.pallas_call(inner_kernel, out_shape=out_shape, in_specs=[VMEM] * 7, ou...  1.38 us
    pallas_call x1, Pallas kernels, inner_forces(): pl.pallas_call(inner_force_kernel, out_shape=pltpu.VMEM((block // LANES *...  0.72 us
    pallas_call x1, Pallas kernels, expand(): pl.pallas_call(functools.partial(expand_kernel, table, beads), out_shape=...  0.64 us
  transfers between devices with their start and end apart: 9, of which 5 were waited for; matrix products, arithmetic and copies ran while one was open for 0% of the time, Pallas kernels for 14%

profile of v6, /device:TPU:0, one launch (start us, length us, event | category | flops | bytes accessed | tf_op | source)
XLA Modules:
  0.0 25.7 jit_solution(1470696150639689516)
XLA Ops:
  0.6 4.1 %collective-permute-start.2 = (f32[24,128]{1,0:T(8,128)}, f32[24,128]{1,0:T(8,128)S(1)}, u32[]{:S(2)}, u32[]{:S(2)}) collective-permute-start(f32[24,128]{1,0:T(8,128)} %bitcast.25), channel_id=1, source_target_pairs={{0,8},{4,12},{8,0},{12,4},{1,9},{5,13},{9,1},{13,5},{2,10},{6,14},... | collective-permute-start | bytes 36872 | tf_op jit(solution)/shard_map/ppermute | solution.py:741
  4.7 1.3 %collective-permute-start.1 = (f32[24,128]{1,0:T(8,128)}, f32[24,128]{1,0:T(8,128)S(1)}, u32[]{:S(2)}, u32[]{:S(2)}) collective-permute-start(f32[24,128]{1,0:T(8,128)} %bitcast.26), channel_id=1, source_target_pairs={{0,12},{4,8},{8,4},{12,0},{1,13},{5,9},{9,5},{13,1},{2,14},{6,10},... | collective-permute-start | bytes 36872 | tf_op jit(solution)/shard_map/ppermute | solution.py:741
  6.1 0.2 collective-permute-start
  6.3 0.0 copy-start
  6.3 1.6 %prepare.1 = (s32[32,512]{1,0:T(8,128)S(1)}, f32[4,128]{1,0:T(4,128)S(1)}, bf16[384,256]{1,0:T(8,128)(2,1)S(1)}, bf16[512,256]{1,0:T(8,128)(2,1)S(1)}, bf16[512,...) custom-call(s32[32,512]{1,0:T(8,128)} %refs_0_.1, ...), custom_call_target="tpu_custom_call" | custom-call | bytes 3600000 | tf_op jit(solution)/shard_map/prepare/pallas_call | solution.py:156
  7.9 0.0 collective-permute-done.2.refs_3_
  7.9 2.5 %collective-permute-done.1.refs_2_.after = f32[24,128]{1,0:T(8,128)S(1)} collective-permute-done((f32[24,128]{1,0:T(8,128)}, f32[24,128]{1,0:T(8,128)S(1)}, u32[]{:S(2)}, u32[]{:S(2)}) %collective-permute-start.1) | collective-permute-done | bytes 12320 | tf_op jit(solution)/shard_map/ppermute | solution.py:741
  10.4 0.0 collective-permute-done.refs_1_.before
  10.4 0.0 copy-done
  10.4 0.1 contract.1
  10.5 0.1 collective-permute-start.3
  10.6 1.6 %collective-permute-start.4 = (f32[4,128]{1,0:T(4,128)S(1)}, f32[4,128]{1,0:T(4,128)S(1)}, u32[]{:S(2)}, u32[]{:S(2)}) collective-permute-start(f32[4,128]{1,0:T(4,128)S(1)} %get-tuple-element.27), channel_id=1, source_target_pairs={{0,1},{1,0},{2,3},{3,2},{4,5},{5,4},{6,7},{7,6},{8,9},{9,8},{10,11... | collective-permute-start | bytes 6152 | tf_op jit(solution)/shard_map/ppermute | solution.py:713
  12.2 1.4 %inner_forward.1 = (f32[2,3,32,128]{3,2,1,0:T(8,128)S(1)}, f32[2,32,128]{2,1,0:T(8,128)S(1)}, f32[2,1024,128]{2,1,0:T(8,128)S(1)}, f32[2,3,128,256]{3,2,1,0:T(8,128)S(1)}) custom-call(f32[16,128]{1,0:T(8,128)S(1)} %get-tuple-element.25.own.refs_0_, s32[32,512]{1,0:T(8,128)S(1)} %get-tuple-element.24.refs_5_.code.refs_3_, ...), custom_call_target="tpu_custom_call" | custom-call | bytes 3000000 | tf_op jit(solution)/shard_map/inner_forward/pallas_call | solution.py:397
  13.6 0.0 collective-permute-done.4.refs_2_
  13.6 0.4 %collective-permute-done.3.refs_1_ = f32[40,128]{1,0:T(8,128)S(1)} collective-permute-done((f32[40,128]{1,0:T(8,128)S(1)}, f32[40,128]{1,0:T(8,128)S(1)}, u32[]{:S(2)}, u32[]{:S(2)}) %collective-permute-start.3) | collective-permute-done | bytes 20512 | tf_op jit(solution)/shard_map/ppermute | solution.py:719
  13.9 3.6 %outer_forces.1 = (f32[24,128]{1,0:T(8,128)S(1)}, f32[4,128]{1,0:T(4,128)S(1)}, f32[2,128,128]{2,1,0:T(8,128)S(1)}) custom-call(f32[16,128]{1,0:T(8,128)S(1)} %get-tuple-element.25.own.refs_0_, f32[40,128]{1,0:T(8,128)S(1)} %collective-permute-done.3.refs_1_, f32[4,128]{1,0:T(4,128)S(1)} %collective-permute-done.4.refs_2_, ...), custom_call_target="tpu_custom_call" | custom-call | bytes 9000000 | tf_op jit(solution)/shard_map/outer_forces/pallas_call | solution.py:501
  17.5 0.2 collective-permute-start.5
  17.7 0.7 %inner_forces.1.refs_0_ = f32[16,128]{1,0:T(8,128)S(1)} custom-call(s32[32,512]{1,0:T(8,128)S(1)} %get-tuple-element.24.refs_5_.code.refs_3_, f32[32,128]{1,0:T(8,128)S(1)} %get-tuple-element.33.rates.refs_9_, f32[2,3,32,128]{3,2,1,0:T(8,128)S(1)} %get-tuple-element.37.off, f32[2,32,128]{2,1,0:T(8,128)S(1)} %get-tuple-element.38.kind, ...), custom_call_target="tpu_custom_call" | custom-call | bytes 3600000 | tf_op jit(solution)/shard_map/inner_forces/pallas_call | solution.py:538
  18.4 0.3 %collective-permute-done.5.refs_1_ = f32[4,128]{1,0:T(4,128)S(1)} collective-permute-done((f32[4,128]{1,0:T(4,128)S(1)}, f32[4,128]{1,0:T(4,128)S(1)}, u32[]{:S(2)}, u32[]{:S(2)}) %collective-permute-start.5) | collective-permute-done | bytes 2080 | tf_op jit(solution)/shard_map/ppermute | solution.py:713
  18.8 0.0 copy-start.1
  18.8 0.1 collective-permute-start.8
  18.8 2.6 %collective-permute-start.7 = (f32[16,128]{1,0:T(8,128)S(1)}, f32[16,128]{1,0:T(8,128)S(1)}, u32[]{:S(2)}, u32[]{:S(2)}) collective-permute-start(f32[16,128]{1,0:T(8,128)S(1)} %combine.1.refs_0_), channel_id=1, source_target_pairs={{0,8},{4,12},{8,0},{12,4},{1,9},{5,13},{9,1},{13,5},{2,10},{6,14},... | collective-permute-start | bytes 24584 | tf_op jit(solution)/shard_map/ppermute | solution.py:741
  21.4 1.6 %collective-permute-start.6 = (f32[16,128]{1,0:T(8,128)S(1)}, f32[16,128]{1,0:T(8,128)S(1)}, u32[]{:S(2)}, u32[]{:S(2)}) collective-permute-start(f32[16,128]{1,0:T(8,128)S(1)} %combine.1.refs_0_), channel_id=1, source_target_pairs={{0,12},{4,0},{8,4},{12,8},{1,13},{5,1},{9,5},{13,9},{2,14},{6,2},{... | collective-permute-start | bytes 24584 | tf_op jit(solution)/shard_map/ppermute | solution.py:741
  23.0 0.0 copy-done.1
  23.0 1.2 %collective-permute-done.8.refs_3_ = f32[16,128]{1,0:T(8,128)S(1)} collective-permute-done((f32[16,128]{1,0:T(8,128)S(1)}, f32[16,128]{1,0:T(8,128)S(1)}, u32[]{:S(2)}, u32[]{:S(2)}) %collective-permute-start.8) | collective-permute-done | bytes 8224 | tf_op jit(solution)/shard_map/ppermute | solution.py:741
  24.3 0.0 collective-permute-done.7.refs_2_
  24.3 0.8 %collective-permute-done.6.refs_1_ = f32[16,128]{1,0:T(8,128)S(1)} collective-permute-done((f32[16,128]{1,0:T(8,128)S(1)}, f32[16,128]{1,0:T(8,128)S(1)}, u32[]{:S(2)}, u32[]{:S(2)}) %collective-permute-start.6) | collective-permute-done | bytes 8224 | tf_op jit(solution)/shard_map/ppermute | solution.py:741
  25.1 0.6 %expand.1 = (f32[24,128]{1,0:T(8,128)}, f32[24,128]{1,0:T(8,128)}) custom-call(f32[16,128]{1,0:T(8,128)S(1)} %combine.1.refs_0_, f32[16,128]{1,0:T(8,128)S(1)} %collective-permute-done.6.refs_1_, f32[16,128]{1,0:T(8,128)S(1)} %collective-permute-done.7.refs_2_, f32[16,128]{1,0:T(8,128)S(1)} %collective-permute-done.8.refs_3_, ...), custom_call_target="tpu_custom_call" | custom-call | bytes 2400000 | tf_op jit(solution)/shard_map/expand/pallas_call | solution.py:700
  (2 shorter events, 0.0 us)
Async XLA Ops:
  0.6 7.3 %collective-permute-start.2 = (f32[24,128]{1,0:T(8,128)}, f32[24,128]{1,0:T(8,128)S(1)}, u32[]{:S(2)}, u32[]{:S(2)}) collective-permute-start(f32[24,128]{1,0:T(8,128)} %bitcast.25), channel_id=1, source_target_pairs={{0,8},{4,12},{8,0},{12,4},{1,9},{5,13},{9,1},{13,5},{2,10},{6,14},... | collective-permute-start | bytes 36872 | tf_op jit(solution)/shard_map/ppermute | solution.py:741
  4.7 5.7 %collective-permute-start.1 = (f32[24,128]{1,0:T(8,128)}, f32[24,128]{1,0:T(8,128)S(1)}, u32[]{:S(2)}, u32[]{:S(2)}) collective-permute-start(f32[24,128]{1,0:T(8,128)} %bitcast.26), channel_id=1, source_target_pairs={{0,12},{4,8},{8,4},{12,0},{1,13},{5,9},{9,5},{13,1},{2,14},{6,10},... | collective-permute-start | bytes 36872 | tf_op jit(solution)/shard_map/ppermute | solution.py:741
  6.1 4.4 %collective-permute-start = (f32[24,128]{1,0:T(8,128)}, f32[24,128]{1,0:T(8,128)S(1)}, u32[]{:S(2)}, u32[]{:S(2)}) collective-permute-start(f32[24,128]{1,0:T(8,128)} %bitcast.27), channel_id=1, source_target_pairs={{0,4},{4,0},{8,12},{12,8},{1,5},{5,1},{9,13},{13,9},{2,6},{6,2},{1... | collective-permute-start | bytes 36872 | tf_op jit(solution)/shard_map/ppermute | solution.py:741
  6.3 4.1 %copy-start = (f32[2,3,512]{2,0,1:T(2,128)S(1)}, f32[2,3,512]{2,0,1:T(2,128)}, u32[]{:S(2)}) copy-start(f32[2,3,512]{2,0,1:T(2,128)} %param.11) | copy-start | bytes 36868
  10.5 3.4 %collective-permute-start.3 = (f32[40,128]{1,0:T(8,128)S(1)}, f32[40,128]{1,0:T(8,128)S(1)}, u32[]{:S(2)}, u32[]{:S(2)}) collective-permute-start(f32[40,128]{1,0:T(8,128)S(1)} %get-tuple-element.26), channel_id=1, source_target_pairs={{0,3},{1,2},{2,1},{3,0},{4,7},{5,6},{6,5},{7,4},{8,11},{9,10},{10,... | collective-permute-start | bytes 61448 | tf_op jit(solution)/shard_map/ppermute | solution.py:719
  10.6 3.0 %collective-permute-start.4 = (f32[4,128]{1,0:T(4,128)S(1)}, f32[4,128]{1,0:T(4,128)S(1)}, u32[]{:S(2)}, u32[]{:S(2)}) collective-permute-start(f32[4,128]{1,0:T(4,128)S(1)} %get-tuple-element.27), channel_id=1, source_target_pairs={{0,1},{1,0},{2,3},{3,2},{4,5},{5,4},{6,7},{7,6},{8,9},{9,8},{10,11... | collective-permute-start | bytes 6152 | tf_op jit(solution)/shard_map/ppermute | solution.py:713
  17.5 1.2 %collective-permute-start.5 = (f32[4,128]{1,0:T(4,128)S(1)}, f32[4,128]{1,0:T(4,128)S(1)}, u32[]{:S(2)}, u32[]{:S(2)}) collective-permute-start(f32[4,128]{1,0:T(4,128)S(1)} %get-tuple-element.41), channel_id=1, source_target_pairs={{0,1},{1,0},{2,3},{3,2},{4,5},{5,4},{6,7},{7,6},{8,9},{9,8},{10,11... | collective-permute-start | bytes 6152 | tf_op jit(solution)/shard_map/ppermute | solution.py:713
  18.8 4.2 %copy-start.1 = (f32[2,3,512]{2,0,1:T(2,128)S(1)}, f32[2,3,512]{2,0,1:T(2,128)}, u32[]{:S(2)}) copy-start(f32[2,3,512]{2,0,1:T(2,128)} %param.12) | copy-start | bytes 36868
  18.8 5.5 %collective-permute-start.8 = (f32[16,128]{1,0:T(8,128)S(1)}, f32[16,128]{1,0:T(8,128)S(1)}, u32[]{:S(2)}, u32[]{:S(2)}) collective-permute-start(f32[16,128]{1,0:T(8,128)S(1)} %combine.1.refs_0_), channel_id=1, source_target_pairs={{0,4},{4,8},{8,12},{12,0},{1,5},{5,9},{9,13},{13,1},{2,6},{6,10},{... | collective-permute-start | bytes 24584 | tf_op jit(solution)/shard_map/ppermute | solution.py:741
  18.8 5.4 %collective-permute-start.7 = (f32[16,128]{1,0:T(8,128)S(1)}, f32[16,128]{1,0:T(8,128)S(1)}, u32[]{:S(2)}, u32[]{:S(2)}) collective-permute-start(f32[16,128]{1,0:T(8,128)S(1)} %combine.1.refs_0_), channel_id=1, source_target_pairs={{0,8},{4,12},{8,0},{12,4},{1,9},{5,13},{9,1},{13,5},{2,10},{6,14},... | collective-permute-start | bytes 24584 | tf_op jit(solution)/shard_map/ppermute | solution.py:741
  21.4 3.7 %collective-permute-start.6 = (f32[16,128]{1,0:T(8,128)S(1)}, f32[16,128]{1,0:T(8,128)S(1)}, u32[]{:S(2)}, u32[]{:S(2)}) collective-permute-start(f32[16,128]{1,0:T(8,128)S(1)} %combine.1.refs_0_), channel_id=1, source_target_pairs={{0,12},{4,0},{8,4},{12,8},{1,13},{5,1},{9,5},{13,9},{2,14},{6,2},{... | collective-permute-start | bytes 24584 | tf_op jit(solution)/shard_map/ppermute | solution.py:741

commit v7 on v6

--- a/solution.py
+++ b/solution.py
@@ -42,9 +42,6 @@
 
 
 VMEM = pl.BlockSpec(memory_space=pltpu.VMEM)
-SMEM = pl.BlockSpec(memory_space=pltpu.SMEM)
-
-
 PARAMS = pltpu.CompilerParams(vmem_limit_bytes=16 * 1024 * 1024)
 
 
@@ -212,7 +209,7 @@
             first = n * rate_count + 8 * o
             rad[first : first + 8, :] = radial
             for s in range(SPECIES):
-                acc[s][o] = acc[s][o] + jnp.where(masks[s], radial, 0.0)
+                acc[s][o] = jnp.where(masks[s], acc[s][o] + radial, acc[s][o])
     for s in range(SPECIES):
         for o in range(octets):
             first = s * rate_count + 8 * o

time: 25.8 us -> 25.8 us (level)
  transfers between devices with their start and end apart: 9 -> 9, of which waited for: 5 -> 5; matrix products, arithmetic and copies ran while one was open for 0% -> 0% of each run, Pallas kernels for 14% -> 15%
where the time goes in v7:
time: 25.8 us; the launch traced here: 25.6 us
  starting transfers between devices  11.7 us (45%)
  Pallas kernels  7.94 us (31%)
  waiting for transfers between devices  5.24 us (20%)
  between operations  0.71 us (3%)
    ppermute x6, starting transfers between devices, around(): blocks.append(lax.ppermute(block, 'bead', pairs))  9.88 us
    ppermute x6, waiting for transfers between devices, around(): blocks.append(lax.ppermute(block, 'bead', pairs))  4.54 us
    pallas_call x1, Pallas kernels, outer_stage(): pl.pallas_call(functools.partial(outer_kernel, direct, inner), out_shape=...  3.51 us
    ppermute x2, starting transfers between devices, swap_inner(): return lax.ppermute(block, 'space', [(i, i ^ 1) for i in range(count)])  1.77 us
    pallas_call x1, Pallas kernels, prepare(): pl.pallas_call(functools.partial(prepare_kernel, slab_atoms, block_start)...  1.59 us
    pallas_call x1, Pallas kernels, inner_stage(): pl.pallas_call(inner_kernel, out_shape=out_shape, in_specs=[VMEM] * 7, ou...  1.37 us
    pallas_call x1, Pallas kernels, inner_forces(): pl.pallas_call(inner_force_kernel, out_shape=pltpu.VMEM((block // LANES *...  0.72 us
    pallas_call x1, Pallas kernels, expand(): pl.pallas_call(functools.partial(expand_kernel, table, beads), out_shape=...  0.64 us
  transfers between devices with their start and end apart: 9, of which 5 were waited for; matrix products, arithmetic and copies ran while one was open for 0% of the time, Pallas kernels for 15%

profile of v7, /device:TPU:0, one launch (start us, length us, event | category | flops | bytes accessed | tf_op | source)
XLA Modules:
  0.0 25.6 jit_solution(4866490332576734133)
XLA Ops:
  0.6 4.1 %collective-permute-start.2 = (f32[24,128]{1,0:T(8,128)}, f32[24,128]{1,0:T(8,128)S(1)}, u32[]{:S(2)}, u32[]{:S(2)}) collective-permute-start(f32[24,128]{1,0:T(8,128)} %bitcast.25), channel_id=1, source_target_pairs={{0,8},{4,12},{8,0},{12,4},{1,9},{5,13},{9,1},{13,5},{2,10},{6,14},... | collective-permute-start | bytes 36872 | tf_op jit(solution)/shard_map/ppermute | solution.py:738
  4.7 1.3 %collective-permute-start.1 = (f32[24,128]{1,0:T(8,128)}, f32[24,128]{1,0:T(8,128)S(1)}, u32[]{:S(2)}, u32[]{:S(2)}) collective-permute-start(f32[24,128]{1,0:T(8,128)} %bitcast.26), channel_id=1, source_target_pairs={{0,12},{4,8},{8,4},{12,0},{1,13},{5,9},{9,5},{13,1},{2,14},{6,10},... | collective-permute-start | bytes 36872 | tf_op jit(solution)/shard_map/ppermute | solution.py:738
  6.1 0.2 collective-permute-start
  6.3 0.0 copy-start
  6.3 1.6 %prepare.1 = (s32[32,512]{1,0:T(8,128)S(1)}, f32[4,128]{1,0:T(4,128)S(1)}, bf16[384,256]{1,0:T(8,128)(2,1)S(1)}, bf16[512,256]{1,0:T(8,128)(2,1)S(1)}, bf16[512,...) custom-call(s32[32,512]{1,0:T(8,128)} %refs_0_.1, ...), custom_call_target="tpu_custom_call" | custom-call | bytes 3600000 | tf_op jit(solution)/shard_map/prepare/pallas_call | solution.py:153
  7.9 0.0 collective-permute-done.2.refs_3_
  7.9 2.5 %collective-permute-done.1.refs_2_.after = f32[24,128]{1,0:T(8,128)S(1)} collective-permute-done((f32[24,128]{1,0:T(8,128)}, f32[24,128]{1,0:T(8,128)S(1)}, u32[]{:S(2)}, u32[]{:S(2)}) %collective-permute-start.1) | collective-permute-done | bytes 12320 | tf_op jit(solution)/shard_map/ppermute | solution.py:738
  10.4 0.0 collective-permute-done.refs_1_.before
  10.4 0.0 copy-done
  10.4 0.1 contract.1
  10.5 0.1 collective-permute-start.3
  10.6 1.6 %collective-permute-start.4 = (f32[4,128]{1,0:T(4,128)S(1)}, f32[4,128]{1,0:T(4,128)S(1)}, u32[]{:S(2)}, u32[]{:S(2)}) collective-permute-start(f32[4,128]{1,0:T(4,128)S(1)} %get-tuple-element.27), channel_id=1, source_target_pairs={{0,1},{1,0},{2,3},{3,2},{4,5},{5,4},{6,7},{7,6},{8,9},{9,8},{10,11... | collective-permute-start | bytes 6152 | tf_op jit(solution)/shard_map/ppermute | solution.py:710
  12.2 1.4 %inner_forward.1 = (f32[2,3,32,128]{3,2,1,0:T(8,128)S(1)}, f32[2,32,128]{2,1,0:T(8,128)S(1)}, f32[2,1024,128]{2,1,0:T(8,128)S(1)}, f32[2,3,128,256]{3,2,1,0:T(8,128)S(1)}) custom-call(f32[16,128]{1,0:T(8,128)S(1)} %get-tuple-element.25.own.refs_0_, s32[32,512]{1,0:T(8,128)S(1)} %get-tuple-element.24.refs_5_.code.refs_3_, ...), custom_call_target="tpu_custom_call" | custom-call | bytes 3000000 | tf_op jit(solution)/shard_map/inner_forward/pallas_call | solution.py:394
  13.6 0.0 collective-permute-done.4.refs_2_
  13.6 0.4 %collective-permute-done.3.refs_1_ = f32[40,128]{1,0:T(8,128)S(1)} collective-permute-done((f32[40,128]{1,0:T(8,128)S(1)}, f32[40,128]{1,0:T(8,128)S(1)}, u32[]{:S(2)}, u32[]{:S(2)}) %collective-permute-start.3) | collective-permute-done | bytes 20512 | tf_op jit(solution)/shard_map/ppermute | solution.py:716
  13.9 3.5 %outer_forces.1 = (f32[24,128]{1,0:T(8,128)S(1)}, f32[4,128]{1,0:T(4,128)S(1)}, f32[2,128,128]{2,1,0:T(8,128)S(1)}) custom-call(f32[16,128]{1,0:T(8,128)S(1)} %get-tuple-element.25.own.refs_0_, f32[40,128]{1,0:T(8,128)S(1)} %collective-permute-done.3.refs_1_, f32[4,128]{1,0:T(4,128)S(1)} %collective-permute-done.4.refs_2_, ...), custom_call_target="tpu_custom_call" | custom-call | bytes 9000000 | tf_op jit(solution)/shard_map/outer_forces/pallas_call | solution.py:498
  17.5 0.2 collective-permute-start.5
  17.6 0.7 %inner_forces.1.refs_0_ = f32[16,128]{1,0:T(8,128)S(1)} custom-call(s32[32,512]{1,0:T(8,128)S(1)} %get-tuple-element.24.refs_5_.code.refs_3_, f32[32,128]{1,0:T(8,128)S(1)} %get-tuple-element.33.rates.refs_9_, f32[2,3,32,128]{3,2,1,0:T(8,128)S(1)} %get-tuple-element.37.off, f32[2,32,128]{2,1,0:T(8,128)S(1)} %get-tuple-element.38.kind, ...), custom_call_target="tpu_custom_call" | custom-call | bytes 3600000 | tf_op jit(solution)/shard_map/inner_forces/pallas_call | solution.py:535
  18.4 0.3 %collective-permute-done.5.refs_1_ = f32[4,128]{1,0:T(4,128)S(1)} collective-permute-done((f32[4,128]{1,0:T(4,128)S(1)}, f32[4,128]{1,0:T(4,128)S(1)}, u32[]{:S(2)}, u32[]{:S(2)}) %collective-permute-start.5) | collective-permute-done | bytes 2080 | tf_op jit(solution)/shard_map/ppermute | solution.py:710
  18.7 0.0 copy-start.1
  18.7 0.1 collective-permute-start.8
  18.8 2.6 %collective-permute-start.7 = (f32[16,128]{1,0:T(8,128)S(1)}, f32[16,128]{1,0:T(8,128)S(1)}, u32[]{:S(2)}, u32[]{:S(2)}) collective-permute-start(f32[16,128]{1,0:T(8,128)S(1)} %combine.1.refs_0_), channel_id=1, source_target_pairs={{0,8},{4,12},{8,0},{12,4},{1,9},{5,13},{9,1},{13,5},{2,10},{6,14},... | collective-permute-start | bytes 24584 | tf_op jit(solution)/shard_map/ppermute | solution.py:738
  21.3 1.6 %collective-permute-start.6 = (f32[16,128]{1,0:T(8,128)S(1)}, f32[16,128]{1,0:T(8,128)S(1)}, u32[]{:S(2)}, u32[]{:S(2)}) collective-permute-start(f32[16,128]{1,0:T(8,128)S(1)} %combine.1.refs_0_), channel_id=1, source_target_pairs={{0,12},{4,0},{8,4},{12,8},{1,13},{5,1},{9,5},{13,9},{2,14},{6,2},{... | collective-permute-start | bytes 24584 | tf_op jit(solution)/shard_map/ppermute | solution.py:738
  22.9 0.0 copy-done.1
  22.9 1.2 %collective-permute-done.8.refs_3_ = f32[16,128]{1,0:T(8,128)S(1)} collective-permute-done((f32[16,128]{1,0:T(8,128)S(1)}, f32[16,128]{1,0:T(8,128)S(1)}, u32[]{:S(2)}, u32[]{:S(2)}) %collective-permute-start.8) | collective-permute-done | bytes 8224 | tf_op jit(solution)/shard_map/ppermute | solution.py:738
  24.2 0.0 collective-permute-done.7.refs_2_
  24.2 0.8 %collective-permute-done.6.refs_1_ = f32[16,128]{1,0:T(8,128)S(1)} collective-permute-done((f32[16,128]{1,0:T(8,128)S(1)}, f32[16,128]{1,0:T(8,128)S(1)}, u32[]{:S(2)}, u32[]{:S(2)}) %collective-permute-start.6) | collective-permute-done | bytes 8224 | tf_op jit(solution)/shard_map/ppermute | solution.py:738
  25.0 0.6 %expand.1 = (f32[24,128]{1,0:T(8,128)}, f32[24,128]{1,0:T(8,128)}) custom-call(f32[16,128]{1,0:T(8,128)S(1)} %combine.1.refs_0_, f32[16,128]{1,0:T(8,128)S(1)} %collective-permute-done.6.refs_1_, f32[16,128]{1,0:T(8,128)S(1)} %collective-permute-done.7.refs_2_, f32[16,128]{1,0:T(8,128)S(1)} %collective-permute-done.8.refs_3_, ...), custom_call_target="tpu_custom_call" | custom-call | bytes 2400000 | tf_op jit(solution)/shard_map/expand/pallas_call | solution.py:697
  (2 shorter events, 0.0 us)
Async XLA Ops:
  0.6 7.3 %collective-permute-start.2 = (f32[24,128]{1,0:T(8,128)}, f32[24,128]{1,0:T(8,128)S(1)}, u32[]{:S(2)}, u32[]{:S(2)}) collective-permute-start(f32[24,128]{1,0:T(8,128)} %bitcast.25), channel_id=1, source_target_pairs={{0,8},{4,12},{8,0},{12,4},{1,9},{5,13},{9,1},{13,5},{2,10},{6,14},... | collective-permute-start | bytes 36872 | tf_op jit(solution)/shard_map/ppermute | solution.py:738
  4.7 5.7 %collective-permute-start.1 = (f32[24,128]{1,0:T(8,128)}, f32[24,128]{1,0:T(8,128)S(1)}, u32[]{:S(2)}, u32[]{:S(2)}) collective-permute-start(f32[24,128]{1,0:T(8,128)} %bitcast.26), channel_id=1, source_target_pairs={{0,12},{4,8},{8,4},{12,0},{1,13},{5,9},{9,5},{13,1},{2,14},{6,10},... | collective-permute-start | bytes 36872 | tf_op jit(solution)/shard_map/ppermute | solution.py:738
  6.1 4.4 %collective-permute-start = (f32[24,128]{1,0:T(8,128)}, f32[24,128]{1,0:T(8,128)S(1)}, u32[]{:S(2)}, u32[]{:S(2)}) collective-permute-start(f32[24,128]{1,0:T(8,128)} %bitcast.27), channel_id=1, source_target_pairs={{0,4},{4,0},{8,12},{12,8},{1,5},{5,1},{9,13},{13,9},{2,6},{6,2},{1... | collective-permute-start | bytes 36872 | tf_op jit(solution)/shard_map/ppermute | solution.py:738
  6.3 4.1 %copy-start = (f32[2,3,512]{2,0,1:T(2,128)S(1)}, f32[2,3,512]{2,0,1:T(2,128)}, u32[]{:S(2)}) copy-start(f32[2,3,512]{2,0,1:T(2,128)} %param.11) | copy-start | bytes 36868
  10.5 3.4 %collective-permute-start.3 = (f32[40,128]{1,0:T(8,128)S(1)}, f32[40,128]{1,0:T(8,128)S(1)}, u32[]{:S(2)}, u32[]{:S(2)}) collective-permute-start(f32[40,128]{1,0:T(8,128)S(1)} %get-tuple-element.26), channel_id=1, source_target_pairs={{0,3},{1,2},{2,1},{3,0},{4,7},{5,6},{6,5},{7,4},{8,11},{9,10},{10,... | collective-permute-start | bytes 61448 | tf_op jit(solution)/shard_map/ppermute | solution.py:716
  10.6 3.0 %collective-permute-start.4 = (f32[4,128]{1,0:T(4,128)S(1)}, f32[4,128]{1,0:T(4,128)S(1)}, u32[]{:S(2)}, u32[]{:S(2)}) collective-permute-start(f32[4,128]{1,0:T(4,128)S(1)} %get-tuple-element.27), channel_id=1, source_target_pairs={{0,1},{1,0},{2,3},{3,2},{4,5},{5,4},{6,7},{7,6},{8,9},{9,8},{10,11... | collective-permute-start | bytes 6152 | tf_op jit(solution)/shard_map/ppermute | solution.py:710
  17.5 1.2 %collective-permute-start.5 = (f32[4,128]{1,0:T(4,128)S(1)}, f32[4,128]{1,0:T(4,128)S(1)}, u32[]{:S(2)}, u32[]{:S(2)}) collective-permute-start(f32[4,128]{1,0:T(4,128)S(1)} %get-tuple-element.41), channel_id=1, source_target_pairs={{0,1},{1,0},{2,3},{3,2},{4,5},{5,4},{6,7},{7,6},{8,9},{9,8},{10,11... | collective-permute-start | bytes 6152 | tf_op jit(solution)/shard_map/ppermute | solution.py:710
  18.7 4.2 %copy-start.1 = (f32[2,3,512]{2,0,1:T(2,128)S(1)}, f32[2,3,512]{2,0,1:T(2,128)}, u32[]{:S(2)}) copy-start(f32[2,3,512]{2,0,1:T(2,128)} %param.12) | copy-start | bytes 36868
  18.7 5.5 %collective-permute-start.8 = (f32[16,128]{1,0:T(8,128)S(1)}, f32[16,128]{1,0:T(8,128)S(1)}, u32[]{:S(2)}, u32[]{:S(2)}) collective-permute-start(f32[16,128]{1,0:T(8,128)S(1)} %combine.1.refs_0_), channel_id=1, source_target_pairs={{0,4},{4,8},{8,12},{12,0},{1,5},{5,9},{9,13},{13,1},{2,6},{6,10},{... | collective-permute-start | bytes 24584 | tf_op jit(solution)/shard_map/ppermute | solution.py:738
  18.8 5.4 %collective-permute-start.7 = (f32[16,128]{1,0:T(8,128)S(1)}, f32[16,128]{1,0:T(8,128)S(1)}, u32[]{:S(2)}, u32[]{:S(2)}) collective-permute-start(f32[16,128]{1,0:T(8,128)S(1)} %combine.1.refs_0_), channel_id=1, source_target_pairs={{0,8},{4,12},{8,0},{12,4},{1,9},{5,13},{9,1},{13,5},{2,10},{6,14},... | collective-permute-start | bytes 24584 | tf_op jit(solution)/shard_map/ppermute | solution.py:738
  21.3 3.7 %collective-permute-start.6 = (f32[16,128]{1,0:T(8,128)S(1)}, f32[16,128]{1,0:T(8,128)S(1)}, u32[]{:S(2)}, u32[]{:S(2)}) collective-permute-start(f32[16,128]{1,0:T(8,128)S(1)} %combine.1.refs_0_), channel_id=1, source_target_pairs={{0,12},{4,0},{8,4},{12,8},{1,13},{5,1},{9,5},{13,9},{2,14},{6,2},{... | collective-permute-start | bytes 24584 | tf_op jit(solution)/shard_map/ppermute | solution.py:738

commit v8 on v7

--- a/solution.py
+++ b/solution.py
@@ -216,14 +216,16 @@
             desc[first : first + 8, :] = acc[s][o]
 
 
-def left_factor(desc, centre):
-    chan = desc.shape[0]
-    high, low = split2(desc[...].T)
+def centre_factor(centre, chan):
     ids = lax.broadcasted_iota(jnp.int32, (chan, LANES), 0)
     ids = jnp.where(ids < 3 * SPECIES, jnp.bitwise_and(ids, SPECIES - 1), -1)
     onehot = jnp.where(ids.astype(jnp.float32) == centre, 1.0, 0.0)
-    onehot = onehot.T.astype(jnp.bfloat16)
-    return jnp.concatenate([high, high, low, onehot], axis=1)
+    return onehot.T.astype(jnp.bfloat16)
+
+
+def left_factor(desc, centre):
+    high, low = split2(desc[...].T)
+    return jnp.concatenate([high, high, low, centre], axis=1)
 
 
 def dense(x, pair):
@@ -367,14 +369,20 @@
             out[row : row + 1, :] = out[row : row + 1, :] + both
 
 
-def inner_kernel(own, code, rates, t1, t2, t3, wout, off, kind, rad, state, dist, desc):
+def inner_kernel(
+    own, code, rates, t1, t2, t3, wout, off, kind, rad, state, centres, dist, desc
+):
+    chan = desc.shape[1]
+    for i, g in enumerate((0, kind.shape[0] + 1)):
+        centres[i] = centre_factor(own[4 * g + 3 : 4 * g + 4, :], chan)
     lefts = []
     for i in range(kind.shape[0]):
         word = code[:, (i + 1) * LANES : (i + 2) * LANES]
         neighbours(own, word, i, off.at[i], kind.at[i], dist.at[i])
         describe(kind.at[i], dist.at[i], rates, rad.at[i], desc.at[i])
         row = 4 * (i + 1) + 3
-        lefts.append(left_factor(desc.at[i], own[row : row + 1, :]))
+        centre = centre_factor(own[row : row + 1, :], chan)
+        lefts.append(left_factor(desc.at[i], centre))
     states = through(forward_layers((t1, t2, t3), wout), lefts)
     for i, values in enumerate(states):
         for j, value in enumerate(values):
@@ -390,12 +398,13 @@
         pltpu.VMEM((count, slots, LANES), jnp.float32),
         pltpu.VMEM((count, slots * rate_count, LANES), jnp.float32),
         pltpu.VMEM((count, 3, LANES, wout.shape[1]), jnp.float32),
+        pltpu.VMEM((2, LANES, chan), jnp.bfloat16),
     ]
     return pl.pallas_call(
         inner_kernel,
         out_shape=out_shape,
         in_specs=[VMEM] * 7,
-        out_specs=[VMEM] * 4,
+        out_specs=[VMEM] * 5,
         scratch_shapes=[
             pltpu.VMEM((count, slots, LANES), jnp.float32),
             pltpu.VMEM((count, chan, LANES), jnp.float32),
@@ -416,7 +425,7 @@
 
     blocks = take(3 if direct else 1)
     code, *pairs, rates, wout = take(9 - 1)
-    state_inner = take(1)[0] if inner else None
+    state_inner, centres = take(2) if inner else (None, None)
     out = take(1)[0]
     to_inner = take(1)[0] if direct else None
     grad_inner = take(1)[0] if inner else None
@@ -451,7 +460,11 @@
         neighbours(rows, word, g, off.at[i], kind.at[i], dist.at[i])
         describe(kind.at[i], dist.at[i], rates, rad.at[i], desc.at[i])
         row = 4 * (g + 1) + 3
-        return left_factor(desc.at[i], rows[row : row + 1, :])
+        if inner and rows is places:
+            centre = centres[i]
+        else:
+            centre = centre_factor(rows[row : row + 1, :], desc.shape[1])
+        return left_factor(desc.at[i], centre)
 
     t1, t2, t3, l2, l3 = pairs
     layers = forward_layers((t1, t2, t3), wout)
@@ -494,7 +507,7 @@
         count += 1
     if inner:
         out_shape.append(pltpu.VMEM((inner, chan, LANES), f32))
-        operands.append(state_inner)
+        operands += state_inner
     return pl.pallas_call(
         functools.partial(outer_kernel, direct, inner),
         out_shape=out_shape,
@@ -799,7 +812,7 @@
         inner_count = max(tiles - 2, 0)
         state_inner, others = None, []
         if inner_count:
-            off, kind, rad, state_inner = inner_stage(
+            off, kind, rad, *state_inner = inner_stage(
                 own, code, rates, pairs, wout, inner_count
             )
         force, to_inner, *grad_inner = outer_stage(
@@ -833,7 +846,7 @@
     state_inner = None
     if groups > 2:
         inside = window[4 : 4 * groups + 4]
-        off, kind, rad, state_inner = inner_stage(
+        off, kind, rad, *state_inner = inner_stage(
             inside, code, rates, pairs, wout, groups - 2
         )
     force, *grad_inner = outer_stage([window], code, pairs, rates, wout, state_inner)

time: 25.8 us -> 25.8 us (level)
  no operation moved by 1% of the time
where the time goes in v8:
time: 25.8 us; the launch traced here: 25.6 us
  starting transfers between devices  11.7 us (45%)
  Pallas kernels  7.95 us (31%)
  waiting for transfers between devices  5.24 us (20%)
  between operations  0.71 us (3%)
    ppermute x6, starting transfers between devices, around(): blocks.append(lax.ppermute(block, 'bead', pairs))  9.88 us
    ppermute x6, waiting for transfers between devices, around(): blocks.append(lax.ppermute(block, 'bead', pairs))  4.54 us
    pallas_call x1, Pallas kernels, outer_stage(): pl.pallas_call(functools.partial(outer_kernel, direct, inner), out_shape=...  3.51 us
    ppermute x2, starting transfers between devices, swap_inner(): return lax.ppermute(block, 'space', [(i, i ^ 1) for i in range(count)])  1.77 us
    pallas_call x1, Pallas kernels, prepare(): pl.pallas_call(functools.partial(prepare_kernel, slab_atoms, block_start)...  1.59 us
    pallas_call x1, Pallas kernels, inner_stage(): pl.pallas_call(inner_kernel, out_shape=out_shape, in_specs=[VMEM] * 7, ou...  1.38 us
    pallas_call x1, Pallas kernels, inner_forces(): pl.pallas_call(inner_force_kernel, out_shape=pltpu.VMEM((block // LANES *...  0.72 us
    pallas_call x1, Pallas kernels, expand(): pl.pallas_call(functools.partial(expand_kernel, table, beads), out_shape=...  0.64 us
  transfers between devices with their start and end apart: 9, of which 5 were waited for; matrix products, arithmetic and copies ran while one was open for 0% of the time, Pallas kernels for 15%

profile of v8, /device:TPU:0, one launch (start us, length us, event | category | flops | bytes accessed | tf_op | source)
XLA Modules:
  0.0 25.6 jit_solution(1082306046254423776)
XLA Ops:
  0.6 4.1 %collective-permute-start.2 = (f32[24,128]{1,0:T(8,128)}, f32[24,128]{1,0:T(8,128)S(1)}, u32[]{:S(2)}, u32[]{:S(2)}) collective-permute-start(f32[24,128]{1,0:T(8,128)} %bitcast.25), channel_id=1, source_target_pairs={{0,8},{4,12},{8,0},{12,4},{1,9},{5,13},{9,1},{13,5},{2,10},{6,14},... | collective-permute-start | bytes 36872 | tf_op jit(solution)/shard_map/ppermute | solution.py:751
  4.7 1.3 %collective-permute-start.1 = (f32[24,128]{1,0:T(8,128)}, f32[24,128]{1,0:T(8,128)S(1)}, u32[]{:S(2)}, u32[]{:S(2)}) collective-permute-start(f32[24,128]{1,0:T(8,128)} %bitcast.26), channel_id=1, source_target_pairs={{0,12},{4,8},{8,4},{12,0},{1,13},{5,9},{9,5},{13,1},{2,14},{6,10},... | collective-permute-start | bytes 36872 | tf_op jit(solution)/shard_map/ppermute | solution.py:751
  6.1 0.2 collective-permute-start
  6.3 0.0 copy-start
  6.3 1.6 %prepare.1 = (s32[32,512]{1,0:T(8,128)S(1)}, f32[4,128]{1,0:T(4,128)S(1)}, bf16[384,256]{1,0:T(8,128)(2,1)S(1)}, bf16[512,256]{1,0:T(8,128)(2,1)S(1)}, bf16[512,...) custom-call(s32[32,512]{1,0:T(8,128)} %refs_0_.1, ...), custom_call_target="tpu_custom_call" | custom-call | bytes 3600000 | tf_op jit(solution)/shard_map/prepare/pallas_call | solution.py:153
  7.9 0.0 collective-permute-done.2.refs_3_
  7.9 2.5 %collective-permute-done.1.refs_2_.after = f32[24,128]{1,0:T(8,128)S(1)} collective-permute-done((f32[24,128]{1,0:T(8,128)}, f32[24,128]{1,0:T(8,128)S(1)}, u32[]{:S(2)}, u32[]{:S(2)}) %collective-permute-start.1) | collective-permute-done | bytes 12320 | tf_op jit(solution)/shard_map/ppermute | solution.py:751
  10.4 0.0 collective-permute-done.refs_1_.before
  10.4 0.0 copy-done
  10.4 0.1 contract.1
  10.5 0.1 collective-permute-start.3
  10.6 1.6 %collective-permute-start.4 = (f32[4,128]{1,0:T(4,128)S(1)}, f32[4,128]{1,0:T(4,128)S(1)}, u32[]{:S(2)}, u32[]{:S(2)}) collective-permute-start(f32[4,128]{1,0:T(4,128)S(1)} %get-tuple-element.28), channel_id=1, source_target_pairs={{0,1},{1,0},{2,3},{3,2},{4,5},{5,4},{6,7},{7,6},{8,9},{9,8},{10,11... | collective-permute-start | bytes 6152 | tf_op jit(solution)/shard_map/ppermute | solution.py:723
  12.2 1.4 %inner_forward.1 = (f32[2,3,32,128]{3,2,1,0:T(8,128)S(1)}, f32[2,32,128]{2,1,0:T(8,128)S(1)}, f32[2,1024,128]{2,1,0:T(8,128)S(1)}, f32[2,3,128,256]{3,2,1,0:T(8,128)S(1)}, bf16[2,128,128]{2,1,0:T(8,128)(2,1)S(1)}) custom-call(f32[16,128]{1,0:T(8,128)S(1)} %get-tuple-element.26.own.refs_0_, s32[32,512]{1,0:T(8,128)S(1)} %get-tuple-element.25.refs_5_.code.refs_3_, ...), custom_call_target="tpu_custom_call" | custom-call | bytes 3000000 | tf_op jit(solution)/shard_map/inner_forward/pallas_call | solution.py:403
  13.6 0.0 collective-permute-done.4.refs_2_
  13.6 0.4 %collective-permute-done.3.refs_1_ = f32[40,128]{1,0:T(8,128)S(1)} collective-permute-done((f32[40,128]{1,0:T(8,128)S(1)}, f32[40,128]{1,0:T(8,128)S(1)}, u32[]{:S(2)}, u32[]{:S(2)}) %collective-permute-start.3) | collective-permute-done | bytes 20512 | tf_op jit(solution)/shard_map/ppermute | solution.py:729
  13.9 3.5 %outer_forces.1 = (f32[24,128]{1,0:T(8,128)S(1)}, f32[4,128]{1,0:T(4,128)S(1)}, f32[2,128,128]{2,1,0:T(8,128)S(1)}) custom-call(f32[16,128]{1,0:T(8,128)S(1)} %get-tuple-element.26.own.refs_0_, f32[40,128]{1,0:T(8,128)S(1)} %collective-permute-done.3.refs_1_, f32[4,128]{1,0:T(4,128)S(1)} %collective-permute-done.4.refs_2_, ...), custom_call_target="tpu_custom_call" | custom-call | bytes 9000000 | tf_op jit(solution)/shard_map/outer_forces/pallas_call | solution.py:511
  17.5 0.2 collective-permute-start.5
  17.6 0.7 %inner_forces.1.refs_0_ = f32[16,128]{1,0:T(8,128)S(1)} custom-call(s32[32,512]{1,0:T(8,128)S(1)} %get-tuple-element.25.refs_5_.code.refs_3_, f32[32,128]{1,0:T(8,128)S(1)} %get-tuple-element.34.rates.refs_9_, f32[2,3,32,128]{3,2,1,0:T(8,128)S(1)} %get-tuple-element.39.off, f32[2,32,128]{2,1,0:T(8,128)S(1)} %get-tuple-element.40.kind, ...), custom_call_target="tpu_custom_call" | custom-call | bytes 3600000 | tf_op jit(solution)/shard_map/inner_forces/pallas_call | solution.py:548
  18.4 0.3 %collective-permute-done.5.refs_1_ = f32[4,128]{1,0:T(4,128)S(1)} collective-permute-done((f32[4,128]{1,0:T(4,128)S(1)}, f32[4,128]{1,0:T(4,128)S(1)}, u32[]{:S(2)}, u32[]{:S(2)}) %collective-permute-start.5) | collective-permute-done | bytes 2080 | tf_op jit(solution)/shard_map/ppermute | solution.py:723
  18.7 0.0 copy-start.1
  18.7 0.1 collective-permute-start.8
  18.8 2.6 %collective-permute-start.7 = (f32[16,128]{1,0:T(8,128)S(1)}, f32[16,128]{1,0:T(8,128)S(1)}, u32[]{:S(2)}, u32[]{:S(2)}) collective-permute-start(f32[16,128]{1,0:T(8,128)S(1)} %combine.1.refs_0_), channel_id=1, source_target_pairs={{0,8},{4,12},{8,0},{12,4},{1,9},{5,13},{9,1},{13,5},{2,10},{6,14},... | collective-permute-start | bytes 24584 | tf_op jit(solution)/shard_map/ppermute | solution.py:751
  21.3 1.6 %collective-permute-start.6 = (f32[16,128]{1,0:T(8,128)S(1)}, f32[16,128]{1,0:T(8,128)S(1)}, u32[]{:S(2)}, u32[]{:S(2)}) collective-permute-start(f32[16,128]{1,0:T(8,128)S(1)} %combine.1.refs_0_), channel_id=1, source_target_pairs={{0,12},{4,0},{8,4},{12,8},{1,13},{5,1},{9,5},{13,9},{2,14},{6,2},{... | collective-permute-start | bytes 24584 | tf_op jit(solution)/shard_map/ppermute | solution.py:751
  22.9 0.0 copy-done.1
  23.0 1.2 %collective-permute-done.8.refs_3_ = f32[16,128]{1,0:T(8,128)S(1)} collective-permute-done((f32[16,128]{1,0:T(8,128)S(1)}, f32[16,128]{1,0:T(8,128)S(1)}, u32[]{:S(2)}, u32[]{:S(2)}) %collective-permute-start.8) | collective-permute-done | bytes 8224 | tf_op jit(solution)/shard_map/ppermute | solution.py:751
  24.2 0.0 collective-permute-done.7.refs_2_
  24.2 0.8 %collective-permute-done.6.refs_1_ = f32[16,128]{1,0:T(8,128)S(1)} collective-permute-done((f32[16,128]{1,0:T(8,128)S(1)}, f32[16,128]{1,0:T(8,128)S(1)}, u32[]{:S(2)}, u32[]{:S(2)}) %collective-permute-start.6) | collective-permute-done | bytes 8224 | tf_op jit(solution)/shard_map/ppermute | solution.py:751
  25.0 0.6 %expand.1 = (f32[24,128]{1,0:T(8,128)}, f32[24,128]{1,0:T(8,128)}) custom-call(f32[16,128]{1,0:T(8,128)S(1)} %combine.1.refs_0_, f32[16,128]{1,0:T(8,128)S(1)} %collective-permute-done.6.refs_1_, f32[16,128]{1,0:T(8,128)S(1)} %collective-permute-done.7.refs_2_, f32[16,128]{1,0:T(8,128)S(1)} %collective-permute-done.8.refs_3_, ...), custom_call_target="tpu_custom_call" | custom-call | bytes 2400000 | tf_op jit(solution)/shard_map/expand/pallas_call | solution.py:710
  (2 shorter events, 0.0 us)
Async XLA Ops:
  0.6 7.3 %collective-permute-start.2 = (f32[24,128]{1,0:T(8,128)}, f32[24,128]{1,0:T(8,128)S(1)}, u32[]{:S(2)}, u32[]{:S(2)}) collective-permute-start(f32[24,128]{1,0:T(8,128)} %bitcast.25), channel_id=1, source_target_pairs={{0,8},{4,12},{8,0},{12,4},{1,9},{5,13},{9,1},{13,5},{2,10},{6,14},... | collective-permute-start | bytes 36872 | tf_op jit(solution)/shard_map/ppermute | solution.py:751
  4.7 5.7 %collective-permute-start.1 = (f32[24,128]{1,0:T(8,128)}, f32[24,128]{1,0:T(8,128)S(1)}, u32[]{:S(2)}, u32[]{:S(2)}) collective-permute-start(f32[24,128]{1,0:T(8,128)} %bitcast.26), channel_id=1, source_target_pairs={{0,12},{4,8},{8,4},{12,0},{1,13},{5,9},{9,5},{13,1},{2,14},{6,10},... | collective-permute-start | bytes 36872 | tf_op jit(solution)/shard_map/ppermute | solution.py:751
  6.1 4.4 %collective-permute-start = (f32[24,128]{1,0:T(8,128)}, f32[24,128]{1,0:T(8,128)S(1)}, u32[]{:S(2)}, u32[]{:S(2)}) collective-permute-start(f32[24,128]{1,0:T(8,128)} %bitcast.27), channel_id=1, source_target_pairs={{0,4},{4,0},{8,12},{12,8},{1,5},{5,1},{9,13},{13,9},{2,6},{6,2},{1... | collective-permute-start | bytes 36872 | tf_op jit(solution)/shard_map/ppermute | solution.py:751
  6.3 4.1 %copy-start = (f32[2,3,512]{2,0,1:T(2,128)S(1)}, f32[2,3,512]{2,0,1:T(2,128)}, u32[]{:S(2)}) copy-start(f32[2,3,512]{2,0,1:T(2,128)} %param.11) | copy-start | bytes 36868
  10.5 3.4 %collective-permute-start.3 = (f32[40,128]{1,0:T(8,128)S(1)}, f32[40,128]{1,0:T(8,128)S(1)}, u32[]{:S(2)}, u32[]{:S(2)}) collective-permute-start(f32[40,128]{1,0:T(8,128)S(1)} %get-tuple-element.27), channel_id=1, source_target_pairs={{0,3},{1,2},{2,1},{3,0},{4,7},{5,6},{6,5},{7,4},{8,11},{9,10},{10,... | collective-permute-start | bytes 61448 | tf_op jit(solution)/shard_map/ppermute | solution.py:729
  10.6 3.0 %collective-permute-start.4 = (f32[4,128]{1,0:T(4,128)S(1)}, f32[4,128]{1,0:T(4,128)S(1)}, u32[]{:S(2)}, u32[]{:S(2)}) collective-permute-start(f32[4,128]{1,0:T(4,128)S(1)} %get-tuple-element.28), channel_id=1, source_target_pairs={{0,1},{1,0},{2,3},{3,2},{4,5},{5,4},{6,7},{7,6},{8,9},{9,8},{10,11... | collective-permute-start | bytes 6152 | tf_op jit(solution)/shard_map/ppermute | solution.py:723
  17.5 1.2 %collective-permute-start.5 = (f32[4,128]{1,0:T(4,128)S(1)}, f32[4,128]{1,0:T(4,128)S(1)}, u32[]{:S(2)}, u32[]{:S(2)}) collective-permute-start(f32[4,128]{1,0:T(4,128)S(1)} %get-tuple-element.43), channel_id=1, source_target_pairs={{0,1},{1,0},{2,3},{3,2},{4,5},{5,4},{6,7},{7,6},{8,9},{9,8},{10,11... | collective-permute-start | bytes 6152 | tf_op jit(solution)/shard_map/ppermute | solution.py:723
  18.7 4.2 %copy-start.1 = (f32[2,3,512]{2,0,1:T(2,128)S(1)}, f32[2,3,512]{2,0,1:T(2,128)}, u32[]{:S(2)}) copy-start(f32[2,3,512]{2,0,1:T(2,128)} %param.12) | copy-start | bytes 36868
  18.7 5.5 %collective-permute-start.8 = (f32[16,128]{1,0:T(8,128)S(1)}, f32[16,128]{1,0:T(8,128)S(1)}, u32[]{:S(2)}, u32[]{:S(2)}) collective-permute-start(f32[16,128]{1,0:T(8,128)S(1)} %combine.1.refs_0_), channel_id=1, source_target_pairs={{0,4},{4,8},{8,12},{12,0},{1,5},{5,9},{9,13},{13,1},{2,6},{6,10},{... | collective-permute-start | bytes 24584 | tf_op jit(solution)/shard_map/ppermute | solution.py:751
  18.8 5.4 %collective-permute-start.7 = (f32[16,128]{1,0:T(8,128)S(1)}, f32[16,128]{1,0:T(8,128)S(1)}, u32[]{:S(2)}, u32[]{:S(2)}) collective-permute-start(f32[16,128]{1,0:T(8,128)S(1)} %combine.1.refs_0_), channel_id=1, source_target_pairs={{0,8},{4,12},{8,0},{12,4},{1,9},{5,13},{9,1},{13,5},{2,10},{6,14},... | collective-permute-start | bytes 24584 | tf_op jit(solution)/shard_map/ppermute | solution.py:751
  21.3 3.7 %collective-permute-start.6 = (f32[16,128]{1,0:T(8,128)S(1)}, f32[16,128]{1,0:T(8,128)S(1)}, u32[]{:S(2)}, u32[]{:S(2)}) collective-permute-start(f32[16,128]{1,0:T(8,128)S(1)} %combine.1.refs_0_), channel_id=1, source_target_pairs={{0,12},{4,0},{8,4},{12,8},{1,13},{5,1},{9,5},{13,9},{2,14},{6,2},{... | collective-permute-start | bytes 24584 | tf_op jit(solution)/shard_map/ppermute | solution.py:751
